TPU v7x, 32 devices: a whole 2x2x4 slice. The times are simulated.
32 devices in a mesh: rep: 2 (over x), seq: 4 (over y, core), fsdp: 4 (over z).
Axes of the slice: x: 2, y: 2, z: 4, core: 2. Of those that a mesh axis runs over, the one named last changes fastest.
Arguments:
- inputs: bfloat16 [8, 1024, 768], P(('rep', 'fsdp'), 'seq'), may hold values from -6 to 6
- expert_choice: int32 [2, 8, 1024, 2], P(None, ('rep', 'fsdp'), 'seq'), may hold values from 0 to 3, all different within a row
- pair_order: int32 [2, 8, 4, 512], P(None, ('rep', 'fsdp'), 'seq'), may hold values from 0 to 511, each once within a row
- norm_gains: bfloat16 [2, 2, 768], P(None, None, ('seq', 'fsdp')), may hold values from 0.099609375 to 1.8984375
- attn_qkv: bfloat16 [2, 768, 2304], P(None, ('seq', 'fsdp')), may hold values from -0.21875 to 0.21875
- attn_out: bfloat16 [2, 768, 768], P(None, ('seq', 'fsdp')), may hold values from -1.25 to 1.25
- router: bfloat16 [2, 768, 4], P(None, ('seq', 'fsdp')), may hold values from -0.109375 to 0.109375
- shared_in: bfloat16 [2, 768, 4096], P(None, ('seq', 'fsdp')), may hold values from -0.21875 to 0.21875
- shared_out: bfloat16 [2, 2048, 768], P(None, ('seq', 'fsdp')), may hold values from -0.125 to 0.125
- expert_in: bfloat16 [2, 4, 768, 4096], P(None, None, ('seq', 'fsdp')), may hold values from -0.21875 to 0.21875
- expert_out: bfloat16 [2, 4, 2048, 768], P(None, None, ('seq', 'fsdp')), may hold values from -0.125 to 0.125
- cotangent: bfloat16 [8, 1024, 768], P(('rep', 'fsdp'), 'seq'), may hold values from -6 to 6
Outputs:
- output: bfloat16 [8, 1024, 768], P(('rep', 'fsdp'), 'seq')
- input_grad: float32 [8, 1024, 768], P(('rep', 'fsdp'), 'seq')
- grad_norm_gains: float32 [2, 2, 768], P(None, None, ('seq', 'fsdp'))
- grad_attn_qkv: float32 [2, 768, 2304], P(None, ('seq', 'fsdp'))
- grad_attn_out: float32 [2, 768, 768], P(None, ('seq', 'fsdp'))
- grad_router: float32 [2, 768, 4], P(None, ('seq', 'fsdp'))
- grad_shared_in: float32 [2, 768, 4096], P(None, ('seq', 'fsdp'))
- grad_shared_out: float32 [2, 2048, 768], P(None, ('seq', 'fsdp'))
- grad_expert_in: float32 [2, 4, 768, 4096], P(None, None, ('seq', 'fsdp'))
- grad_expert_out: float32 [2, 4, 2048, 768], P(None, None, ('seq', 'fsdp'))
Inputs may be any that keep to these rules, and one draw needn't show every extreme that they name: `expert_choice`: each token's two choices in a layer are different experts. `pair_order`: each row lists each of the 512 pairs of one block once.
All inputs are finite; a program needn't handle non-finite values.
Results may differ from a plain program's by a relative error of at most 0.03.
Values may be sent and summed in bfloat16 or wider, within the bound.
A program may use at most 320 MiB of HBM per device.

v0:
```python
from functools import partial
from functools import reduce

import jax
import jax.numpy as jnp
from jax import lax
from jax.sharding import PartitionSpec as P

D = 768
HEADS = 12
HEAD_DIM = 64
FF = 2048
EXPERTS = 4
LAYERS = 2
CAP = 144


epsilon = 1e-06
masked_value = -1e30


def rms_forward(hidden_state, gain_row):
    factor = lax.rsqrt(jnp.mean(hidden_state * hidden_state, -1, keepdims=True) + epsilon)
    return (hidden_state * factor * gain_row, factor)


def rms_backward(hidden_state, factor, gain_row, gradient):
    weighted = gradient * gain_row
    inner = jnp.mean(weighted * hidden_state, -1, keepdims=True)
    d_state = factor * weighted - hidden_state * (factor * factor * factor) * inner
    d_gain = jnp.sum(gradient * hidden_state * factor, 0)
    return (d_state, d_gain)


def rotary(start, count):
    half_dim = HEAD_DIM // 2
    inverse = jnp.exp(-jnp.log(10000.0) * jnp.arange(half_dim, dtype=jnp.float32) * 2.0 / HEAD_DIM)
    position = (start + jnp.arange(count, dtype=jnp.int32)).astype(jnp.float32)
    angle = position[:, None] * inverse[None, :]
    return (jnp.cos(angle)[:, None, :], jnp.sin(angle)[:, None, :])


def rotate(heads_in, cosine, sine_table):
    half_dim = heads_in.shape[-1] // 2
    first_half = heads_in[..., :half_dim]
    second_half = heads_in[..., half_dim:]
    return jnp.concatenate(
        [
            first_half * cosine - second_half * sine_table,
            second_half * cosine + first_half * sine_table,
        ],
        -1,
    )


def rotate_back(heads_in, cosine, sine_table):
    half_dim = heads_in.shape[-1] // 2
    first_half = heads_in[..., :half_dim]
    second_half = heads_in[..., half_dim:]
    return jnp.concatenate(
        [
            first_half * cosine + second_half * sine_table,
            second_half * cosine - first_half * sine_table,
        ],
        -1,
    )


def routing(choices_here, order_here):
    tokens_here = choices_here.shape[0]
    pair_expert = choices_here.reshape(-1)
    placed = pair_expert[order_here]
    onehot = (placed[:, None] == jnp.arange(EXPERTS, dtype=jnp.int32)[None, :]).astype(jnp.int32)
    before = jnp.cumsum(onehot, 0) - onehot
    slot_placed = jnp.sum(before * onehot, 1)
    slot_pair = jnp.zeros((2 * tokens_here,), jnp.int32).at[order_here].set(slot_placed)
    kept = slot_pair < CAP
    destination = jnp.where(kept, pair_expert * CAP + slot_pair, EXPERTS * CAP)
    row_pair = (
        jnp.full((EXPERTS * CAP,), 2 * tokens_here, jnp.int32)
        .at[destination]
        .set(jnp.arange(2 * tokens_here, dtype=jnp.int32), mode="drop")
    )
    return (kept.reshape(tokens_here, 2), destination, row_pair)


def contract_last(left_side, right_side):
    return lax.dot_general(
        left_side,
        right_side,
        (((left_side.ndim - 1,), (right_side.ndim - 1,)), ((), ())),
        preferred_element_type=jnp.float32,
    )


def contract_first(left_side, right_side):
    return lax.dot_general(
        left_side, right_side, (((0,), (0,)), ((), ())), preferred_element_type=jnp.float32
    )


def swiglu_back(joint, gradient):
    half_dim = joint.shape[-1] // 2
    gate_part = joint[..., :half_dim]
    up_part = joint[..., half_dim:]
    sigmoid_gate = jax.nn.sigmoid(gate_part)
    d_gate = gradient * up_part * sigmoid_gate * (1.0 + gate_part * (1.0 - sigmoid_gate))
    d_up = gradient * gate_part * sigmoid_gate
    return jnp.concatenate([d_gate, d_up], -1).astype(jnp.bfloat16)


def fetch_experts(expert_in, expert_out, layer_index):
    first_rows, second_rows = (
        lax.all_to_all(expert_in[layer_index], "fsdp", split_axis=0, concat_axis=1, tiled=True),
        lax.all_to_all(expert_out[layer_index], "fsdp", split_axis=0, concat_axis=1, tiled=True),
    )
    return (
        lax.all_gather(first_rows, "seq", axis=1, tiled=True),
        lax.all_gather(second_rows, "seq", axis=1, tiled=True),
    )


def dense_members(shards, layer_index):
    return tuple((member[layer_index] for member in shards))


def fetch_forward(shards, layer_index):
    gain_rows, qkv_rows, out_rows, router_rows, first_rows, second_rows = dense_members(
        shards, layer_index
    )
    return (
        lax.all_gather(gain_rows, ("seq", "fsdp"), axis=1, tiled=True),
        lax.all_gather(qkv_rows, ("seq", "fsdp"), axis=0, tiled=True),
        lax.all_gather(out_rows, ("seq", "fsdp"), axis=0, tiled=True),
        lax.all_gather(router_rows, ("seq", "fsdp"), axis=0, tiled=True),
        lax.all_gather(first_rows, ("seq", "fsdp"), axis=0, tiled=True),
        lax.all_gather(second_rows, ("seq", "fsdp"), axis=0, tiled=True),
    )


def fetch_backward(shards, layer_index):
    gain_rows, qkv_rows, out_rows, router_rows, first_rows, second_rows = dense_members(
        shards, layer_index
    )
    return (
        lax.all_gather(gain_rows, ("seq", "fsdp"), axis=1, tiled=True),
        lax.all_gather(qkv_rows, ("seq", "fsdp"), axis=0, tiled=True),
        lax.all_gather(out_rows, ("seq", "fsdp"), axis=0, tiled=True),
        lax.all_gather(router_rows, ("seq", "fsdp"), axis=0, tiled=True),
        lax.all_gather(first_rows, ("seq", "fsdp"), axis=0, tiled=True),
        lax.all_gather(second_rows, ("seq", "fsdp"), axis=0, tiled=True),
    )


def block_scores(queries, key_rows, query_place, key_start):
    count = key_rows.shape[0]
    scores = jnp.einsum(
        "qhd,khd->hqk", queries, key_rows, preferred_element_type=jnp.float32
    ) * HEAD_DIM ** (-0.5)
    visible = query_place[:, None] >= (key_start + jnp.arange(count, dtype=jnp.int32))[None, :]
    return jnp.where(visible[None], scores, masked_value)


def weigh_values(scores, log_total, value_rows):
    attention = jnp.exp(scores - log_total[..., None]).astype(jnp.bfloat16)
    return jnp.einsum("hqk,khd->qhd", attention, value_rows, preferred_element_type=jnp.float32)


def attention_forward(queries, key_all, value_all, query_place, seq_place):
    tokens_here = queries.shape[0]
    blocks = key_all.shape[0] // tokens_here
    key_heads = key_all.reshape(blocks, tokens_here, HEADS, HEAD_DIM)
    value_heads = value_all.reshape(blocks, tokens_here, HEADS, HEAD_DIM)
    empty_scores = partial(jnp.full, (HEADS, tokens_here, tokens_here), masked_value, jnp.float32)
    score_list = []
    for block_index in range(blocks):
        compute = partial(
            block_scores, queries, key_heads[block_index], query_place, block_index * tokens_here
        )
        score_list.append(lax.cond(block_index <= seq_place, compute, empty_scores))
    top_score = reduce(jnp.maximum, [jnp.max(scores, -1) for scores in score_list])
    totals = reduce(
        jnp.add, [jnp.sum(jnp.exp(scores - top_score[..., None]), -1) for scores in score_list]
    )
    log_total = top_score + jnp.log(totals)
    empty_out = partial(jnp.zeros, (tokens_here, HEADS, HEAD_DIM), jnp.float32)
    attended = jnp.zeros((tokens_here, HEADS, HEAD_DIM), jnp.float32)
    for block_index in range(blocks):
        compute = partial(
            weigh_values, score_list[block_index], log_total, value_heads[block_index]
        )
        attended = attended + lax.cond(block_index <= seq_place, compute, empty_out)
    return (attended, log_total)


def block_back(queries, key_rows, value_rows, query_place, key_start, log_total, delta, d_attended):
    scale = HEAD_DIM ** (-0.5)
    attention = jnp.exp(
        block_scores(queries, key_rows, query_place, key_start) - log_total[..., None]
    )
    d_attention = jnp.einsum(
        "qhd,khd->hqk", d_attended, value_rows, preferred_element_type=jnp.float32
    )
    d_scores = (attention * (d_attention - delta[..., None])).astype(jnp.bfloat16)
    d_query_part = (
        jnp.einsum("hqk,khd->qhd", d_scores, key_rows, preferred_element_type=jnp.float32) * scale
    )
    d_key_part = (
        jnp.einsum("hqk,qhd->khd", d_scores, queries, preferred_element_type=jnp.float32) * scale
    )
    d_value_part = jnp.einsum(
        "hqk,qhd->khd",
        attention.astype(jnp.bfloat16),
        d_attended,
        preferred_element_type=jnp.float32,
    )
    return (d_query_part, d_key_part, d_value_part)


def empty_triple(tokens_here):
    zero_block = jnp.zeros((tokens_here, HEADS, HEAD_DIM), jnp.float32)
    return (zero_block, zero_block, zero_block)


def attention_backward(
    queries, key_all, value_all, query_place, seq_place, log_total, attended, d_attended
):
    tokens_here = queries.shape[0]
    blocks = key_all.shape[0] // tokens_here
    key_heads = key_all.reshape(blocks, tokens_here, HEADS, HEAD_DIM)
    value_heads = value_all.reshape(blocks, tokens_here, HEADS, HEAD_DIM)
    delta = jnp.sum(d_attended.astype(jnp.float32) * attended, -1).T
    d_queries = jnp.zeros((tokens_here, HEADS, HEAD_DIM), jnp.float32)
    key_grads = []
    value_grads = []
    for block_index in range(blocks):
        compute = partial(
            block_back,
            queries,
            key_heads[block_index],
            value_heads[block_index],
            query_place,
            block_index * tokens_here,
            log_total,
            delta,
            d_attended,
        )
        d_query_part, d_key_part, d_value_part = lax.cond(
            block_index <= seq_place, compute, partial(empty_triple, tokens_here)
        )
        d_queries = d_queries + d_query_part
        key_grads.append(d_key_part)
        value_grads.append(d_value_part)
    key_total = jnp.concatenate(key_grads, 0).reshape(blocks * tokens_here, D)
    value_total = jnp.concatenate(value_grads, 0).reshape(blocks * tokens_here, D)
    return (d_queries, key_total, value_total)


def layer_forward(
    hidden_state,
    weights,
    own_pair,
    routes,
    choices_here,
    cosine,
    sine_table,
    query_place,
    seq_place,
):
    gain_pair, qkv_weight, out_weight, router_weight, shared_first, shared_second = weights
    first_here, second_here = own_pair
    kept, destination, row_pair = routes
    tokens_here = hidden_state.shape[0]
    head_shape = (tokens_here, HEADS, HEAD_DIM)
    normed, factor_first = rms_forward(hidden_state, gain_pair[0].astype(jnp.float32))
    normed_first = normed.astype(jnp.bfloat16)
    joint_qkv = jnp.dot(normed_first, qkv_weight, preferred_element_type=jnp.float32)
    queries = rotate(joint_qkv[:, :D].reshape(head_shape), cosine, sine_table).astype(jnp.bfloat16)
    keys_local = (
        rotate(joint_qkv[:, D : 2 * D].reshape(head_shape), cosine, sine_table)
        .astype(jnp.bfloat16)
        .reshape(tokens_here, D)
    )
    values_local = joint_qkv[:, 2 * D :].astype(jnp.bfloat16)
    key_all, value_all = (
        lax.all_gather(keys_local, "seq", axis=0, tiled=True),
        lax.all_gather(values_local, "seq", axis=0, tiled=True),
    )
    attended, log_total = attention_forward(queries, key_all, value_all, query_place, seq_place)
    attended_low = attended.reshape(tokens_here, D).astype(jnp.bfloat16)
    middle = hidden_state + jnp.dot(attended_low, out_weight, preferred_element_type=jnp.float32)
    normed, factor_second = rms_forward(middle, gain_pair[1].astype(jnp.float32))
    normed_second = normed.astype(jnp.bfloat16)
    logits = jnp.dot(normed_second, router_weight, preferred_element_type=jnp.float32)
    gates = jax.nn.softmax(jnp.take_along_axis(logits, choices_here, 1), -1)
    joint_shared = jnp.dot(normed_second, shared_first, preferred_element_type=jnp.float32)
    hidden_shared = (jax.nn.silu(joint_shared[:, :FF]) * joint_shared[:, FF:]).astype(jnp.bfloat16)
    branch_shared = jnp.dot(hidden_shared, shared_second, preferred_element_type=jnp.float32)
    padded = jnp.concatenate([normed_second, jnp.zeros((1, D), jnp.bfloat16)], 0)
    buffer_rows = padded[row_pair // 2].reshape(EXPERTS, CAP, D)
    expert_rows = lax.all_to_all(buffer_rows, "fsdp", split_axis=0, concat_axis=1, tiled=True)
    joint_expert = jnp.einsum(
        "ecd,edf->ecf", expert_rows, first_here, preferred_element_type=jnp.float32
    )
    hidden_expert = (jax.nn.silu(joint_expert[..., :FF]) * joint_expert[..., FF:]).astype(
        jnp.bfloat16
    )
    produced = jnp.einsum(
        "ecf,efd->ecd", hidden_expert, second_here, preferred_element_type=jnp.float32
    )
    yields = lax.all_to_all(
        produced.astype(jnp.bfloat16), "fsdp", split_axis=1, concat_axis=0, tiled=True
    ).astype(produced.dtype)
    flat = jnp.concatenate([yields.reshape(EXPERTS * CAP, D), jnp.zeros((1, D), jnp.float32)], 0)
    gathered = flat[destination].reshape(tokens_here, 2, D)
    scaled = gates * kept.astype(jnp.float32)
    mixture = jnp.sum(gathered * scaled[..., None], 1)
    result = middle + branch_shared + mixture
    stored = (
        hidden_state,
        factor_first,
        normed_first,
        queries,
        key_all,
        value_all,
        log_total,
        attended,
        attended_low,
        middle,
        factor_second,
        normed_second,
        gates,
        joint_shared,
        hidden_shared,
        expert_rows,
        joint_expert,
        hidden_expert,
        gathered,
    )
    return (result, stored)


def layer_backward(
    gradient,
    weights,
    own_pair,
    routes,
    stored,
    choices_here,
    cosine,
    sine_table,
    query_place,
    seq_place,
):
    gain_pair, qkv_weight, out_weight, router_weight, shared_first, shared_second = weights
    first_here, second_here = own_pair
    kept, destination, row_pair = routes
    (
        hidden_state,
        factor_first,
        normed_first,
        queries,
        key_all,
        value_all,
        log_total,
        attended,
        attended_low,
        middle,
        factor_second,
        normed_second,
        gates,
        joint_shared,
        hidden_shared,
        expert_rows,
        joint_expert,
        hidden_expert,
        gathered,
    ) = stored
    tokens_here = gradient.shape[0]
    head_shape = (tokens_here, HEADS, HEAD_DIM)
    gradient_low = gradient.astype(jnp.bfloat16)
    d_shared_second = contract_first(hidden_shared, gradient_low)
    d_joint_shared = swiglu_back(joint_shared, contract_last(gradient_low, shared_second))
    d_shared_first = contract_first(normed_second, d_joint_shared)
    d_normed = contract_last(d_joint_shared, shared_first)
    kept_float = kept.astype(jnp.float32)
    d_gates = kept_float * jnp.sum(gradient[:, None, :] * gathered, -1)
    d_chosen = gates * (d_gates - jnp.sum(gates * d_gates, -1, keepdims=True))
    expert_ids = jnp.arange(EXPERTS, dtype=jnp.int32)
    d_logits = jnp.sum(
        d_chosen[..., None] * (choices_here[..., None] == expert_ids).astype(jnp.float32), 1
    )
    d_logits_low = d_logits.astype(jnp.bfloat16)
    d_router = contract_first(normed_second, d_logits_low)
    d_normed = d_normed + contract_last(d_logits_low, router_weight)
    scaled = (gates * kept_float).reshape(-1)
    row_scale = jnp.concatenate([scaled, jnp.zeros((1,), jnp.float32)])[row_pair]
    gradient_pad = jnp.concatenate([gradient, jnp.zeros((1, D), jnp.float32)], 0)
    d_yields = (
        (row_scale[:, None] * gradient_pad[row_pair // 2])
        .astype(jnp.bfloat16)
        .reshape(EXPERTS, CAP, D)
    )
    d_arrived = lax.all_to_all(d_yields, "fsdp", split_axis=0, concat_axis=1, tiled=True)
    d_second_here = jnp.einsum(
        "ecf,ecd->efd", hidden_expert, d_arrived, preferred_element_type=jnp.float32
    )
    d_joint = swiglu_back(
        joint_expert,
        jnp.einsum("ecd,efd->ecf", d_arrived, second_here, preferred_element_type=jnp.float32),
    )
    d_first_here = jnp.einsum(
        "ecd,ecf->edf", expert_rows, d_joint, preferred_element_type=jnp.float32
    )
    rows_back = jnp.einsum("ecf,edf->ecd", d_joint, first_here, preferred_element_type=jnp.float32)
    buffer_back = lax.all_to_all(
        rows_back.astype(jnp.bfloat16), "fsdp", split_axis=1, concat_axis=0, tiled=True
    ).astype(rows_back.dtype)
    d_first_here, d_second_here = (
        lax.psum_scatter(
            d_first_here.astype(jnp.bfloat16), "seq", scatter_dimension=1, tiled=True
        ).astype(jnp.float32),
        lax.psum_scatter(
            d_second_here.astype(jnp.bfloat16), "seq", scatter_dimension=1, tiled=True
        ).astype(jnp.float32),
    )
    first_stack, second_stack = (
        lax.all_to_all(
            d_first_here.astype(jnp.bfloat16), "fsdp", split_axis=1, concat_axis=0, tiled=True
        ).astype(d_first_here.dtype),
        lax.all_to_all(
            d_second_here.astype(jnp.bfloat16), "fsdp", split_axis=1, concat_axis=0, tiled=True
        ).astype(d_second_here.dtype),
    )
    flat_back = jnp.concatenate(
        [buffer_back.reshape(EXPERTS * CAP, D), jnp.zeros((1, D), jnp.float32)], 0
    )
    d_normed = d_normed + jnp.sum(flat_back[destination].reshape(tokens_here, 2, D), 1)
    d_middle, d_gain_second = rms_backward(
        middle, factor_second, gain_pair[1].astype(jnp.float32), d_normed
    )
    d_middle = gradient + d_middle
    d_middle_low = d_middle.astype(jnp.bfloat16)
    d_out_weight = contract_first(attended_low, d_middle_low)
    d_attended = contract_last(d_middle_low, out_weight).astype(jnp.bfloat16).reshape(head_shape)
    d_queries, key_total, value_total = attention_backward(
        queries, key_all, value_all, query_place, seq_place, log_total, attended, d_attended
    )
    d_keys, d_values = (
        lax.psum_scatter(
            key_total.astype(jnp.bfloat16), "seq", scatter_dimension=0, tiled=True
        ).astype(jnp.float32),
        lax.psum_scatter(
            value_total.astype(jnp.bfloat16), "seq", scatter_dimension=0, tiled=True
        ).astype(jnp.float32),
    )
    d_query_raw = rotate_back(d_queries, cosine, sine_table).reshape(tokens_here, D)
    d_key_raw = rotate_back(d_keys.reshape(head_shape), cosine, sine_table).reshape(tokens_here, D)
    d_joint_qkv = jnp.concatenate([d_query_raw, d_key_raw, d_values], 1).astype(jnp.bfloat16)
    d_qkv_weight = contract_first(normed_first, d_joint_qkv)
    d_normed_first = contract_last(d_joint_qkv, qkv_weight)
    d_state, d_gain_first = rms_backward(
        hidden_state, factor_first, gain_pair[0].astype(jnp.float32), d_normed_first
    )
    d_state = d_middle + d_state
    gain_grads = jnp.stack([d_gain_first, d_gain_second])
    gain_part, qkv_part, out_part, router_part, shared_one, shared_two = (
        lax.psum_scatter(
            gain_grads.astype(jnp.bfloat16), ("seq", "fsdp"), scatter_dimension=1, tiled=True
        ).astype(jnp.float32),
        lax.psum_scatter(
            d_qkv_weight.astype(jnp.bfloat16), ("seq", "fsdp"), scatter_dimension=0, tiled=True
        ).astype(jnp.float32),
        lax.psum_scatter(
            d_out_weight.astype(jnp.bfloat16), ("seq", "fsdp"), scatter_dimension=0, tiled=True
        ).astype(jnp.float32),
        lax.psum_scatter(
            d_router.astype(jnp.bfloat16), ("seq", "fsdp"), scatter_dimension=0, tiled=True
        ).astype(jnp.float32),
        lax.psum_scatter(
            d_shared_first.astype(jnp.bfloat16), ("seq", "fsdp"), scatter_dimension=0, tiled=True
        ).astype(jnp.float32),
        lax.psum_scatter(
            d_shared_second.astype(jnp.bfloat16), ("seq", "fsdp"), scatter_dimension=0, tiled=True
        ).astype(jnp.float32),
    )
    layer_grads = (
        lax.psum(gain_part.astype(jnp.bfloat16), "rep").astype(jnp.float32),
        lax.psum(qkv_part.astype(jnp.bfloat16), "rep").astype(jnp.float32),
        lax.psum(out_part.astype(jnp.bfloat16), "rep").astype(jnp.float32),
        lax.psum(router_part.astype(jnp.bfloat16), "rep").astype(jnp.float32),
        lax.psum(shared_one.astype(jnp.bfloat16), "rep").astype(jnp.float32),
        lax.psum(shared_two.astype(jnp.bfloat16), "rep").astype(jnp.float32),
        lax.psum(first_stack.astype(jnp.bfloat16), "rep").astype(jnp.float32),
        lax.psum(second_stack.astype(jnp.bfloat16), "rep").astype(jnp.float32),
    )
    return (d_state, layer_grads)


def local(
    inputs,
    expert_choice,
    pair_order,
    norm_gains,
    attn_qkv,
    attn_out,
    router,
    shared_in,
    shared_out,
    expert_in,
    expert_out,
    cotangent,
):
    tokens_here = inputs.shape[1]
    seq_place = lax.axis_index("seq")
    query_place = seq_place * tokens_here + jnp.arange(tokens_here, dtype=jnp.int32)
    cosine, sine_table = rotary(seq_place * tokens_here, tokens_here)
    shards = (norm_gains, attn_qkv, attn_out, router, shared_in, shared_out)
    hidden_state = inputs[0].astype(jnp.float32)
    stored_layers = []
    for layer_index in range(LAYERS):
        weights = fetch_forward(shards, layer_index)
        own_pair = fetch_experts(expert_in, expert_out, layer_index)
        routes = routing(expert_choice[layer_index, 0], pair_order[layer_index, 0, 0])
        hidden_state, stored = layer_forward(
            hidden_state,
            weights,
            own_pair,
            routes,
            expert_choice[layer_index, 0],
            cosine,
            sine_table,
            query_place,
            seq_place,
        )
        stored_layers.append((routes, stored, own_pair))
    output = hidden_state.astype(jnp.bfloat16)[None]
    gradient = cotangent[0].astype(jnp.float32)
    all_grads = [None] * LAYERS
    for layer_index in reversed(range(LAYERS)):
        weights = fetch_backward(shards, layer_index)
        routes, stored, own_pair = stored_layers[layer_index]
        gradient, all_grads[layer_index] = layer_backward(
            gradient,
            weights,
            own_pair,
            routes,
            stored,
            expert_choice[layer_index, 0],
            cosine,
            sine_table,
            query_place,
            seq_place,
        )
    stacked = [jnp.stack([member[position] for member in all_grads]) for position in range(8)]
    return (
        output,
        gradient[None],
        stacked[0],
        stacked[1],
        stacked[2],
        stacked[3],
        stacked[4],
        stacked[5],
        stacked[6],
        stacked[7],
    )


def solution(mesh):
    in_specs = (
        P(("rep", "fsdp"), "seq", None),
        P(None, ("rep", "fsdp"), "seq", None),
        P(None, ("rep", "fsdp"), "seq", None),
        P(None, None, ("seq", "fsdp")),
        P(None, ("seq", "fsdp"), None),
        P(None, ("seq", "fsdp"), None),
        P(None, ("seq", "fsdp"), None),
        P(None, ("seq", "fsdp"), None),
        P(None, ("seq", "fsdp"), None),
        P(None, None, ("seq", "fsdp"), None),
        P(None, None, ("seq", "fsdp"), None),
        P(("rep", "fsdp"), "seq", None),
    )
    out_specs = (
        P(("rep", "fsdp"), "seq", None),
        P(("rep", "fsdp"), "seq", None),
        P(None, None, ("seq", "fsdp")),
        P(None, ("seq", "fsdp"), None),
        P(None, ("seq", "fsdp"), None),
        P(None, ("seq", "fsdp"), None),
        P(None, ("seq", "fsdp"), None),
        P(None, ("seq", "fsdp"), None),
        P(None, None, ("seq", "fsdp"), None),
        P(None, None, ("seq", "fsdp"), None),
    )
    return jax.shard_map(local, mesh=mesh, in_specs=in_specs, out_specs=out_specs, check_vma=False)
```

profile of v0, /device:TPU:8, one launch (start us, length us, event | category | flops | bytes accessed | tf_op | source)
XLA Modules:
  0.0 2268.6 jit_solution(15140911967240856210)
XLA Ops:
  10.4 34.4 %all-gather = bf16[1,2,768]{1,0,2:T(2,128)(2,1)S(1)} all-gather(bf16[1,2,48]{1,0,2:T(2,128)(2,1)S(1)} %copy.226), channel_id=2, replica_groups=mesh['rep'=2,'seq'=4,'fsdp'=4] {'seq','fsdp'}, dimensions={2}, use_global_device_ids=true | all-gather | bytes 3264 | tf_op jit(solution)/shard_map/all_gather | solution.py:132
  82.3 33.8 %all-to-all-done.1 = bf16[4,48,4096]{2,1,0:T(8,128)(2,1)S(1)} async-done(((bf16[4,48,4096]{2,1,0:T(8,128)(2,1)}), bf16[4,48,4096]{2,1,0:T(8,128)(2,1)S(1)}, u32[]{:S(2)}, u32[]{:S(2)}) %all-to-all-start.1) | async-done | bytes 1572896 | tf_op jit(solution)/shard_map/all_to_all | solution.py:114
  118.3 28.3 %all_to_all.168 = bf16[4,128,768]{2,1,0:T(8,128)(2,1)} all-to-all(bf16[4,128,768]{2,1,0:T(8,128)(2,1)S(1)} %get-tuple-element.753), channel_id=1, replica_groups=mesh['rep'=2,'seq'=4,'fsdp'=4] {'fsdp'}, dimensions={0} | all-to-all | bytes 1572864 | tf_op jit(solution)/shard_map/all_to_all | solution.py:115
  216.7 78.9 %all-gather.5 = bf16[1,768,4]{2,0,1:T(2,128)(2,1)S(1)} all-gather(bf16[1,48,4]{2,0,1:T(2,128)(2,1)S(1)} %copy.228), channel_id=7, replica_groups=mesh['rep'=2,'seq'=4,'fsdp'=4] {'seq','fsdp'}, dimensions={1}, use_global_device_ids=true | all-gather | bytes 6528 | tf_op jit(solution)/shard_map/all_gather | solution.py:135
  296.4 34.4 %all-gather.6 = bf16[1,2,768]{1,0,2:T(2,128)(2,1)S(1)} all-gather(bf16[1,2,48]{1,0,2:T(2,128)(2,1)S(1)} %copy.229), channel_id=8, replica_groups=mesh['rep'=2,'seq'=4,'fsdp'=4] {'seq','fsdp'}, dimensions={2}, use_global_device_ids=true | all-gather | bytes 3264 | tf_op jit(solution)/shard_map/all_gather | solution.py:132
  386.2 22.6 all-to-all-done.3
  434.5 39.8 %all_to_all.169 = bf16[4,48,4096]{2,1,0:T(8,128)(2,1)} all-to-all(bf16[4,48,4096]{2,1,0:T(8,128)(2,1)} %get-tuple-element.731), channel_id=1, replica_groups=mesh['rep'=2,'seq'=4,'fsdp'=4] {'fsdp'}, dimensions={0} | all-to-all | bytes 3145728 | tf_op jit(solution)/shard_map/all_to_all | solution.py:114
  485.5 40.4 %all-gather.11 = bf16[1,768,4]{2,0,1:T(2,128)(2,1)S(1)} all-gather(bf16[1,48,4]{2,0,1:T(2,128)(2,1)S(1)} %copy.231), channel_id=13, replica_groups=mesh['rep'=2,'seq'=4,'fsdp'=4] {'seq','fsdp'}, dimensions={1}, use_global_device_ids=true | all-gather | bytes 6528 | tf_op jit(solution)/shard_map/all_gather | solution.py:135
  618.0 17.5 all-to-all-done.4
  650.8 36.0 %all-gather.41.cloned.1.call-done = bf16[1,768,4096]{2,1,0:T(8,128)(2,1)} async-done(((bf16[1,192,4096]{2,1,0:T(8,128)(2,1)}), bf16[1,768,4096]{2,1,0:T(8,128)(2,1)}) %all-gather.41.cloned.1.call-update) | async-done | bytes 6291472 | tf_op jit(solution)/shard_map/all_gather | solution.py:118
  686.8 11.1 convolution_bitcast_fusion
  697.8 19.5 all-gather.43.cloned.1.call-done
  834.4 38.6 %reduce-scatter.29.cloned.1.call-done = bf16[256,768]{0,1:T(8,128)(2,1)} async-done(((bf16[1024,768]{0,1:T(8,128)(2,1)}), bf16[256,768]{0,1:T(8,128)(2,1)}) %reduce-scatter.29.cloned.1.call-update) | async-done | bytes 393232 | tf_op jit(solution)/shard_map/reduce_scatter | solution.py:450
  874.4 29.9 %reduce-scatter.31.cloned.1.call-done = bf16[256,768]{0,1:T(8,128)(2,1)} async-done(((bf16[1024,768]{0,1:T(8,128)(2,1)}), bf16[256,768]{0,1:T(8,128)(2,1)}) %reduce-scatter.31.cloned.1.call-update) | async-done | bytes 393232 | tf_op jit(solution)/shard_map/reduce_scatter | solution.py:453
  1118.9 24.0 %reduce-scatter.57.cloned.1.call-done = bf16[1,512,768]{2,1,0:T(8,128)(2,1)} async-done(((bf16[1,2048,768]{2,1,0:T(8,128)(2,1)}), bf16[1,512,768]{2,1,0:T(8,128)(2,1)}) %reduce-scatter.57.cloned.1.call-update) | async-done | bytes 786448 | tf_op jit(solution)/shard_map/reduce_scatter | solution.py:423
  1156.9 46.9 %reduce-scatter.55.cloned.1.call-done = bf16[1,192,4096]{2,1,0:T(8,128)(2,1)} async-done(((bf16[1,768,4096]{2,1,0:T(8,128)(2,1)}), bf16[1,192,4096]{2,1,0:T(8,128)(2,1)}) %reduce-scatter.55.cloned.1.call-update) | async-done | bytes 1572880 | tf_op jit(solution)/shard_map/reduce_scatter | solution.py:420
  1210.4 13.0 reduce.24
  1231.0 33.8 %reduce-scatter.53.cloned.1.call-done = bf16[1,192,4096]{2,1,0:T(8,128)(2,1)} async-done(((bf16[1,768,4096]{2,1,0:T(8,128)(2,1)}), bf16[1,192,4096]{2,1,0:T(8,128)(2,1)}) %reduce-scatter.53.cloned.1.call-update) | async-done | bytes 1572880 | tf_op jit(solution)/shard_map/reduce_scatter | solution.py:420
  1271.4 11.8 reduce.25
  1311.0 18.7 all-to-all-done.12
  1341.8 69.2 %reduce-scatter.51.cloned.1.call-done = bf16[128,768]{1,0:T(8,128)(2,1)} async-done(((bf16[2048,768]{1,0:T(8,128)(2,1)}), bf16[128,768]{1,0:T(8,128)(2,1)}) %reduce-scatter.51.cloned.1.call-update) | async-done | bytes 196624 | tf_op jit(solution)/shard_map/reduce_scatter | solution.py:483
  1411.0 88.5 %reduce-scatter.47.cloned.1.call-done = bf16[48,4096]{1,0:T(8,128)(2,1)} async-done(((bf16[768,4096]{1,0:T(8,128)(2,1)}), bf16[48,4096]{1,0:T(8,128)(2,1)}) %reduce-scatter.47.cloned.1.call-update) | async-done | bytes 393232 | tf_op jit(solution)/shard_map/reduce_scatter | solution.py:480
  1499.5 61.7 %reduce-scatter.41.cloned.1.call-done = bf16[48,768]{1,0:T(8,128)(2,1)} async-done(((bf16[768,768]{1,0:T(8,128)(2,1)}), bf16[48,768]{1,0:T(8,128)(2,1)}) %reduce-scatter.41.cloned.1.call-update) | async-done | bytes 73744 | tf_op jit(solution)/shard_map/reduce_scatter | solution.py:474
  1561.2 69.2 %reduce-scatter.49.cloned.1.call-done = bf16[128,768]{1,0:T(8,128)(2,1)} async-done(((bf16[2048,768]{1,0:T(8,128)(2,1)}), bf16[128,768]{1,0:T(8,128)(2,1)}) %reduce-scatter.49.cloned.1.call-update) | async-done | bytes 196624 | tf_op jit(solution)/shard_map/reduce_scatter | solution.py:483
  1630.4 71.2 %reduce-scatter.39.cloned.1.call-done = bf16[48,2304]{1,0:T(8,128)(2,1)} async-done(((bf16[768,2304]{1,0:T(8,128)(2,1)}), bf16[48,2304]{1,0:T(8,128)(2,1)}) %reduce-scatter.39.cloned.1.call-update) | async-done | bytes 221200 | tf_op jit(solution)/shard_map/reduce_scatter | solution.py:471
  1701.5 88.7 %reduce-scatter.45.cloned.1.call-done = bf16[48,4096]{1,0:T(8,128)(2,1)} async-done(((bf16[768,4096]{1,0:T(8,128)(2,1)}), bf16[48,4096]{1,0:T(8,128)(2,1)}) %reduce-scatter.45.cloned.1.call-update) | async-done | bytes 393232 | tf_op jit(solution)/shard_map/reduce_scatter | solution.py:480
  1790.3 71.1 %reduce-scatter.37.cloned.1.call-done = bf16[48,2304]{1,0:T(8,128)(2,1)} async-done(((bf16[768,2304]{1,0:T(8,128)(2,1)}), bf16[48,2304]{1,0:T(8,128)(2,1)}) %reduce-scatter.37.cloned.1.call-update) | async-done | bytes 221200 | tf_op jit(solution)/shard_map/reduce_scatter | solution.py:471
  1866.7 50.9 %reduce-scatter.67.cloned.1.call-done = bf16[48,4]{1,0:T(8,128)(2,1)} async-done(((bf16[768,4]{1,0:T(8,128)(2,1)}), bf16[48,4]{1,0:T(8,128)(2,1)}) %reduce-scatter.67.cloned.1.call-update) | async-done | bytes 400
  1918.4 55.9 %reduce-scatter.63.cloned.1.call-done = bf16[48,2]{1,0:T(8,128)(2,1)} async-done(((bf16[768,2]{1,0:T(8,128)(2,1)}), bf16[48,2]{1,0:T(8,128)(2,1)}) %reduce-scatter.63.cloned.1.call-update) | async-done | bytes 208
  1975.1 55.3 %reduce-scatter.65.cloned.1.call-done = bf16[48,4]{1,0:T(8,128)(2,1)} async-done(((bf16[768,4]{1,0:T(8,128)(2,1)}), bf16[48,4]{1,0:T(8,128)(2,1)}) %reduce-scatter.65.cloned.1.call-update) | async-done | bytes 400
  2033.5 52.9 %reduce-scatter.61.cloned.1.call-done = bf16[48,2]{1,0:T(8,128)(2,1)} async-done(((bf16[768,2]{1,0:T(8,128)(2,1)}), bf16[48,2]{1,0:T(8,128)(2,1)}) %reduce-scatter.61.cloned.1.call-update) | async-done | bytes 208
  2093.3 157.7 %all-reduce.12.cloned.1.call-done = (bf16[1,48,2304]{2,1,0:T(8,128)(2,1)}, bf16[1,48,2304]{2,1,0:T(8,128)(2,1)}, bf16[1,48,768]{2,1,0:T(8,128)(2,1)}, bf16[1,48,...) async-done(((bf16[1,48,2304]{2,1,0:T(8,128)(2,1)}, ...) | async-done | bytes 6488080 | tf_op jit(solution)/shard_map/psum | solution.py:489
  (905 shorter events, 789.8 us)
Async XLA Ops:
  9.1 153.1 %all-gather.29.cloned.1.call-start = ((), (), s32[]{:S(2)}) async-start(), calls=%async_computation.36 | async-start | bytes 1966080 | tf_op jit(solution)/shard_map/all_gather | solution.py:286
  81.5 123.0 %all-gather.47.cloned.1.call-start = ((), (), s32[]{:S(2)}) async-start(), calls=%async_computation.61 | async-start | bytes 1253376 | tf_op jit(solution)/shard_map/all_gather | solution.py:134
  82.2 258.8 %all-gather.33.cloned.1.call-start = ((), (), s32[]{:S(2)}) async-start(), calls=%async_computation.38 | async-start | bytes 7864320 | tf_op jit(solution)/shard_map/all_gather | solution.py:118
  117.3 236.1 %all-gather.35.cloned.1.call-start = ((), (), s32[]{:S(2)}) async-start(), calls=%async_computation.39 | async-start | bytes 3932160 | tf_op jit(solution)/shard_map/all_gather | solution.py:119
  146.7 231.3 %all-gather.49.cloned.1.call-start = ((), (), s32[]{:S(2)}) async-start(), calls=%async_computation.62 | async-start | bytes 6684672 | tf_op jit(solution)/shard_map/all_gather | solution.py:136
  147.7 269.1 %all-gather.51.cloned.1.call-start = ((), (), s32[]{:S(2)}) async-start(), calls=%async_computation.63 | async-start | bytes 3342336 | tf_op jit(solution)/shard_map/all_gather | solution.py:137
  148.5 272.2 %all-gather.53.cloned.1.call-start = ((), (), s32[]{:S(2)}) async-start(), calls=%async_computation.64 | async-start | bytes 3760128 | tf_op jit(solution)/shard_map/all_gather | solution.py:133
  210.9 130.1 %all-to-all-start = ((bf16[4,144,768]{2,1,0:T(8,128)(2,1)}), bf16[4,144,768]{2,1,0:T(8,128)(2,1)S(1)}, u32[]{:S(2)}, u32[]{:S(2)}) async-start(bf16[4,144,768]{2,1,0:T(8,128)(2,1)} %bitcast.63), calls=%async_computation | async-start | bytes 1769472 | tf_op jit(solution)/shard_map/all_to_all | solution.py:301
  376.7 163.4 %all-gather.37.cloned.1.call-start = ((), (), s32[]{:S(2)}) async-start(), calls=%async_computation.40 | async-start | bytes 1966080 | tf_op jit(solution)/shard_map/all_gather | solution.py:286
  431.7 128.9 %all-gather.39.cloned.1.call-start = ((), (), s32[]{:S(2)}) async-start(), calls=%async_computation.41 | async-start | bytes 1966080 | tf_op jit(solution)/shard_map/all_gather | solution.py:287
  432.5 153.0 %all-gather.55.cloned.1.call-start = ((), (), s32[]{:S(2)}) async-start(), calls=%async_computation.65 | async-start | bytes 1253376 | tf_op jit(solution)/shard_map/all_gather | solution.py:134
  433.1 178.2 %all-gather.57.cloned.1.call-start = ((), (), s32[]{:S(2)}) async-start(), calls=%async_computation.66 | async-start | bytes 6684672 | tf_op jit(solution)/shard_map/all_gather | solution.py:136
  433.8 210.2 %all-gather.59.cloned.1.call-start = ((), (), s32[]{:S(2)}) async-start(), calls=%async_computation.67 | async-start | bytes 3342336 | tf_op jit(solution)/shard_map/all_gather | solution.py:137
  434.4 252.3 %all-gather.41.cloned.1.call-start = ((), (), s32[]{:S(2)}) async-start(), calls=%async_computation.42 | async-start | bytes 7864320 | tf_op jit(solution)/shard_map/all_gather | solution.py:118
  479.8 237.5 %all-gather.43.cloned.1.call-start = ((), (), s32[]{:S(2)}) async-start(), calls=%async_computation.43 | async-start | bytes 3932160 | tf_op jit(solution)/shard_map/all_gather | solution.py:119
  920.1 173.5 %reduce-scatter.59.cloned.1.call-start = ((), (), s32[]{:S(2)}) async-start(), calls=%async_computation.59 | async-start | bytes 3932160 | tf_op jit(solution)/shard_map/reduce_scatter | solution.py:423
  977.7 134.5 %reduce-scatter.33.cloned.1.call-start = ((), (), s32[]{:S(2)}) async-start(), calls=%async_computation.46 | async-start | bytes 1966080 | tf_op jit(solution)/shard_map/reduce_scatter | solution.py:450
  1040.0 163.8 %reduce-scatter.55.cloned.1.call-start = ((), (), s32[]{:S(2)}) async-start(), calls=%async_computation.57 | async-start | bytes 7864320 | tf_op jit(solution)/shard_map/reduce_scatter | solution.py:420
  1049.8 215.0 %reduce-scatter.53.cloned.1.call-start = ((), (), s32[]{:S(2)}) async-start(), calls=%async_computation.56 | async-start | bytes 7864320 | tf_op jit(solution)/shard_map/reduce_scatter | solution.py:420
  1060.6 281.2 %reduce-scatter.43.cloned.1.call-start = ((), (), s32[]{:S(2)}) async-start(), calls=%async_computation.51 | async-start | bytes 1253376 | tf_op jit(solution)/shard_map/reduce_scatter | solution.py:474
  1063.3 347.6 %reduce-scatter.51.cloned.1.call-start = ((), (), s32[]{:S(2)}) async-start(), calls=%async_computation.55 | async-start | bytes 3342336 | tf_op jit(solution)/shard_map/reduce_scatter | solution.py:483
  1067.3 432.2 %reduce-scatter.47.cloned.1.call-start = ((), (), s32[]{:S(2)}) async-start(), calls=%async_computation.53 | async-start | bytes 6684672 | tf_op jit(solution)/shard_map/reduce_scatter | solution.py:480
  1074.4 486.8 %reduce-scatter.41.cloned.1.call-start = ((), (), s32[]{:S(2)}) async-start(), calls=%async_computation.50 | async-start | bytes 1253376 | tf_op jit(solution)/shard_map/reduce_scatter | solution.py:474
  1078.1 552.3 %reduce-scatter.49.cloned.1.call-start = ((), (), s32[]{:S(2)}) async-start(), calls=%async_computation.54 | async-start | bytes 3342336 | tf_op jit(solution)/shard_map/reduce_scatter | solution.py:483
  1082.1 619.4 %reduce-scatter.39.cloned.1.call-start = ((), (), s32[]{:S(2)}) async-start(), calls=%async_computation.49 | async-start | bytes 3760128 | tf_op jit(solution)/shard_map/reduce_scatter | solution.py:471
  1086.4 703.9 %reduce-scatter.45.cloned.1.call-start = ((), (), s32[]{:S(2)}) async-start(), calls=%async_computation.52 | async-start | bytes 6684672 | tf_op jit(solution)/shard_map/reduce_scatter | solution.py:480
  1109.6 751.7 %reduce-scatter.37.cloned.1.call-start = ((), (), s32[]{:S(2)}) async-start(), calls=%async_computation.48 | async-start | bytes 3760128 | tf_op jit(solution)/shard_map/reduce_scatter | solution.py:471
  1291.0 626.6 %reduce-scatter.67.cloned.1.call-start = ((), (), s32[]{:S(2)}) async-start(), calls=%async_computation.71 | async-start | bytes 208896
  1292.1 682.2 %reduce-scatter.63.cloned.1.call-start = ((), (), s32[]{:S(2)}) async-start(), calls=%async_computation.69 | async-start | bytes 208896
  1293.0 737.4 %reduce-scatter.65.cloned.1.call-start = ((), (), s32[]{:S(2)}) async-start(), calls=%async_computation.70 | async-start | bytes 208896
  1294.1 792.3 %reduce-scatter.61.cloned.1.call-start = ((), (), s32[]{:S(2)}) async-start(), calls=%async_computation.68 | async-start | bytes 208896
  1299.8 951.3 %all-reduce.12.cloned.1.call-start = ((), (), s32[]{:S(2)}) async-start(), calls=%async_computation.72 | async-start | bytes 12976128 | tf_op jit(solution)/shard_map/psum | solution.py:489
  (224 other events, 4321.7 us)
Sparse Core Ops, SparseCore 0:
  10.9 50.9 all-gather.44
  115.4 39.7 all-gather.46
  156.6 46.0 all-gather.32
  204.0 28.5 all-gather.34
  234.9 72.8 all-gather.48
  310.0 47.9 all-gather.50
  361.0 54.0 all-gather.52
  475.6 42.7 all-gather.54
  520.7 62.1 all-gather.56
  585.0 51.7 all-gather.58
  638.2 48.5 all-gather.40
  688.7 28.5 all-gather.42
  827.3 45.5 reduce-scatter.28
  926.6 37.8 reduce-scatter.58
  1031.4 39.4 reduce-scatter.32
  1074.0 28.1 reduce-scatter.34
  1104.9 37.9 reduce-scatter.56
  1145.4 58.3 reduce-scatter.54
  1206.4 58.3 reduce-scatter.52
  1268.4 73.3 reduce-scatter.42
  1346.0 64.8 reduce-scatter.50
  1415.3 84.1 reduce-scatter.46
  1503.5 57.6 reduce-scatter.40
  1565.5 64.8 reduce-scatter.48
  1634.6 66.8 reduce-scatter.38
  1706.0 84.2 reduce-scatter.44
  1794.2 67.1 reduce-scatter.36
  1864.7 52.8 reduce-scatter.66
  1921.7 52.5 reduce-scatter.62
  1977.8 52.5 reduce-scatter.64
  2033.8 52.5 reduce-scatter.60
  2090.6 160.4 all-reduce.11
  (5 shorter events, 105.8 us)
where the time goes:
time: 2290 us; the launch traced here: 2270 us
  waiting for transfers between devices  1250 us (55%)
  local copies, waits for them, and re-layouts  265 us (12%)
  blocking collectives  261 us (11%)
  matrix products  209 us (9%)
  other arithmetic  174 us (8%)
  starting transfers between devices  90.4 us (4%)
    unnamed x41, waiting for transfers between devices  218 us
    reduce_scatter x2, waiting for transfers between devices, layer_backward(): lax.psum_scatter(d_shared_first.astype(jnp.bfloat16), ('seq', 'fsdp'), sc...  177 us
    psum x1, waiting for transfers between devices, layer_backward(): lax.psum(qkv_part.astype(jnp.bfloat16), 'rep').astype(jnp.float32)  158 us
    reduce_scatter x2, waiting for transfers between devices, layer_backward(): lax.psum_scatter(d_qkv_weight.astype(jnp.bfloat16), ('seq', 'fsdp'), scat...  142 us
    reduce_scatter x2, waiting for transfers between devices, layer_backward(): lax.psum_scatter(d_shared_second.astype(jnp.bfloat16), ('seq', 'fsdp'), s...  138 us
    all_gather x2, blocking collectives, fetch_forward(): lax.all_gather(router_rows, ('seq', 'fsdp'), axis=0, tiled=True)  119 us
    unnamed x441, local copies, waits for them, and re-layouts  95.4 us
    reduce_scatter x2, waiting for transfers between devices, layer_backward(): lax.psum_scatter(d_first_here.astype(jnp.bfloat16), 'seq', scatter_dimens...  80.7 us
  transfers between devices with their start and end apart: 51, of which 27 were waited for; matrix products, arithmetic and copies ran while one was open for 22% of the time, Pallas kernels for 0%

commit v1 on v0

v1 whole, which is shorter than its diff:
```python
import functools

import jax
import jax.numpy as jnp
from jax import lax
from jax.experimental import pallas as pl
from jax.experimental.pallas import tpu as pltpu
from jax.sharding import PartitionSpec as P

D = 768
HEADS = 12
HEAD_DIM = 64
FF = 2048
EXPERTS = 4
LAYERS = 2
CAP = 144
EPS = 1e-06
MASKED = -1e30
SEQ = 4
FSDP = 4
HEADS_DEV = HEADS // SEQ
COLS = HEADS_DEV * HEAD_DIM
FF_DEV = FF // SEQ
FF_CORE = FF // 2
SLOTS = EXPERTS * CAP
bf16 = jnp.bfloat16
f32 = jnp.float32
MESH = pl.DeviceIdType.MESH

SIB = [(i, i ^ 1) for i in range(SEQ)]
FAR = [(i, i ^ 2) for i in range(SEQ)]


def dot(a, b):
    return jnp.dot(a, b, preferred_element_type=f32)


def dot_nt(a, b):
    return lax.dot_general(a, b, (((1,), (1,)), ((), ())), preferred_element_type=f32)


def dot_tn(a, b):
    return lax.dot_general(a, b, (((0,), (0,)), ((), ())), preferred_element_type=f32)


def exchange_kernel(x, o, send, recv, local_sem):
    z = lax.axis_index("fsdp")
    barrier = pltpu.get_barrier_semaphore()
    for k in (1, 2, 3):
        pl.semaphore_signal(
            barrier, inc=1, device_id={"fsdp": lax.rem(z + k, FSDP)}, device_id_type=MESH
        )
    pl.semaphore_wait(barrier, 3)
    copies = []
    for k in (2, 1, 3):
        peer = lax.rem(z + k, FSDP)
        copy = pltpu.make_async_remote_copy(
            src_ref=x.at[peer],
            dst_ref=o.at[z],
            send_sem=send.at[k],
            recv_sem=recv.at[k],
            device_id={"fsdp": peer},
            device_id_type=MESH,
        )
        copy.start()
        copies.append(copy)
    own = pltpu.make_async_copy(x.at[z], o.at[z], local_sem)
    own.start()
    own.wait()
    for copy in copies:
        copy.wait()


def exchange(x, cid):
    return pl.pallas_call(
        exchange_kernel,
        out_shape=jax.ShapeDtypeStruct(x.shape, x.dtype),
        in_specs=[pl.BlockSpec(memory_space=pltpu.VMEM)],
        out_specs=pl.BlockSpec(memory_space=pltpu.VMEM),
        scratch_shapes=[
            pltpu.SemaphoreType.DMA((4,)),
            pltpu.SemaphoreType.DMA((4,)),
            pltpu.SemaphoreType.DMA,
        ],
        compiler_params=pltpu.CompilerParams(
            collective_id=cid, has_side_effects=True, vmem_limit_bytes=32 << 20
        ),
    )(x)


def gather_seq(x):
    far = lax.ppermute(x, "seq", FAR)
    both = lax.ppermute(jnp.stack([x, far]), "seq", SIB)
    return jnp.concatenate([x, both[0], far, both[1]], 0)


def scatter_seq(partial):
    blocks = partial.astype(bf16).reshape(4, -1, partial.shape[-1])
    kept = partial.reshape(4, -1, partial.shape[-1])
    near = lax.ppermute(jnp.stack([blocks[1], blocks[3]]), "seq", SIB).astype(f32)
    away = (kept[2] + near[1]).astype(bf16)
    return kept[0] + near[0] + lax.ppermute(away, "seq", FAR).astype(f32)


def rep_pairs(reps):
    return [(i, i ^ 1) for i in range(reps)]


def rep_rest(x, reps):
    bit = 2
    while bit < reps:
        x = x + lax.ppermute(x, "rep", [(i, i ^ bit) for i in range(reps)])
        bit *= 2
    return x


def scatter_rep(x, reps, r):
    half = lax.rem(r, 2)
    mine = lax.dynamic_index_in_dim(x, half, 0, False)
    other = lax.dynamic_index_in_dim(x, 1 - half, 0, False)
    got = lax.ppermute(other, "rep", rep_pairs(reps))
    return rep_rest((mine.astype(f32) + got.astype(f32)).astype(bf16), reps)


def gather_rep(x, reps, r, axis):
    half = lax.rem(r, 2)
    got = lax.ppermute(x, "rep", rep_pairs(reps))
    return jnp.stack([jnp.where(half == 0, x, got), jnp.where(half == 0, got, x)], axis)


def absolute(blocks, s):
    return jnp.stack([lax.dynamic_index_in_dim(blocks, s ^ i, 0, False) for i in range(4)])


def fetch_dense(qkv, out, first, second):
    columns = jnp.concatenate(
        [
            qkv.reshape(48, 3, 4, COLS).transpose(2, 0, 1, 3).reshape(4, 48, 3 * COLS),
            first.reshape(48, 2, 4, FF_DEV).transpose(2, 0, 1, 3).reshape(4, 48, 2 * FF_DEV),
        ],
        2,
    )
    columns = lax.all_to_all(columns, "seq", split_axis=0, concat_axis=0, tiled=True)
    columns = lax.all_gather(columns, "fsdp", axis=1).reshape(D, -1)
    rows = lax.all_gather(jnp.concatenate([out, second], 0), "fsdp", axis=0)
    return (
        columns[:, : 3 * COLS],
        columns[:, 3 * COLS :],
        rows[:, :48].reshape(COLS, D),
        rows[:, 48:].reshape(FF_DEV, D),
    )


def fetch_expert(first, second, s):
    core = lax.rem(s, 2)
    far = s // 2
    first = lax.all_to_all(first, "fsdp", split_axis=0, concat_axis=0, tiled=True)
    first = first.reshape(4, 48, 2, 2, 2, FF_DEV)
    own = lax.dynamic_index_in_dim(first, core, 4, False).reshape(4, 48, 2 * FF_CORE)
    sent = lax.dynamic_index_in_dim(first, 1 - core, 4, False).reshape(4, 48, 2 * FF_CORE)
    pair = jnp.stack([own, lax.ppermute(sent, "seq", SIB)])
    pair = jnp.concatenate([pair, lax.ppermute(pair, "seq", FAR)], 0)
    first = absolute(pair, s).reshape(D, 2 * FF_CORE)
    second = lax.all_to_all(second, "fsdp", split_axis=0, concat_axis=0, tiled=True)
    other = lax.ppermute(second, "seq", FAR)
    second = jnp.stack([jnp.where(far == 0, second, other), jnp.where(far == 0, other, second)])
    return first, second.reshape(FF_CORE, D)


def return_dense(d_columns, d_rows, s, z, r, reps):
    width = d_columns.shape[1]
    d_columns = d_columns.astype(bf16).reshape(4, 4, 2, 24, width).transpose(2, 1, 0, 3, 4)
    d_columns = scatter_rep(d_columns, reps, r)
    d_columns = lax.psum_scatter(d_columns, "fsdp", scatter_dimension=0)
    d_columns = lax.all_to_all(d_columns, "seq", split_axis=0, concat_axis=0, tiled=True)
    d_columns = gather_rep(d_columns, reps, r, 1).reshape(4, 48, width)
    d_qkv = d_columns[..., : 3 * COLS].reshape(4, 48, 3, COLS).transpose(1, 2, 0, 3)
    d_first = d_columns[..., 3 * COLS :].reshape(4, 48, 2, FF_DEV).transpose(1, 2, 0, 3)
    d_rows = d_rows.astype(bf16).reshape(4, 2, 88, D).transpose(1, 0, 2, 3)
    d_rows = scatter_rep(d_rows, reps, r)
    d_rows = lax.psum_scatter(d_rows, "fsdp", scatter_dimension=0)
    d_rows = gather_rep(d_rows, reps, r, 0).reshape(176, D)
    return (
        d_qkv.reshape(48, 3 * D).astype(f32),
        d_rows[:48].astype(f32),
        d_first.reshape(48, 2 * FF).astype(f32),
        d_rows[48:].astype(f32),
    )


def return_expert(d_first, d_second, s, r, reps):
    core = lax.rem(s, 2)
    far = s // 2
    d_first = d_first.astype(bf16).reshape(2, 2, 4, 48, 2, 2, FF_DEV)
    d_first = scatter_rep(d_first.transpose(5, 0, 1, 2, 3, 4, 6), reps, r)
    mine = lax.dynamic_index_in_dim(d_first, far, 0, False)
    other = lax.dynamic_index_in_dim(d_first, 1 - far, 0, False)
    d_first = mine + lax.ppermute(other, "seq", FAR)
    own = lax.dynamic_index_in_dim(d_first, core, 0, False)
    sent = lax.dynamic_index_in_dim(d_first, 1 - core, 0, False)
    got = lax.ppermute(sent, "seq", SIB)
    d_first = jnp.stack([jnp.where(core == 0, own, got), jnp.where(core == 0, got, own)], 3)
    d_first = lax.all_to_all(d_first, "fsdp", split_axis=0, concat_axis=0, tiled=True)
    d_first = gather_rep(d_first, reps, r, 3).reshape(4, 48, 2 * FF)
    d_second = d_second.astype(bf16).reshape(2, 4, 2, 64, D).transpose(2, 0, 1, 3, 4)
    d_second = scatter_rep(d_second, reps, r)
    mine = lax.dynamic_index_in_dim(d_second, far, 0, False)
    other = lax.dynamic_index_in_dim(d_second, 1 - far, 0, False)
    d_second = mine + lax.ppermute(other, "seq", FAR)
    d_second = lax.all_to_all(d_second, "fsdp", split_axis=0, concat_axis=0, tiled=True)
    d_second = gather_rep(d_second, reps, r, 1).reshape(4, 128, D)
    return d_first.astype(f32), d_second.astype(f32)


def rms_forward(hidden_state, gain_row):
    factor = lax.rsqrt(jnp.mean(hidden_state * hidden_state, -1, keepdims=True) + EPS)
    return hidden_state * factor * gain_row, factor


def rms_backward(hidden_state, factor, gain_row, gradient):
    weighted = gradient * gain_row
    inner = jnp.mean(weighted * hidden_state, -1, keepdims=True)
    d_state = factor * weighted - hidden_state * (factor * factor * factor) * inner
    d_gain = jnp.sum(gradient * hidden_state * factor, 0)
    return d_state, d_gain


def swiglu(joint):
    half = joint.shape[-1] // 2
    return (jax.nn.silu(joint[..., :half]) * joint[..., half:]).astype(bf16)


def swiglu_back(joint, gradient):
    half = joint.shape[-1] // 2
    gate, up = joint[..., :half], joint[..., half:]
    sig = jax.nn.sigmoid(gate)
    d_gate = gradient * up * sig * (1.0 + gate * (1.0 - sig))
    d_up = gradient * gate * sig
    return jnp.concatenate([d_gate, d_up], -1).astype(bf16)


def routing(choices, order):
    tokens = choices.shape[0]
    pairs = 2 * tokens
    flat = choices.reshape(-1)
    ids = jnp.arange(pairs, dtype=jnp.int32)
    place = (order[:, None] == ids[None, :]).astype(bf16)
    experts = (flat[:, None] == jnp.arange(EXPERTS, dtype=jnp.int32)[None, :]).astype(bf16)
    placed = dot(place, experts).astype(bf16)
    lower = (ids[:, None] > ids[None, :]).astype(bf16)
    slot_placed = jnp.minimum(jnp.sum(dot(lower, placed) * placed.astype(f32), 1), float(CAP))
    slot = dot_tn(place, slot_placed[:, None].astype(bf16))[:, 0].astype(jnp.int32)
    kept = slot < CAP
    target = jnp.where(kept, flat * CAP + slot, SLOTS).reshape(tokens, 2)
    target = target.T.reshape(-1)
    chosen = (target[None, :] == jnp.arange(SLOTS, dtype=jnp.int32)[:, None]).astype(bf16)
    return kept.reshape(tokens, 2).astype(f32), chosen


def rotate(x, cosine, sine):
    half = HEAD_DIM // 2
    a, b = x[..., :half], x[..., half:]
    return jnp.concatenate([a * cosine - b * sine, b * cosine + a * sine], -1)


def attention(queries, keys, values, visible):
    scores = jnp.einsum("qhd,khd->hqk", queries, keys, preferred_element_type=f32)
    scores = jnp.where(visible[None], scores * HEAD_DIM**-0.5, MASKED)
    top = jnp.max(scores, -1, keepdims=True)
    total = top + jnp.log(jnp.sum(jnp.exp(scores - top), -1, keepdims=True))
    weights = jnp.exp(scores - total).astype(bf16)
    return jnp.einsum("hqk,khd->qhd", weights, values, preferred_element_type=f32), total


def attention_back(queries, keys, values, visible, total, attended, d_attended):
    scale = HEAD_DIM**-0.5
    scores = jnp.einsum("qhd,khd->hqk", queries, keys, preferred_element_type=f32)
    scores = jnp.where(visible[None], scores * scale, MASKED)
    weights = jnp.exp(scores - total)
    delta = jnp.sum(d_attended.astype(f32) * attended, -1).T[..., None]
    d_weights = jnp.einsum("qhd,khd->hqk", d_attended, values, preferred_element_type=f32)
    d_scores = (weights * (d_weights - delta)).astype(bf16)
    d_q = jnp.einsum("hqk,khd->qhd", d_scores, keys, preferred_element_type=f32) * scale
    d_k = jnp.einsum("hqk,qhd->khd", d_scores, queries, preferred_element_type=f32) * scale
    d_v = jnp.einsum("hqk,qhd->khd", weights.astype(bf16), d_attended, preferred_element_type=f32)
    return d_q, d_k, d_v


def layer_forward(layer, h, dense, expert, gains, router, choices, routes, cosine, sine, visible):
    w_qkv, w_first, w_out, w_second = dense
    e_first, e_second = expert
    kept, chosen = routes
    tokens = h.shape[0]
    normed, factor_one = rms_forward(h, gains[0])
    normed_all = gather_seq(normed.astype(bf16))
    joint = dot(normed_all, w_qkv).reshape(-1, 3, HEADS_DEV, HEAD_DIM)
    queries = rotate(joint[:, 0], cosine, sine).astype(bf16)
    keys = rotate(joint[:, 1], cosine, sine).astype(bf16)
    values = joint[:, 2].astype(bf16)
    attended, total = attention(queries, keys, values, visible)
    attended_low = attended.reshape(-1, COLS).astype(bf16)
    middle = h + scatter_seq(dot(attended_low, w_out))
    normed, factor_two = rms_forward(middle, gains[1])
    second = normed.astype(bf16)
    logits = dot(second, router)
    onehot = (choices[..., None] == jnp.arange(EXPERTS, dtype=jnp.int32)).astype(f32)
    gates = jax.nn.softmax(jnp.sum(onehot * logits[:, None, :], -1), -1)
    second_all = gather_seq(second)
    joint_shared = dot(second_all, w_first)
    hidden_shared = swiglu(joint_shared)
    shared_part = dot(hidden_shared, w_second)
    picked = chosen[:, :tokens] + chosen[:, tokens:]
    rows = dot(picked, second).astype(bf16).reshape(EXPERTS, CAP, D)
    rows = exchange(rows, 1 + 4 * layer).reshape(SLOTS, D)
    rows_all = jnp.concatenate([rows, lax.ppermute(rows, "seq", SIB)], 0)
    joint_expert = dot(rows_all, e_first)
    hidden_expert = swiglu(joint_expert)
    produced = dot(hidden_expert, e_second)
    got = lax.ppermute(produced[SLOTS:].astype(bf16), "seq", SIB)
    produced = (produced[:SLOTS] + got.astype(f32)).astype(bf16)
    yields = exchange(produced.reshape(EXPERTS, CAP, D), 2 + 4 * layer).reshape(SLOTS, D)
    gathered = dot_tn(chosen, yields)
    mixture = gates[:, :1] * gathered[:tokens] + gates[:, 1:] * gathered[tokens:]
    result = middle + scatter_seq(shared_part) + mixture
    stored = (
        h, factor_one, normed_all, queries, keys, values, total, attended, attended_low, middle,
        factor_two, second, gates, onehot, second_all, joint_shared, hidden_shared, rows_all,
        joint_expert, hidden_expert, gathered,
    )
    return result, stored


def layer_backward(layer, grad, dense, expert, gains, router, routes, stored, cosine, sine, visible):
    w_qkv, w_first, w_out, w_second = dense
    e_first, e_second = expert
    kept, chosen = routes
    (
        h, factor_one, normed_all, queries, keys, values, total, attended, attended_low, middle,
        factor_two, second, gates, onehot, second_all, joint_shared, hidden_shared, rows_all,
        joint_expert, hidden_expert, gathered,
    ) = stored
    tokens = grad.shape[0]
    scaled = gates * kept
    d_yields = jnp.concatenate([grad * scaled[:, :1], grad * scaled[:, 1:]], 0).astype(bf16)
    d_yields = dot(chosen, d_yields).astype(bf16).reshape(EXPERTS, CAP, D)
    d_rows = exchange(d_yields, 3 + 4 * layer).reshape(SLOTS, D)
    d_rows = jnp.concatenate([d_rows, lax.ppermute(d_rows, "seq", SIB)], 0)
    de_second = dot_tn(hidden_expert, d_rows)
    d_joint = swiglu_back(joint_expert, dot_nt(d_rows, e_second))
    de_first = dot_tn(rows_all, d_joint)
    back = dot_nt(d_joint, e_first)
    got = lax.ppermute(back[SLOTS:].astype(bf16), "seq", SIB)
    back = (back[:SLOTS] + got.astype(f32)).astype(bf16)
    back = exchange(back.reshape(EXPERTS, CAP, D), 4 + 4 * layer).reshape(SLOTS, D)
    picked = chosen[:, :tokens] + chosen[:, tokens:]

    grad_all = gather_seq(grad.astype(bf16))
    d_second_w = dot_tn(hidden_shared, grad_all)
    d_joint_shared = swiglu_back(joint_shared, dot_nt(grad_all, w_second))
    d_first_w = dot_tn(second_all, d_joint_shared)
    d_normed = scatter_seq(dot_nt(d_joint_shared, w_first))

    d_gates = kept * jnp.stack(
        [jnp.sum(grad * gathered[:tokens], -1), jnp.sum(grad * gathered[tokens:], -1)], -1
    )
    d_chosen = gates * (d_gates - jnp.sum(gates * d_gates, -1, keepdims=True))
    d_logits = jnp.sum(d_chosen[..., None] * onehot, 1).astype(bf16)
    d_router = dot_tn(second, d_logits)
    d_normed = d_normed + dot_nt(d_logits, router) + dot_tn(picked, back)
    d_middle, d_gain_two = rms_backward(middle, factor_two, gains[1], d_normed)
    d_middle = grad + d_middle
    middle_all = gather_seq(d_middle.astype(bf16))
    d_out_w = dot_tn(attended_low, middle_all)
    d_attended = dot_nt(middle_all, w_out).astype(bf16).reshape(-1, HEADS_DEV, HEAD_DIM)
    d_q, d_k, d_v = attention_back(queries, keys, values, visible, total, attended, d_attended)
    d_qkv = jnp.stack([rotate(d_q, cosine, -sine), rotate(d_k, cosine, -sine), d_v], 1)
    d_qkv = d_qkv.reshape(-1, 3 * COLS).astype(bf16)
    d_qkv_w = dot_tn(normed_all, d_qkv)
    d_first = scatter_seq(dot_nt(d_qkv, w_qkv))
    d_state, d_gain_one = rms_backward(h, factor_one, gains[0], d_first)
    d_columns = jnp.concatenate([d_qkv_w, d_first_w], 1)
    d_rows_w = jnp.concatenate([d_out_w.reshape(4, 48, D), d_second_w.reshape(4, 128, D)], 1)
    small = jnp.concatenate([jnp.stack([d_gain_one, d_gain_two]), d_router.T], 0)
    return d_middle + d_state, (d_columns, d_rows_w), (de_first, de_second), small


def local(
    reps, inputs, expert_choice, pair_order, norm_gains, attn_qkv, attn_out, router, shared_in,
    shared_out, expert_in, expert_out, cotangent,
):
    r, s, z = lax.axis_index("rep"), lax.axis_index("seq"), lax.axis_index("fsdp")
    tokens = inputs.shape[1]
    position = jnp.concatenate([(s ^ j) * tokens + jnp.arange(tokens, dtype=jnp.int32) for j in range(4)])
    half = HEAD_DIM // 2
    inverse = jnp.exp(-jnp.log(10000.0) * jnp.arange(half, dtype=f32) * 2.0 / HEAD_DIM)
    angle = position.astype(f32)[:, None] * inverse[None, :]
    cosine, sine = jnp.cos(angle)[:, None, :], jnp.sin(angle)[:, None, :]
    visible = position[:, None] >= position[None, :]
    small = jnp.concatenate([norm_gains, router.transpose(0, 2, 1)], 1)
    small = lax.all_gather(small, ("seq", "fsdp"), axis=2, tiled=True)
    gains = small[:, :2].astype(f32)
    routers = small[:, 2:].transpose(0, 2, 1)
    h = inputs[0].astype(f32)
    kept_layers = []
    for layer in range(LAYERS):
        dense = fetch_dense(attn_qkv[layer], attn_out[layer], shared_in[layer], shared_out[layer])
        expert = fetch_expert(expert_in[layer], expert_out[layer], s)
        routes = routing(expert_choice[layer, 0], pair_order[layer, 0, 0])
        h, stored = layer_forward(
            layer, h, dense, expert, gains[layer], routers[layer], expert_choice[layer, 0], routes,
            cosine, sine, visible,
        )
        kept_layers.append((dense, expert, routes, stored))
    output = h.astype(bf16)[None]
    grad = cotangent[0].astype(f32)
    grads = [None] * LAYERS
    smalls = [None] * LAYERS
    for layer in reversed(range(LAYERS)):
        dense, expert, routes, stored = kept_layers[layer]
        grad, d_dense, d_expert, smalls[layer] = layer_backward(
            layer, grad, dense, expert, gains[layer], routers[layer], routes, stored, cosine, sine,
            visible,
        )
        grads[layer] = return_dense(*d_dense, s, z, r, reps) + return_expert(*d_expert, s, r, reps)
    total = lax.psum(jnp.stack(smalls), ("rep", "seq", "fsdp"))
    total = lax.dynamic_slice_in_dim(total, (s * FSDP + z) * 48, 48, 2)
    d_qkv, d_out, d_in, d_so, d_ein, d_eout = (
        jnp.stack([grads[layer][k] for layer in range(LAYERS)]) for k in range(6)
    )
    return (
        output, grad[None], total[:, :2], d_qkv, d_out, total[:, 2:].transpose(0, 2, 1), d_in, d_so,
        d_ein, d_eout,
    )


def solution(mesh):
    tokens = P(("rep", "fsdp"), "seq", None)
    routes = P(None, ("rep", "fsdp"), "seq", None)
    gains = P(None, None, ("seq", "fsdp"))
    dense = P(None, ("seq", "fsdp"), None)
    expert = P(None, None, ("seq", "fsdp"), None)
    in_specs = (
        tokens, routes, routes, gains, dense, dense, dense, dense, dense, expert, expert, tokens,
    )
    out_specs = (tokens, tokens, gains, dense, dense, dense, dense, dense, expert, expert)
    return jax.shard_map(
        functools.partial(local, mesh.shape["rep"]),
        mesh=mesh, in_specs=in_specs, out_specs=out_specs, check_vma=False,
    )
```

time: 2290 us -> 1280 us (0.56)
  waiting for transfers between devices: 1250 us -> 264 us
  Pallas kernels: 0 us -> 181 us
  blocking collectives: 261 us -> 152 us
  local copies, waits for them, and re-layouts: 265 us -> 211 us
  matrix products: 209 us -> 180 us
    reduce_scatter x16 -> x4, waiting for transfers between devices: 699 us -> 0.01 us  [the longest x2 0.01 us: return_dense(): d_rows = lax.psum_scatter(d_rows, 'fsdp', scatter_dimension=0)]
    ppermute x0 -> x68, waiting for transfers between devices: none -> 229 us  [the longest x8 128 us: scatter_rep(): got = lax.ppermute(other, 'rep', rep_pairs(reps))]
    unnamed x41 -> x8, waiting for transfers between devices: 218 us -> 0.13 us
    pallas_call x0 -> x8, Pallas kernels: none -> 181 us  [exchange(): pl.pallas_call(exchange_kernel, out_shape=jax.ShapeDtypeStruct(x.shape, x...]
    psum x1 -> x0, waiting for transfers between devices: 158 us -> none  [layer_backward(): lax.psum(qkv_part.astype(jnp.bfloat16), 'rep').astype(jnp.float32)]
    all_gather x4 -> x1, blocking collectives: 188 us -> 95.7 us  [local(): small = lax.all_gather(small, ('seq', 'fsdp'), axis=2, tiled=True)]
    all_to_all x14 -> x11, waiting for transfers between devices: 109 us -> 34.5 us  [the longest x2 15.7 us: fetch_expert(): lax.all_to_all(first, 'fsdp', split_axis=0, concat_axis=0, tiled=True)]
    all_gather x16 -> x4, waiting for transfers between devices: 66.1 us -> 0.03 us  [the longest x2 0.02 us: fetch_dense(): rows = lax.all_gather(jnp.concatenate([out, second], 0), 'fsdp', axis=0)]
  transfers between devices with their start and end apart: 51 -> 87, of which waited for: 27 -> 23; matrix products, arithmetic and copies ran while one was open for 22% -> 38% of each run, Pallas kernels for 0% -> 14%
where the time goes in v1:
time: 1280 us; the launch traced here: 1270 us
  waiting for transfers between devices  264 us (21%)
  local copies, waits for them, and re-layouts  211 us (16%)
  Pallas kernels  181 us (14%)
  matrix products  180 us (14%)
  other arithmetic  157 us (12%)
  blocking collectives  152 us (12%)
  starting transfers between devices  107 us (8%)
  between operations  18.1 us (1%)
    pallas_call x8, Pallas kernels, exchange(): pl.pallas_call(exchange_kernel, out_shape=jax.ShapeDtypeStruct(x.shape, x...  181 us
    ppermute x8, waiting for transfers between devices, scatter_rep(): got = lax.ppermute(other, 'rep', rep_pairs(reps))  128 us
    all_gather x1, blocking collectives, local(): small = lax.all_gather(small, ('seq', 'fsdp'), axis=2, tiled=True)  95.7 us
    dot_general x20, matrix products, dot_tn(): lax.dot_general(a, b, (((0,), (0,)), ((), ())), preferred_element_type=f32)  51.1 us
    psum x1, blocking collectives, local(): total = lax.psum(jnp.stack(smalls), ('rep', 'seq', 'fsdp'))  43.6 us
    dot_general x14, matrix products, dot_nt(): lax.dot_general(a, b, (((1,), (1,)), ((), ())), preferred_element_type=f32)  41.8 us
    dot_general x22, matrix products, dot(): return jnp.dot(a, b, preferred_element_type=f32)  37.6 us
    unnamed x438, local copies, waits for them, and re-layouts  35.7 us
  transfers between devices with their start and end apart: 87, of which 23 were waited for; matrix products, arithmetic and copies ran while one was open for 38% of the time, Pallas kernels for 14%

profile of v1, /device:TPU:8, one launch (start us, length us, event | category | flops | bytes accessed | tf_op | source)
XLA Modules:
  0.0 1269.0 jit_solution(6787788359317297444)
XLA Ops:
  14.7 13.2 %all_to_all.60 = bf16[4,48,1600]{2,1,0:T(8,128)(2,1)} all-to-all(bf16[4,48,1600]{2,1,0:T(8,128)(2,1)S(1)} %pad_maximum_fusion.64), channel_id=1, replica_groups=mesh['rep'=2,'seq'=4,'fsdp'=4] {'seq'}, dimensions={0} | all-to-all | bytes 1228800 | tf_op jit(solution)/shard_map/all_to_all | solution.py:143
  39.4 15.6 %all-to-all-done.5 = bf16[4,128,768]{2,1,0:T(8,128)(2,1)} async-done(((bf16[4,128,768]{2,1,0:T(8,128)(2,1)}), bf16[4,128,768]{2,1,0:T(8,128)(2,1)}, u32[]{:S(2)}, u32[]{:S(2)}) %all-to-all-start.5) | async-done | bytes 786464 | tf_op jit(solution)/shard_map/all_to_all | solution.py:164
  55.0 7.4 all-to-all-start.4
  62.5 95.7 %all_gather.27 = bf16[2,6,768]{1,0,2:T(2,128)(2,1)S(1)} all-gather(bf16[2,6,48]{1,0,2:T(2,128)(2,1)S(1)} %pad_maximum_fusion.99), channel_id=1, replica_groups=mesh['rep'=2,'seq'=4,'fsdp'=4] {'seq','fsdp'}, dimensions={2}, use_global_device_ids=true | all-gather | bytes 19584 | tf_op jit(solution)/shard_map/all_gather | solution.py:400
  159.2 9.8 slice_reduce_fusion
  175.6 7.8 all-to-all-start.1
  215.5 15.7 %all-to-all-done.1 = bf16[4,48,4096]{2,1,0:T(8,128)(2,1)S(1)} async-done(((bf16[4,48,4096]{2,1,0:T(8,128)(2,1)}), bf16[4,48,4096]{2,1,0:T(8,128)(2,1)S(1)}, u32[]{:S(2)}, u32[]{:S(2)}) %all-to-all-start.1) | async-done | bytes 1572896 | tf_op jit(solution)/shard_map/all_to_all | solution.py:157
  231.2 7.4 all-to-all-start.2
  244.8 22.5 %dynamic-slice_reduce_fusion.1 = (bf16[4,48,2,2,512]{4,3,2,1,0:T(2,128)(2,1)}, bf16[4,48,2,2,512]{4,3,2,1,0:T(2,128)(2,1)}, bf16[4,48,2,2,512]{4,3,2,1,0:T(2,128)(2,1)}, bf16[4,48,2,2,512]{4,3,2,1,0:T(2,128)(2,1)}) fusion(bf16[4,48,2,2,2,512]{5,4,3,2,1,0:T(2,128)(2,1)S(1)} %reshape.876, s32[]{:T(128)S(6)} %select_n.220, s32[]{:T(128)S(6)} %select_n.221, ...), kind=kLoop, calls=%fused_computation.113 | loop fusion | bytes 6291464 | tf_op jit(solution)/shard_map/jit(dynamic_index_in_dim)/dynamic_slice | solution.py:159
  326.0 27.0 %collective-permute-done.10 = bf16[2,4,48,2048]{3,2,1,0:T(8,128)(2,1)} collective-permute-done((bf16[2,4,48,2048]{3,2,1,0:T(8,128)(2,1)}, bf16[2,4,48,2048]{3,2,1,0:T(8,128)(2,1)}, u32[]{:S(2)}, u32[]{:S(2)}) %collective-permute-start.10) | collective-permute-done | bytes 1572896 | tf_op jit(solution)/shard_map/ppermute | solution.py:162
  363.1 22.4 %shard_map.195 = bf16[4,144,768]{2,1,0:T(8,128)(2,1)S(1)} custom-call(bf16[4,144,768]{2,1,0:T(8,128)(2,1)S(1)} %bitcast.705), custom_call_target="tpu_custom_call" | custom-call | tf_op jit(solution)/shard_map/pallas_call | solution.py:75
  388.0 9.6 collective-permute-done.4
  423.7 21.9 %shard_map.196 = bf16[4,144,768]{2,1,0:T(8,128)(2,1)S(1)} custom-call(bf16[4,144,768]{2,1,0:T(8,128)(2,1)S(1)} %bitcast.699), custom_call_target="tpu_custom_call" | custom-call | tf_op jit(solution)/shard_map/pallas_call | solution.py:75
  484.6 7.3 exponential_reduce_fusion
  492.0 7.3 fusion.242
  534.2 20.8 %shard_map.197 = bf16[4,144,768]{2,1,0:T(8,128)(2,1)S(1)} custom-call(bf16[4,144,768]{2,1,0:T(8,128)(2,1)S(1)} %bitcast.706), custom_call_target="tpu_custom_call" | custom-call | tf_op jit(solution)/shard_map/pallas_call | solution.py:75
  558.3 22.2 %shard_map.199 = bf16[4,144,768]{2,1,0:T(8,128)(2,1)S(1)} custom-call(bf16[4,144,768]{2,1,0:T(8,128)(2,1)S(1)} %bitcast.721), custom_call_target="tpu_custom_call" | custom-call | tf_op jit(solution)/shard_map/pallas_call | solution.py:75
  605.1 7.0 convolution_convert_fusion
  618.4 11.6 constant_dynamic-slice_fusion.2
  652.1 33.4 %collective-permute-done.65 = bf16[2,4,64,768]{3,2,1,0:T(8,128)(2,1)S(1)} collective-permute-done((bf16[2,4,64,768]{3,2,1,0:T(8,128)(2,1)S(1)}, bf16[2,4,64,768]{3,2,1,0:T(8,128)(2,1)S(1)}, u32[]{:S(2)}, u32[]{:S(2)}) %collective-permute-start.65) | collective-permute-done | bytes 786464 | tf_op jit(solution)/shard_map/ppermute | solution.py:121
  688.1 21.8 %shard_map.198 = bf16[4,144,768]{2,1,0:T(8,128)(2,1)S(1)} custom-call(bf16[4,144,768]{2,1,0:T(8,128)(2,1)S(1)} %bitcast.700), custom_call_target="tpu_custom_call" | custom-call | tf_op jit(solution)/shard_map/pallas_call | solution.py:75
  711.2 20.9 %shard_map.200 = bf16[4,144,768]{2,1,0:T(8,128)(2,1)S(1)} custom-call(bf16[4,144,768]{2,1,0:T(8,128)(2,1)S(1)} %bitcast.701), custom_call_target="tpu_custom_call" | custom-call | tf_op jit(solution)/shard_map/pallas_call | solution.py:75
  774.8 9.4 collective-permute-done.59
  825.5 28.3 %collective-permute-done.52 = bf16[4,88,768]{2,1,0:T(8,128)(2,1)S(1)} collective-permute-done((bf16[4,88,768]{2,1,0:T(8,128)(2,1)}, bf16[4,88,768]{2,1,0:T(8,128)(2,1)S(1)}, u32[]{:S(2)}, u32[]{:S(2)}) %collective-permute-start.52) | collective-permute-done | bytes 540704 | tf_op jit(solution)/shard_map/ppermute | solution.py:121
  860.2 30.5 %shard_map.201 = bf16[4,144,768]{2,1,0:T(8,128)(2,1)S(1)} custom-call(bf16[4,144,768]{2,1,0:T(8,128)(2,1)S(1)} %bitcast.720), custom_call_target="tpu_custom_call" | custom-call | tf_op jit(solution)/shard_map/pallas_call | solution.py:75
  933.2 15.2 %constant_dynamic-slice_fusion.4 = (bf16[2,2,4,48,2,1,512]{6,5,4,3,2,1,0:T(2,128)(2,1)}, bf16[2,2,4,48,2,1,512]{6,5,4,3,2,1,0:T(2,128)(2,1)}) fusion(bf16[2,2,4,48,2,2,512]{6,5,4,3,2,1,0:T(2,128)(2,1)} %reshape.898, s32[]{:T(128)S(6)} %select_n.236, s32[]{:T(128)S(6)} %select_n.237), kind=kLoop, calls=%fused_computation.493 | loop fusion | bytes 6291464 | tf_op jit(solution)/shard_map/dynamic-slice.8
  980.5 33.3 %collective-permute-done.62 = bf16[2,4,64,768]{3,2,1,0:T(8,128)(2,1)S(1)} collective-permute-done((bf16[2,4,64,768]{3,2,1,0:T(8,128)(2,1)S(1)}, bf16[2,4,64,768]{3,2,1,0:T(8,128)(2,1)S(1)}, u32[]{:S(2)}, u32[]{:S(2)}) %collective-permute-start.62) | collective-permute-done | bytes 786464 | tf_op jit(solution)/shard_map/ppermute | solution.py:121
  1018.6 20.4 %shard_map.202 = bf16[4,144,768]{2,1,0:T(8,128)(2,1)S(1)} custom-call(bf16[4,144,768]{2,1,0:T(8,128)(2,1)S(1)} %bitcast.702), custom_call_target="tpu_custom_call" | custom-call | tf_op jit(solution)/shard_map/pallas_call | solution.py:75
  1090.0 6.9 convolution_bitcast_fusion
  1122.1 32.5 %collective-permute-done.50 = bf16[4,88,768]{2,1,0:T(8,128)(2,1)S(1)} collective-permute-done((bf16[4,88,768]{2,1,0:T(8,128)(2,1)S(1)}, bf16[4,88,768]{2,1,0:T(8,128)(2,1)S(1)}, u32[]{:S(2)}, u32[]{:S(2)}) %collective-permute-start.50) | collective-permute-done | bytes 540704 | tf_op jit(solution)/shard_map/ppermute | solution.py:121
  1174.3 43.6 %psum.7 = f32[2,6,768]{2,1,0:T(8,128)S(1)} all-reduce(f32[2,6,768]{2,1,0:T(8,128)S(1)} %pad_maximum_fusion.98), channel_id=1, replica_groups=mesh['rep'=2,'seq'=4,'fsdp'=4] {'rep','seq','fsdp'}, use_global_device_ids=true, to_apply=%region_34.35 | all-reduce | flops 9216 | bytes 73728 | tf_op jit(solution)/shard_map/psum | solution.py:425
  1234.1 9.1 collective-permute-done.57
  (963 shorter events, 593.3 us)
Async XLA Ops:
  7.2 276.2 %all-gather.11.cloned.1.call-start = ((), (), s32[]{:S(2)}) async-start(), calls=%async_computation.21 | async-start | bytes 1351680 | tf_op jit(solution)/shard_map/all_gather | solution.py:145
  11.3 276.2 %all-gather.9.cloned.1.call-start = ((), (), s32[]{:S(2)}) async-start(), calls=%async_computation.20 | async-start | bytes 3194880 | tf_op jit(solution)/shard_map/all_gather | solution.py:144
  55.0 120.6 %all-to-all-start.4 = ((bf16[4,48,4096]{2,1,0:T(8,128)(2,1)}), bf16[4,48,4096]{2,1,0:T(8,128)(2,1)S(1)}, u32[]{:S(2)}, u32[]{:S(2)}) async-start(bf16[4,48,4096]{2,1,0:T(8,128)(2,1)} %get-tuple-element.67), calls=%async_computation.4 | async-start | bytes 3145728 | tf_op jit(solution)/shard_map/all_to_all | solution.py:157
  62.4 405.2 %all-gather.15.cloned.1.call-start = ((), (), s32[]{:S(2)}) async-start(), calls=%async_computation.23 | async-start | bytes 1351680 | tf_op jit(solution)/shard_map/all_gather | solution.py:145
  169.9 68.7 %collective-permute-start = (bf16[256,768]{1,0:T(8,128)(2,1)}, bf16[256,768]{1,0:T(8,128)(2,1)}, u32[]{:S(2)}, u32[]{:S(2)}) collective-permute-start(bf16[256,768]{1,0:T(8,128)(2,1)} %fusion.72), channel_id=1, source_target_pairs={{0,8},{4,12},{8,0},{12,4},{1,9},{5,13},{9,1},{13,5},{2,10},{6,14},... | collective-permute-start | bytes 1179656 | tf_op jit(solution)/shard_map/ppermute | solution.py:92
  171.3 278.6 %collective-permute-start.26 = (bf16[256,768]{1,0:T(8,128)(2,1)}, bf16[256,768]{1,0:T(8,128)(2,1)}, u32[]{:S(2)}, u32[]{:S(2)}) collective-permute-start(bf16[256,768]{1,0:T(8,128)(2,1)} %bitcast.99), channel_id=1, source_target_pairs={{0,8},{4,12},{8,0},{12,4},{1,9},{5,13},{9,1},{13,5},{2,10},{6,14},... | collective-permute-start | bytes 1179656 | tf_op jit(solution)/shard_map/ppermute | solution.py:92
  175.6 55.7 %all-to-all-start.1 = ((bf16[4,48,4096]{2,1,0:T(8,128)(2,1)}), bf16[4,48,4096]{2,1,0:T(8,128)(2,1)S(1)}, u32[]{:S(2)}, u32[]{:S(2)}) async-start(bf16[4,48,4096]{2,1,0:T(8,128)(2,1)} %get-tuple-element.66), calls=%async_computation.1 | async-start | bytes 3145728 | tf_op jit(solution)/shard_map/all_to_all | solution.py:157
  231.2 44.8 %all-to-all-start.2 = ((bf16[4,128,768]{2,1,0:T(8,128)(2,1)}), bf16[4,128,768]{2,1,0:T(8,128)(2,1)}, u32[]{:S(2)}, u32[]{:S(2)}) async-start(bf16[4,128,768]{2,1,0:T(8,128)(2,1)} %get-tuple-element.98), calls=%async_computation.2 | async-start | bytes 1572864 | tf_op jit(solution)/shard_map/all_to_all | solution.py:164
  280.2 193.4 %all-gather.13.cloned.1.call-start = ((), (), s32[]{:S(2)}) async-start(), calls=%async_computation.22 | async-start | bytes 3194880 | tf_op jit(solution)/shard_map/all_gather | solution.py:144
  287.4 65.7 %collective-permute-start.10 = (bf16[2,4,48,2048]{3,2,1,0:T(8,128)(2,1)}, bf16[2,4,48,2048]{3,2,1,0:T(8,128)(2,1)}, u32[]{:S(2)}, u32[]{:S(2)}) collective-permute-start(bf16[2,4,48,2048]{3,2,1,0:T(8,128)(2,1)} %pad_maximum_fusion.18), channel_id=1, source_target_pairs={{0,8},{4,12},{8,0},{12,4},{1,9},{5,13},{9,1},{13,5},{2,10},{6,14},... | collective-permute-start | bytes 4718600 | tf_op jit(solution)/shard_map/ppermute | solution.py:162
  531.3 49.4 %collective-permute-start.17 = (bf16[256,768]{1,0:T(8,128)(2,1)}, bf16[256,768]{1,0:T(8,128)(2,1)}, u32[]{:S(2)}, u32[]{:S(2)}) collective-permute-start(bf16[256,768]{1,0:T(8,128)(2,1)} %multiply_convert_fusion.16), channel_id=1, source_target_pairs={{0,8},{4,12},{8,0},{12,4},{1,9},{5,13},{9,1},{13,5},{2,10},{6,14},... | collective-permute-start | bytes 1179656 | tf_op jit(solution)/shard_map/ppermute | solution.py:92
  582.7 53.8 %collective-permute-start.18 = (bf16[2,256,768]{2,1,0:T(8,128)(2,1)}, bf16[2,256,768]{2,1,0:T(8,128)(2,1)}, u32[]{:S(2)}, u32[]{:S(2)}) collective-permute-start(bf16[2,256,768]{2,1,0:T(8,128)(2,1)} %pad_maximum_fusion.50), channel_id=1, source_target_pairs={{0,4},{4,0},{8,12},{12,8},{1,5},{5,1},{9,13},{13,9},{2,6},{6,2},{1... | collective-permute-start | bytes 2359304 | tf_op jit(solution)/shard_map/ppermute | solution.py:93
  597.6 88.2 %collective-permute-start.25 = (bf16[576,768]{1,0:T(8,128)(2,1)}, bf16[576,768]{1,0:T(8,128)(2,1)}, u32[]{:S(2)}, u32[]{:S(2)}) collective-permute-start(bf16[576,768]{1,0:T(8,128)(2,1)} %slice.1212), channel_id=1, source_target_pairs={{0,4},{4,0},{8,12},{12,8},{1,5},{5,1},{9,13},{13,9},{2,6},{6,2},{1... | collective-permute-start | bytes 2654216 | tf_op jit(solution)/shard_map/ppermute | solution.py:319
  605.0 104.8 %collective-permute-start.31 = (bf16[576,768]{1,0:T(8,128)(2,1)}, bf16[576,768]{1,0:T(8,128)(2,1)}, u32[]{:S(2)}, u32[]{:S(2)}) collective-permute-start(bf16[576,768]{1,0:T(8,128)(2,1)} %slice.1211), channel_id=1, source_target_pairs={{0,4},{4,0},{8,12},{12,8},{1,5},{5,1},{9,13},{13,9},{2,6},{6,2},{1... | collective-permute-start | bytes 2654216 | tf_op jit(solution)/shard_map/ppermute | solution.py:352
  631.7 128.2 %collective-permute-start.58 = (bf16[2,2,4,48,2,512]{5,3,4,2,1,0:T(8,128)(2,1)}, bf16[2,2,4,48,2,512]{5,3,4,2,1,0:T(8,128)(2,1)}, u32[]{:S(2)}, u32[]{:S(2)}) collective-permute-start(bf16[2,2,4,48,2,512]{5,3,4,2,1,0:T(8,128)(2,1)} %bitcast.691), channel_id=1, source_target_pairs={{0,16},{16,0},{1,17},{17,1},{2,18},{18,2},{3,19},{19,3},{4,20},{20... | collective-permute-start | bytes 4718600 | tf_op jit(solution)/shard_map/ppermute | solution.py:121
  635.6 49.9 %collective-permute-start.65 = (bf16[2,4,64,768]{3,2,1,0:T(8,128)(2,1)S(1)}, bf16[2,4,64,768]{3,2,1,0:T(8,128)(2,1)S(1)}, u32[]{:S(2)}, u32[]{:S(2)}) collective-permute-start(bf16[2,4,64,768]{3,2,1,0:T(8,128)(2,1)S(1)} %dynamic-slice_bitcast_fusion), channel_id=1, source_target_pairs={{0,16},{16,0},{1,17},{17,1},{2,18},{18,2},{3,19},{19,3},{4,20},{20... | collective-permute-start | bytes 2359304 | tf_op jit(solution)/shard_map/ppermute | solution.py:121
  645.7 88.5 %collective-permute-start.19 = (bf16[2,256,768]{2,1,0:T(8,128)(2,1)S(1)}, bf16[2,256,768]{2,1,0:T(8,128)(2,1)S(1)}, u32[]{:S(2)}, u32[]{:S(2)}) collective-permute-start(bf16[2,256,768]{2,1,0:T(8,128)(2,1)S(1)} %pad_maximum_fusion.51), channel_id=1, source_target_pairs={{0,4},{4,0},{8,12},{12,8},{1,5},{5,1},{9,13},{13,9},{2,6},{6,2},{1... | collective-permute-start | bytes 2359304 | tf_op jit(solution)/shard_map/ppermute | solution.py:100
  685.5 51.2 %collective-permute-start.28 = (bf16[2,256,768]{2,1,0:T(8,128)(2,1)S(1)}, bf16[2,256,768]{2,1,0:T(8,128)(2,1)S(1)}, u32[]{:S(2)}, u32[]{:S(2)}) collective-permute-start(bf16[2,256,768]{2,1,0:T(8,128)(2,1)S(1)} %pad_maximum_fusion.53), channel_id=1, source_target_pairs={{0,4},{4,0},{8,12},{12,8},{1,5},{5,1},{9,13},{13,9},{2,6},{6,2},{1... | collective-permute-start | bytes 2359304 | tf_op jit(solution)/shard_map/ppermute | solution.py:100
  685.8 53.6 %collective-permute-start.66 = (bf16[4,64,768]{2,1,0:T(8,128)(2,1)S(1)}, bf16[4,64,768]{2,1,0:T(8,128)(2,1)S(1)}, u32[]{:S(2)}, u32[]{:S(2)}) collective-permute-start(bf16[4,64,768]{2,1,0:T(8,128)(2,1)S(1)} %dynamic-slice_bitcast_fusion.6), channel_id=1, source_target_pairs={{0,8},{4,12},{8,0},{12,4},{1,9},{5,13},{9,1},{13,5},{2,10},{6,14},... | collective-permute-start | bytes 1179656 | tf_op jit(solution)/shard_map/ppermute | solution.py:209
  811.5 84.4 %collective-permute-start.48 = (bf16[4,4,24,1600]{3,2,1,0:T(8,128)(2,1)}, bf16[4,4,24,1600]{3,2,1,0:T(8,128)(2,1)}, u32[]{:S(2)}, u32[]{:S(2)}) collective-permute-start(bf16[4,4,24,1600]{3,2,1,0:T(8,128)(2,1)} %bitcast.693), channel_id=1, source_target_pairs={{0,16},{16,0},{1,17},{17,1},{2,18},{18,2},{3,19},{19,3},{4,20},{20... | collective-permute-start | bytes 3686408 | tf_op jit(solution)/shard_map/ppermute | solution.py:121
  821.3 77.7 %all-to-all-start.9 = ((bf16[4,48,2,2,512]{4,1,3,2,0:T(8,128)(2,1)}), bf16[4,48,2,2,512]{4,1,3,2,0:T(8,128)(2,1)}, u32[]{:S(2)}, u32[]{:S(2)}) async-start(bf16[4,48,2,2,512]{4,1,3,2,0:T(8,128)(2,1)} %pad_maximum_fusion.61), calls=%async_computation.13 | async-start | bytes 1572864 | tf_op jit(solution)/shard_map/all_to_all | solution.py:203
  825.5 69.0 %reduce-scatter.11.cloned.1.call-start = ((), (), s32[]{:S(2)}) async-start(), calls=%async_computation.19 | async-start | bytes 675840 | tf_op jit(solution)/shard_map/reduce_scatter | solution.py:181
  855.8 184.0 %reduce-scatter.7.cloned.1.call-start = ((), (), s32[]{:S(2)}) async-start(), calls=%async_computation.17 | async-start | bytes 1597440 | tf_op jit(solution)/shard_map/reduce_scatter | solution.py:174
  899.0 49.4 %collective-permute-start.61 = (bf16[4,48,2,2,512]{4,1,3,2,0:T(8,128)(2,1)}, bf16[4,48,2,2,512]{4,1,3,2,0:T(8,128)(2,1)}, u32[]{:S(2)}, u32[]{:S(2)}) collective-permute-start(bf16[4,48,2,2,512]{4,1,3,2,0:T(8,128)(2,1)} %all-to-all-done.9), channel_id=1, source_target_pairs={{0,16},{16,0},{1,17},{17,1},{2,18},{18,2},{3,19},{19,3},{4,20},{20... | collective-permute-start | bytes 2359304 | tf_op jit(solution)/shard_map/ppermute | solution.py:127
  904.6 61.7 %collective-permute-start.37 = (bf16[2,256,768]{2,1,0:T(8,128)(2,1)}, bf16[2,256,768]{2,1,0:T(8,128)(2,1)}, u32[]{:S(2)}, u32[]{:S(2)}) collective-permute-start(bf16[2,256,768]{2,1,0:T(8,128)(2,1)} %pad_maximum_fusion.56), channel_id=1, source_target_pairs={{0,4},{4,0},{8,12},{12,8},{1,5},{5,1},{9,13},{13,9},{2,6},{6,2},{1... | collective-permute-start | bytes 2359304 | tf_op jit(solution)/shard_map/ppermute | solution.py:93
  920.3 96.8 %collective-permute-start.41 = (bf16[576,768]{1,0:T(8,128)(2,1)}, bf16[576,768]{1,0:T(8,128)(2,1)}, u32[]{:S(2)}, u32[]{:S(2)}) collective-permute-start(bf16[576,768]{1,0:T(8,128)(2,1)} %slice.1210), channel_id=1, source_target_pairs={{0,4},{4,0},{8,12},{12,8},{1,5},{5,1},{9,13},{13,9},{2,6},{6,2},{1... | collective-permute-start | bytes 2654216 | tf_op jit(solution)/shard_map/ppermute | solution.py:352
  960.5 99.3 %collective-permute-start.54 = (bf16[2,2,4,48,2,512]{5,3,4,2,1,0:T(8,128)(2,1)}, bf16[2,2,4,48,2,512]{5,3,4,2,1,0:T(8,128)(2,1)}, u32[]{:S(2)}, u32[]{:S(2)}) collective-permute-start(bf16[2,2,4,48,2,512]{5,3,4,2,1,0:T(8,128)(2,1)} %bitcast.692), channel_id=1, source_target_pairs={{0,16},{16,0},{1,17},{17,1},{2,18},{18,2},{3,19},{19,3},{4,20},{20... | collective-permute-start | bytes 4718600 | tf_op jit(solution)/shard_map/ppermute | solution.py:121
  965.7 48.2 %collective-permute-start.62 = (bf16[2,4,64,768]{3,2,1,0:T(8,128)(2,1)S(1)}, bf16[2,4,64,768]{3,2,1,0:T(8,128)(2,1)S(1)}, u32[]{:S(2)}, u32[]{:S(2)}) collective-permute-start(bf16[2,4,64,768]{3,2,1,0:T(8,128)(2,1)S(1)} %dynamic-slice_bitcast_fusion.1), channel_id=1, source_target_pairs={{0,16},{16,0},{1,17},{17,1},{2,18},{18,2},{3,19},{19,3},{4,20},{20... | collective-permute-start | bytes 2359304 | tf_op jit(solution)/shard_map/ppermute | solution.py:121
  1054.8 166.4 %reduce-scatter.9.cloned.1.call-start = ((), (), s32[]{:S(2)}) async-start(), calls=%async_computation.18 | async-start | bytes 675840 | tf_op jit(solution)/shard_map/reduce_scatter | solution.py:181
  1114.1 48.1 %collective-permute-start.46 = (bf16[4,4,24,1600]{3,2,1,0:T(8,128)(2,1)}, bf16[4,4,24,1600]{3,2,1,0:T(8,128)(2,1)}, u32[]{:S(2)}, u32[]{:S(2)}) collective-permute-start(bf16[4,4,24,1600]{3,2,1,0:T(8,128)(2,1)} %bitcast.694), channel_id=1, source_target_pairs={{0,16},{16,0},{1,17},{17,1},{2,18},{18,2},{3,19},{19,3},{4,20},{20... | collective-permute-start | bytes 3686408 | tf_op jit(solution)/shard_map/ppermute | solution.py:121
  1155.6 75.1 %reduce-scatter.5.cloned.1.call-start = ((), (), s32[]{:S(2)}) async-start(), calls=%async_computation.16 | async-start | bytes 1597440 | tf_op jit(solution)/shard_map/reduce_scatter | solution.py:174
  1167.0 57.6 %all-to-all-start.8 = ((bf16[4,48,2,2,512]{4,1,3,2,0:T(8,128)(2,1)}), bf16[4,48,2,2,512]{4,1,3,2,0:T(8,128)(2,1)}, u32[]{:S(2)}, u32[]{:S(2)}) async-start(bf16[4,48,2,2,512]{4,1,3,2,0:T(8,128)(2,1)} %pad_maximum_fusion.60), calls=%async_computation.12 | async-start | bytes 1572864 | tf_op jit(solution)/shard_map/all_to_all | solution.py:203
  (270 other events, 4056.9 us)
Sparse Core Ops, SparseCore 0:
  11.4 31.0 all-gather.10
  44.1 87.5 all-gather.8
  172.9 51.7 all-gather.14
  312.7 53.2 all-gather.12
  855.9 31.2 reduce-scatter.10
  899.1 26.5 reduce-scatter.6
  1155.7 20.2 reduce-scatter.8
  1179.0 32.7 reduce-scatter.4

commit v2 on v1

--- a/solution.py
+++ b/solution.py
@@ -88,15 +88,15 @@
     )(x)
 
 
-def gather_seq(x):
+def gather_seq(x, s):
     far = lax.ppermute(x, "seq", FAR)
     both = lax.ppermute(jnp.stack([x, far]), "seq", SIB)
-    return jnp.concatenate([x, both[0], far, both[1]], 0)
-
-
-def scatter_seq(partial):
-    blocks = partial.astype(bf16).reshape(4, -1, partial.shape[-1])
-    kept = partial.reshape(4, -1, partial.shape[-1])
+    return absolute(jnp.stack([x, both[0], far, both[1]]), s).reshape(-1, x.shape[-1])
+
+
+def scatter_seq(partial, s):
+    kept = absolute(partial.reshape(4, -1, partial.shape[-1]), s)
+    blocks = kept.astype(bf16)
     near = lax.ppermute(jnp.stack([blocks[1], blocks[3]]), "seq", SIB).astype(f32)
     away = (kept[2] + near[1]).astype(bf16)
     return kept[0] + near[0] + lax.ppermute(away, "seq", FAR).astype(f32)
@@ -130,41 +130,6 @@
 
 def absolute(blocks, s):
     return jnp.stack([lax.dynamic_index_in_dim(blocks, s ^ i, 0, False) for i in range(4)])
-
-
-def fetch_dense(qkv, out, first, second):
-    columns = jnp.concatenate(
-        [
-            qkv.reshape(48, 3, 4, COLS).transpose(2, 0, 1, 3).reshape(4, 48, 3 * COLS),
-            first.reshape(48, 2, 4, FF_DEV).transpose(2, 0, 1, 3).reshape(4, 48, 2 * FF_DEV),
-        ],
-        2,
-    )
-    columns = lax.all_to_all(columns, "seq", split_axis=0, concat_axis=0, tiled=True)
-    columns = lax.all_gather(columns, "fsdp", axis=1).reshape(D, -1)
-    rows = lax.all_gather(jnp.concatenate([out, second], 0), "fsdp", axis=0)
-    return (
-        columns[:, : 3 * COLS],
-        columns[:, 3 * COLS :],
-        rows[:, :48].reshape(COLS, D),
-        rows[:, 48:].reshape(FF_DEV, D),
-    )
-
-
-def fetch_expert(first, second, s):
-    core = lax.rem(s, 2)
-    far = s // 2
-    first = lax.all_to_all(first, "fsdp", split_axis=0, concat_axis=0, tiled=True)
-    first = first.reshape(4, 48, 2, 2, 2, FF_DEV)
-    own = lax.dynamic_index_in_dim(first, core, 4, False).reshape(4, 48, 2 * FF_CORE)
-    sent = lax.dynamic_index_in_dim(first, 1 - core, 4, False).reshape(4, 48, 2 * FF_CORE)
-    pair = jnp.stack([own, lax.ppermute(sent, "seq", SIB)])
-    pair = jnp.concatenate([pair, lax.ppermute(pair, "seq", FAR)], 0)
-    first = absolute(pair, s).reshape(D, 2 * FF_CORE)
-    second = lax.all_to_all(second, "fsdp", split_axis=0, concat_axis=0, tiled=True)
-    other = lax.ppermute(second, "seq", FAR)
-    second = jnp.stack([jnp.where(far == 0, second, other), jnp.where(far == 0, other, second)])
-    return first, second.reshape(FF_CORE, D)
 
 
 def return_dense(d_columns, d_rows, s, z, r, reps):
@@ -263,15 +228,6 @@
     return jnp.concatenate([a * cosine - b * sine, b * cosine + a * sine], -1)
 
 
-def attention(queries, keys, values, visible):
-    scores = jnp.einsum("qhd,khd->hqk", queries, keys, preferred_element_type=f32)
-    scores = jnp.where(visible[None], scores * HEAD_DIM**-0.5, MASKED)
-    top = jnp.max(scores, -1, keepdims=True)
-    total = top + jnp.log(jnp.sum(jnp.exp(scores - top), -1, keepdims=True))
-    weights = jnp.exp(scores - total).astype(bf16)
-    return jnp.einsum("hqk,khd->qhd", weights, values, preferred_element_type=f32), total
-
-
 def attention_back(queries, keys, values, visible, total, attended, d_attended):
     scale = HEAD_DIM**-0.5
     scores = jnp.einsum("qhd,khd->hqk", queries, keys, preferred_element_type=f32)
@@ -286,51 +242,536 @@
     return d_q, d_k, d_v
 
 
-def layer_forward(layer, h, dense, expert, gains, router, choices, routes, cosine, sine, visible):
-    w_qkv, w_first, w_out, w_second = dense
-    e_first, e_second = expert
-    kept, chosen = routes
+class Net:
+    def __init__(self, send, recv, local_sems):
+        self.send, self.recv, self.local_sems = send, recv, local_sems
+        self.count = 0
+        self.local_count = 0
+        self.r, self.s, self.z = (lax.axis_index(a) for a in ("rep", "seq", "fsdp"))
+        self.half = lax.rem(self.r, 2)
+        self.core = lax.rem(self.s, 2)
+        self.far = self.s // 2
+        self.partner = self.r + 1 - 2 * self.half
+
+    def seq(self, d):
+        core = self.core if d % 2 == 0 else 1 - self.core
+        far = self.far if d < 2 else 1 - self.far
+        return far * 2 + core
+
+    def plane(self, k):
+        return lax.rem(self.z + k, FSDP)
+
+    def copy(self, src, dst, **device):
+        k = self.count
+        self.count += 1
+        out = pltpu.make_async_remote_copy(
+            src_ref=src, dst_ref=dst, send_sem=self.send.at[k], recv_sem=self.recv.at[k],
+            device_id=device, device_id_type=MESH,
+        )
+        out.start()
+        return out
+
+    def move(self, src, dst):
+        k = self.local_count
+        self.local_count += 1
+        out = pltpu.make_async_copy(src, dst, self.local_sems.at[k])
+        out.start()
+        return out
+
+    def greet(self, devices):
+        self.barrier = pltpu.get_barrier_semaphore()
+        for device in devices:
+            pl.semaphore_signal(self.barrier, inc=1, device_id=device, device_id_type=MESH)
+        self.greeted = len(devices)
+
+    def met(self):
+        pl.semaphore_wait(self.barrier, self.greeted)
+
+    def everyone(self):
+        seqs = [{"seq": self.seq(d)} for d in (1, 2, 3)]
+        planes = [{"fsdp": self.plane(k)} for k in (1, 2, 3)]
+        both = [{"seq": self.seq(1), "fsdp": self.plane(k)} for k in (1, 2, 3)]
+        return seqs + planes + both + [{"rep": self.partner}]
+
+
+def columns(start, size):
+    return pl.ds(pl.multiple_of(start, 128), size)
+
+
+class ExpertJob:
+    inputs = ("expert_in", "expert_out")
+    shapes = ((2, 2, 4, 4, 48, FF_DEV), (2, 4, 128, D))
+
+    def __init__(self, net, layer, ins, outs):
+        self.net, self.layer = net, layer
+        self.first, self.second = ins
+        self.w1, self.w2 = outs
+
+    def stages(self):
+        return [self.begin, self.second_hop, self.third_hop, self.finish]
+
+    def begin(self):
+        n = self.net
+        self.first_copies, self.second_copies = [], []
+        for k in (2, 1, 3, 0):
+            e = n.plane(k)
+            for d in (0, 1):
+                core = n.core if d == 0 else 1 - n.core
+                for gu in (0, 1):
+                    src = self.first.at[
+                        self.layer, e, :, columns(gu * FF + n.half * FF_CORE + core * FF_DEV, FF_DEV)
+                    ]
+                    dst = self.w1.at[n.half, gu, n.s, n.z]
+                    if k == 0 and d == 0:
+                        self.first_copies.append(n.move(src, dst))
+                    else:
+                        self.first_copies.append(n.copy(src, dst, seq=n.seq(d), fsdp=e))
+            src = self.second.at[self.layer, e, :, columns(n.half * 384, 384)]
+            dst = self.w2.at[n.far, n.z, :, columns(n.half * 384, 384)]
+            if k == 0:
+                self.second_copies.append(n.move(src, dst))
+            else:
+                self.second_copies.append(n.copy(src, dst, fsdp=e))
+
+    def second_hop(self):
+        n = self.net
+        for copy in self.first_copies:
+            copy.wait()
+        part = self.w1.at[n.half, :, pl.ds(2 * n.far, 2)]
+        self.first_copies = [n.copy(part, part, seq=n.seq(2))]
+        for copy in self.second_copies:
+            copy.wait()
+        part = self.w2.at[n.far, :, :, columns(n.half * 384, 384)]
+        self.second_copies = [n.copy(part, part, rep=n.partner)]
+
+    def third_hop(self):
+        n = self.net
+        for copy in self.first_copies + self.second_copies:
+            copy.wait()
+        self.first_copies = [n.copy(self.w1.at[n.half], self.w1.at[n.half], rep=n.partner)]
+        self.second_copies = [n.copy(self.w2.at[n.far], self.w2.at[n.far], seq=n.seq(2))]
+
+    def finish(self):
+        for copy in self.first_copies + self.second_copies:
+            copy.wait()
+
+
+class SharedJob:
+    inputs = ("shared_in", "shared_out")
+    shapes = ((2, 4, 4, 48, FF_DEV), (4, 128, D))
+
+    def __init__(self, net, layer, ins, outs):
+        self.net, self.layer = net, layer
+        self.first, self.second = ins
+        self.w_in, self.w_out = outs
+
+    def stages(self):
+        return [self.begin, self.second_hop, self.third_hop, self.finish]
+
+    def begin(self):
+        n = self.net
+        self.first_copies, self.second_copies = [], []
+        for d in (3, 2, 1, 0):
+            src = self.first.at[
+                self.layer, :, columns(n.half * FF + n.seq(d) * FF_DEV, FF_DEV)
+            ]
+            dst = self.w_in.at[n.half, n.s, n.z]
+            if d == 0:
+                self.first_copies.append(n.move(src, dst))
+            else:
+                self.first_copies.append(n.copy(src, dst, seq=n.seq(d)))
+        for k in (2, 1, 3, 0):
+            src = self.second.at[self.layer, :, columns(n.half * 384, 384)]
+            dst = self.w_out.at[n.z, :, columns(n.half * 384, 384)]
+            if k == 0:
+                self.second_copies.append(n.move(src, dst))
+            else:
+                self.second_copies.append(n.copy(src, dst, fsdp=n.plane(k)))
+
+    def second_hop(self):
+        n = self.net
+        for copy in self.first_copies:
+            copy.wait()
+        part = self.w_in.at[n.half, :, n.z]
+        self.first_copies = [n.copy(part, part, fsdp=n.plane(k)) for k in (2, 1, 3)]
+        for copy in self.second_copies:
+            copy.wait()
+        part = self.w_out.at[:, :, columns(n.half * 384, 384)]
+        self.second_copies = [n.copy(part, part, rep=n.partner)]
+
+    def third_hop(self):
+        n = self.net
+        for copy in self.first_copies:
+            copy.wait()
+        self.first_copies = [n.copy(self.w_in.at[n.half], self.w_in.at[n.half], rep=n.partner)]
+
+    def finish(self):
+        for copy in self.first_copies + self.second_copies:
+            copy.wait()
+
+
+class AttnJob:
+    inputs = ("attn_qkv", "attn_out")
+    shapes = ((4, 4, 48, 3 * COLS), (4, 48, D))
+
+    def __init__(self, net, layer, ins, outs):
+        self.net, self.layer = net, layer
+        self.qkv, self.out = ins
+        self.w_qkv, self.w_out = outs
+
+    def stages(self):
+        return [self.begin, self.second_hop, self.finish]
+
+    def begin(self):
+        n = self.net
+        self.copies, self.rest = [], []
+        for d in (3, 2, 1):
+            self.copies.append(
+                n.copy(self.qkv.at[self.layer, n.seq(d)], self.w_qkv.at[n.s, n.z], seq=n.seq(d))
+            )
+        self.copies.append(n.move(self.qkv.at[self.layer, n.s], self.w_qkv.at[n.s, n.z]))
+        for k in (2, 1, 3):
+            self.rest.append(n.copy(self.out.at[self.layer], self.w_out.at[n.z], fsdp=n.plane(k)))
+        self.rest.append(n.move(self.out.at[self.layer], self.w_out.at[n.z]))
+
+    def second_hop(self):
+        n = self.net
+        for copy in self.copies:
+            copy.wait()
+        part = self.w_qkv.at[:, n.z]
+        self.copies = [n.copy(part, part, fsdp=n.plane(k)) for k in (2, 1, 3)]
+
+    def finish(self):
+        for copy in self.copies + self.rest:
+            copy.wait()
+
+
+class SmallJob:
+    inputs = ("small",)
+    shapes = ((4, 4, 16, 128),)
+
+    def __init__(self, net, layer, ins, outs):
+        self.net = net
+        (self.src,) = ins
+        (self.dst,) = outs
+
+    def stages(self):
+        return [self.begin, self.second_hop, self.finish]
+
+    def begin(self):
+        n = self.net
+        self.copies = [
+            n.copy(self.src, self.dst.at[n.s, n.z], seq=n.seq(d)) for d in (3, 2, 1)
+        ] + [n.move(self.src, self.dst.at[n.s, n.z])]
+
+    def second_hop(self):
+        n = self.net
+        for copy in self.copies:
+            copy.wait()
+        part = self.dst.at[:, n.z]
+        self.copies = [n.copy(part, part, fsdp=n.plane(k)) for k in (2, 1, 3)]
+
+    def finish(self):
+        for copy in self.copies:
+            copy.wait()
+
+
+class Background:
+    def __init__(self, net, jobs, refs):
+        ins = sum(len(j.inputs) for j, _ in jobs)
+        given, results = refs[:ins], refs[ins:]
+        self.queues = []
+        for job, layer in jobs:
+            a, b = len(job.inputs), len(job.shapes)
+            made = job(net, layer, given[:a], results[:b])
+            self.queues.append(made.stages())
+            given, results = given[a:], results[b:]
+
+    def step(self):
+        for queue in self.queues:
+            if queue:
+                queue.pop(0)()
+
+    def drain(self):
+        while any(self.queues):
+            self.step()
+
+
+def job_inputs(jobs, shards):
+    return [shards[name] for job, _ in jobs for name in job.inputs]
+
+
+def job_outputs(jobs):
+    return [jax.ShapeDtypeStruct(shape, bf16) for job, _ in jobs for shape in job.shapes]
+
+
+COPIES = 80
+
+
+def call(kernel, inputs, outputs, scratch, jobs, shards, cid, flops=0):
+    given = job_inputs(jobs, shards)
+    results = job_outputs(jobs)
+    vmem, anywhere = pl.BlockSpec(memory_space=pltpu.VMEM), pl.BlockSpec(memory_space=pl.ANY)
+
+    def body(*refs):
+        a = len(inputs)
+        b = a + len(given)
+        c = b + len(outputs)
+        d = c + len(results)
+        e = d + len(scratch)
+        net = Net(*refs[e:])
+        ground = Background(net, jobs, refs[a:b] + refs[c:d])
+        kernel(net, ground, *refs[:a], *refs[b:c], *refs[d:e])
+
+    made = pl.pallas_call(
+        body,
+        out_shape=[jax.ShapeDtypeStruct(shape, kind) for shape, kind in outputs] + results,
+        in_specs=[vmem] * len(inputs) + [anywhere] * len(given),
+        out_specs=[vmem] * len(outputs) + [anywhere] * len(results),
+        scratch_shapes=[pltpu.VMEM(shape, kind) for shape, kind in scratch]
+        + [
+            pltpu.SemaphoreType.DMA((COPIES,)),
+            pltpu.SemaphoreType.DMA((COPIES,)),
+            pltpu.SemaphoreType.DMA((16,)),
+        ],
+        compiler_params=pltpu.CompilerParams(
+            collective_id=cid, has_side_effects=True, vmem_limit_bytes=56 << 20
+        ),
+        cost_estimate=pl.CostEstimate(flops=flops, bytes_accessed=1 << 20, transcendentals=0),
+    )(*inputs, *given)
+    return made[: len(outputs)], made[len(outputs) :]
+
+
+def prologue_kernel(net, ground):
+    net.greet(net.everyone())
+    net.met()
+    ground.drain()
+
+
+def rms_rows(x):
+    return lax.rsqrt(jnp.mean(x * x, -1, keepdims=True) + EPS)
+
+
+def turn(x, cosine, sine):
+    half = HEAD_DIM // 2
+    return x * cosine + jnp.concatenate([x[:, half:], x[:, :half]], 1) * sine
+
+
+def attn_forward_kernel(
+    net, ground, h, gains, w_qkv, w_out, cosine, sine,
+    middle, second, every, queries, keys, values, attended, totals,
+    near_out, near_in, away_out, away_in,
+):
+    net.greet(net.everyone())
+    x = h[...]
+    every[net.s] = (x * rms_rows(x) * gains[0:1, :]).astype(bf16)
+    net.met()
+    far = net.copy(every.at[net.s], every.at[net.s], seq=net.seq(2))
+    near = net.copy(every.at[net.s], every.at[net.s], seq=net.seq(1))
+    ground.step()
+
+    def project(b):
+        joint = dot(every[b], w_qkv[...])
+        c, sn = cosine[b], sine[b]
+        for i in range(HEADS_DEV):
+            at = i * HEAD_DIM
+            queries[i, b] = turn(joint[:, at : at + HEAD_DIM], c, sn).astype(bf16)
+            at += COLS
+            keys[i, b] = turn(joint[:, at : at + HEAD_DIM], c, sn).astype(bf16)
+            at += COLS
+            values[i, b] = joint[:, at : at + HEAD_DIM].astype(bf16)
+
+    project(net.s)
+    near.wait_recv()
+    project(net.seq(1))
+    far.wait_recv()
+    passed = net.copy(every.at[net.seq(2)], every.at[net.seq(2)], seq=net.seq(1))
+    project(net.seq(2))
+    passed.wait_recv()
+    project(net.seq(3))
+    ground.step()
     tokens = h.shape[0]
-    normed, factor_one = rms_forward(h, gains[0])
-    normed_all = gather_seq(normed.astype(bf16))
-    joint = dot(normed_all, w_qkv).reshape(-1, 3, HEADS_DEV, HEAD_DIM)
-    queries = rotate(joint[:, 0], cosine, sine).astype(bf16)
-    keys = rotate(joint[:, 1], cosine, sine).astype(bf16)
-    values = joint[:, 2].astype(bf16)
-    attended, total = attention(queries, keys, values, visible)
-    attended_low = attended.reshape(-1, COLS).astype(bf16)
-    middle = h + scatter_seq(dot(attended_low, w_out))
-    normed, factor_two = rms_forward(middle, gains[1])
-    second = normed.astype(bf16)
-    logits = dot(second, router)
-    onehot = (choices[..., None] == jnp.arange(EXPERTS, dtype=jnp.int32)).astype(f32)
-    gates = jax.nn.softmax(jnp.sum(onehot * logits[:, None, :], -1), -1)
-    second_all = gather_seq(second)
-    joint_shared = dot(second_all, w_first)
-    hidden_shared = swiglu(joint_shared)
-    shared_part = dot(hidden_shared, w_second)
-    picked = chosen[:, :tokens] + chosen[:, tokens:]
-    rows = dot(picked, second).astype(bf16).reshape(EXPERTS, CAP, D)
-    rows = exchange(rows, 1 + 4 * layer).reshape(SLOTS, D)
-    rows_all = jnp.concatenate([rows, lax.ppermute(rows, "seq", SIB)], 0)
-    joint_expert = dot(rows_all, e_first)
-    hidden_expert = swiglu(joint_expert)
-    produced = dot(hidden_expert, e_second)
-    got = lax.ppermute(produced[SLOTS:].astype(bf16), "seq", SIB)
-    produced = (produced[:SLOTS] + got.astype(f32)).astype(bf16)
-    yields = exchange(produced.reshape(EXPERTS, CAP, D), 2 + 4 * layer).reshape(SLOTS, D)
-    gathered = dot_tn(chosen, yields)
-    mixture = gates[:, :1] * gathered[:tokens] + gates[:, 1:] * gathered[tokens:]
-    result = middle + scatter_seq(shared_part) + mixture
-    stored = (
-        h, factor_one, normed_all, queries, keys, values, total, attended, attended_low, middle,
-        factor_two, second, gates, onehot, second_all, joint_shared, hidden_shared, rows_all,
-        joint_expert, hidden_expert, gathered,
+
+    def head(i, carry):
+        for b in range(SEQ):
+            size = (b + 1) * tokens
+            scores = dot_nt(queries[i, b], keys[i, : b + 1].reshape(size, HEAD_DIM))
+            row = lax.broadcasted_iota(jnp.int32, (tokens, size), 0) + b * tokens
+            col = lax.broadcasted_iota(jnp.int32, (tokens, size), 1)
+            scores = jnp.where(row >= col, scores * HEAD_DIM**-0.5, MASKED)
+            top = jnp.max(scores, -1, keepdims=True)
+            weights = jnp.exp(scores - top)
+            total = jnp.sum(weights, -1, keepdims=True)
+            weights = (weights * (1.0 / total)).astype(bf16)
+            attended[i, b] = dot(weights, values[i, : b + 1].reshape(size, HEAD_DIM))
+            totals[i, b] = jnp.broadcast_to(top + jnp.log(total), (tokens, 128))
+        return carry
+
+    lax.fori_loop(0, HEADS_DEV, head, 0)
+    ground.step()
+
+    def part(b):
+        low = jnp.concatenate([attended[i, b].astype(bf16) for i in range(HEADS_DEV)], 1)
+        return dot(low, w_out[...])
+
+    near_out[0] = part(net.seq(1)).astype(bf16)
+    near_out[1] = part(net.seq(3)).astype(bf16)
+    near_sum = net.copy(near_out, near_in, seq=net.seq(1))
+    away = part(net.seq(2))
+    own = part(net.s)
+    near_sum.wait_recv()
+    away_out[...] = (away + near_in[1].astype(f32)).astype(bf16)
+    away_sum = net.copy(away_out, away_in, seq=net.seq(2))
+    own = h[...] + own + near_in[0].astype(f32)
+    ground.step()
+    away_sum.wait_recv()
+    own = own + away_in[...].astype(f32)
+    middle[...] = own
+    second[...] = (own * rms_rows(own) * gains[1:2, :]).astype(bf16)
+    for copy in (far, near, passed, near_sum, away_sum):
+        copy.wait_send()
+    ground.drain()
+
+
+def attn_forward(h, gains, w_qkv, w_out, cosine, sine, jobs, shards, cid):
+    t = h.shape[0]
+    head = (HEADS_DEV, SEQ, t, HEAD_DIM)
+    return call(
+        attn_forward_kernel,
+        [h, gains, w_qkv, w_out, cosine, sine],
+        [
+            ((t, D), f32), ((t, D), bf16), ((SEQ, t, D), bf16), (head, bf16), (head, bf16),
+            (head, bf16), (head, f32), ((HEADS_DEV, SEQ, t, 128), f32),
+        ],
+        [((2, t, D), bf16), ((2, t, D), bf16), ((t, D), bf16), ((t, D), bf16)],
+        jobs, shards, cid,
     )
-    return result, stored
-
-
-def layer_backward(layer, grad, dense, expert, gains, router, routes, stored, cosine, sine, visible):
+
+
+def silu_gate(g, u):
+    return g / (1.0 + jnp.exp(-g)) * u
+
+
+def ffn_forward_kernel(
+    net, ground, second, middle, router, onehot, chosen, w_in, w_so, w1, w2,
+    result, gates, gathered, every, joint, hidden, rows, joint_e, hidden_e,
+    rows_out, prod_out, prod_in, prod_own, back_out, yields, near_out, near_in, away_out, away_in,
+):
+    t = second.shape[0]
+    net.greet(net.everyone())
+    picked = chosen[:, :t] + chosen[:, t:]
+    rows_out[...] = dot(picked, second[...]).astype(bf16).reshape(EXPERTS, CAP, D)
+    every[net.s] = second[...]
+    net.met()
+    sent = {}
+    for k in (2, 1, 3):
+        e = net.plane(k)
+        sent[k] = net.copy(rows_out.at[e], rows.at[net.core, net.z], fsdp=e)
+    far = net.copy(every.at[net.s], every.at[net.s], seq=net.seq(2))
+    near = net.copy(every.at[net.s], every.at[net.s], seq=net.seq(1))
+    rows[net.core, net.z] = rows_out[net.z]
+    passed = []
+
+    def pass_rows(k):
+        if k:
+            sent[k].wait_recv()
+        part = rows.at[net.core, net.plane(FSDP - k)]
+        passed.append(net.copy(part, part, seq=net.seq(1)))
+
+    pass_rows(0)
+    ground.step()
+    logits = dot(second[...], router[...])
+    l0 = jnp.sum(onehot[0] * logits, -1, keepdims=True)
+    l1 = jnp.sum(onehot[1] * logits, -1, keepdims=True)
+    top = jnp.maximum(l0, l1)
+    e0, e1 = jnp.exp(l0 - top), jnp.exp(l1 - top)
+    g0, g1 = e0 / (e0 + e1), e1 / (e0 + e1)
+    lane = lax.broadcasted_iota(jnp.int32, (t, 128), 1)
+    gates[...] = jnp.where(lane == 0, g0, jnp.where(lane == 1, g1, 0.0))
+
+    def shared(b):
+        g, u = dot(every[b], w_in[0]), dot(every[b], w_in[1])
+        joint[0, b] = g.astype(bf16)
+        joint[1, b] = u.astype(bf16)
+        low = silu_gate(g, u).astype(bf16)
+        hidden[b] = low
+        return dot(low, w_so[...])
+
+    own_part = shared(net.s)
+    near.wait_recv()
+    near_out[0] = shared(net.seq(1)).astype(bf16)
+    pass_rows(1)
+    pass_rows(3)
+    far.wait_recv()
+    passed_far = net.copy(every.at[net.seq(2)], every.at[net.seq(2)], seq=net.seq(1))
+    far_part = shared(net.seq(2))
+    pass_rows(2)
+    passed_far.wait_recv()
+    near_out[1] = shared(net.seq(3)).astype(bf16)
+    near_sum = net.copy(near_out, near_in, seq=net.seq(1))
+    ground.step()
+
+    def expert(core):
+        x = rows[core].reshape(SLOTS, D)
+        total = None
+        for half in (0, 1):
+            g, u = dot(x, w1[half, 0]), dot(x, w1[half, 1])
+            joint_e[core, half, 0] = g.astype(bf16)
+            joint_e[core, half, 1] = u.astype(bf16)
+            low = silu_gate(g, u).astype(bf16)
+            hidden_e[core, half] = low
+            new = dot(low, w2[half * FF_DEV : (half + 1) * FF_DEV, :])
+            total = new if total is None else total + new
+        return total
+
+    for copy in passed:
+        copy.wait_recv()
+    prod_out[...] = expert(1 - net.core).astype(bf16)
+    prod_sum = net.copy(prod_out, prod_in, seq=net.seq(1))
+    near_sum.wait_recv()
+    away_out[...] = (far_part + near_in[1].astype(f32)).astype(bf16)
+    away_sum = net.copy(away_out, away_in, seq=net.seq(2))
+    prod_own[...] = expert(net.core)
+    prod_sum.wait_recv()
+    back_out[...] = (prod_own[...] + prod_in[...].astype(f32)).astype(bf16).reshape(EXPERTS, CAP, D)
+    returned = []
+    for k in (2, 1, 3):
+        e = net.plane(k)
+        returned.append(net.copy(back_out.at[e], yields.at[net.z], fsdp=e))
+    yields[net.z] = back_out[net.z]
+    ground.step()
+    away_sum.wait_recv()
+    base = middle[...] + own_part + near_in[0].astype(f32) + away_in[...].astype(f32)
+    for copy in returned:
+        copy.wait_recv()
+    got = dot_tn(chosen[...], yields[...].reshape(SLOTS, D))
+    gathered[...] = got.astype(bf16)
+    result[...] = base + g0 * got[:t] + g1 * got[t:]
+    for copy in [far, near, passed_far, near_sum, prod_sum, away_sum, *passed, *sent.values(), *returned]:
+        copy.wait_send()
+    ground.drain()
+
+
+def ffn_forward(second, middle, router, onehot, chosen, w_in, w_so, w1, w2, jobs, shards, cid):
+    t = second.shape[0]
+    return call(
+        ffn_forward_kernel,
+        [second, middle, router, onehot, chosen, w_in, w_so, w1, w2],
+        [
+            ((t, D), f32), ((t, 128), f32), ((2 * t, D), bf16), ((SEQ, t, D), bf16),
+            ((2, SEQ, t, FF_DEV), bf16), ((SEQ, t, FF_DEV), bf16), ((2, EXPERTS, CAP, D), bf16),
+            ((2, 2, 2, SLOTS, FF_DEV), bf16), ((2, 2, SLOTS, FF_DEV), bf16),
+        ],
+        [
+            ((EXPERTS, CAP, D), bf16), ((SLOTS, D), bf16), ((SLOTS, D), bf16), ((SLOTS, D), f32),
+            ((EXPERTS, CAP, D), bf16), ((EXPERTS, CAP, D), bf16), ((2, t, D), bf16),
+            ((2, t, D), bf16), ((t, D), bf16), ((t, D), bf16),
+        ],
+        jobs, shards, cid,
+    )
+
+
+def layer_backward(layer, s, grad, dense, expert, gains, router, routes, stored, cosine, sine, visible):
     w_qkv, w_first, w_out, w_second = dense
     e_first, e_second = expert
     kept, chosen = routes
@@ -344,21 +785,27 @@
     d_yields = jnp.concatenate([grad * scaled[:, :1], grad * scaled[:, 1:]], 0).astype(bf16)
     d_yields = dot(chosen, d_yields).astype(bf16).reshape(EXPERTS, CAP, D)
     d_rows = exchange(d_yields, 3 + 4 * layer).reshape(SLOTS, D)
-    d_rows = jnp.concatenate([d_rows, lax.ppermute(d_rows, "seq", SIB)], 0)
+    other = lax.ppermute(d_rows, "seq", SIB)
+    core = lax.rem(s, 2)
+    d_rows = jnp.concatenate([jnp.where(core == 0, d_rows, other), jnp.where(core == 0, other, d_rows)], 0)
     de_second = dot_tn(hidden_expert, d_rows)
     d_joint = swiglu_back(joint_expert, dot_nt(d_rows, e_second))
     de_first = dot_tn(rows_all, d_joint)
     back = dot_nt(d_joint, e_first)
-    got = lax.ppermute(back[SLOTS:].astype(bf16), "seq", SIB)
-    back = (back[:SLOTS] + got.astype(f32)).astype(bf16)
+    back = back.reshape(2, SLOTS, D)
+    own = lax.dynamic_index_in_dim(back, core, 0, False)
+    got = lax.ppermute(
+        lax.dynamic_index_in_dim(back, 1 - core, 0, False).astype(bf16), "seq", SIB
+    )
+    back = (own + got.astype(f32)).astype(bf16)
     back = exchange(back.reshape(EXPERTS, CAP, D), 4 + 4 * layer).reshape(SLOTS, D)
     picked = chosen[:, :tokens] + chosen[:, tokens:]
 
-    grad_all = gather_seq(grad.astype(bf16))
+    grad_all = gather_seq(grad.astype(bf16), s)
     d_second_w = dot_tn(hidden_shared, grad_all)
     d_joint_shared = swiglu_back(joint_shared, dot_nt(grad_all, w_second))
     d_first_w = dot_tn(second_all, d_joint_shared)
-    d_normed = scatter_seq(dot_nt(d_joint_shared, w_first))
+    d_normed = scatter_seq(dot_nt(d_joint_shared, w_first), s)
 
     d_gates = kept * jnp.stack(
         [jnp.sum(grad * gathered[:tokens], -1), jnp.sum(grad * gathered[tokens:], -1)], -1
@@ -369,14 +816,14 @@
     d_normed = d_normed + dot_nt(d_logits, router) + dot_tn(picked, back)
     d_middle, d_gain_two = rms_backward(middle, factor_two, gains[1], d_normed)
     d_middle = grad + d_middle
-    middle_all = gather_seq(d_middle.astype(bf16))
+    middle_all = gather_seq(d_middle.astype(bf16), s)
     d_out_w = dot_tn(attended_low, middle_all)
     d_attended = dot_nt(middle_all, w_out).astype(bf16).reshape(-1, HEADS_DEV, HEAD_DIM)
     d_q, d_k, d_v = attention_back(queries, keys, values, visible, total, attended, d_attended)
     d_qkv = jnp.stack([rotate(d_q, cosine, -sine), rotate(d_k, cosine, -sine), d_v], 1)
     d_qkv = d_qkv.reshape(-1, 3 * COLS).astype(bf16)
     d_qkv_w = dot_tn(normed_all, d_qkv)
-    d_first = scatter_seq(dot_nt(d_qkv, w_qkv))
+    d_first = scatter_seq(dot_nt(d_qkv, w_qkv), s)
     d_state, d_gain_one = rms_backward(h, factor_one, gains[0], d_first)
     d_columns = jnp.concatenate([d_qkv_w, d_first_w], 1)
     d_rows_w = jnp.concatenate([d_out_w.reshape(4, 48, D), d_second_w.reshape(4, 128, D)], 1)
@@ -390,26 +837,76 @@
 ):
     r, s, z = lax.axis_index("rep"), lax.axis_index("seq"), lax.axis_index("fsdp")
     tokens = inputs.shape[1]
-    position = jnp.concatenate([(s ^ j) * tokens + jnp.arange(tokens, dtype=jnp.int32) for j in range(4)])
+    position = jnp.arange(SEQ * tokens, dtype=jnp.int32)
     half = HEAD_DIM // 2
     inverse = jnp.exp(-jnp.log(10000.0) * jnp.arange(half, dtype=f32) * 2.0 / HEAD_DIM)
     angle = position.astype(f32)[:, None] * inverse[None, :]
     cosine, sine = jnp.cos(angle)[:, None, :], jnp.sin(angle)[:, None, :]
+    table_cos = jnp.concatenate([cosine, cosine], -1).reshape(SEQ, tokens, HEAD_DIM)
+    table_sin = jnp.concatenate([-sine, sine], -1).reshape(SEQ, tokens, HEAD_DIM)
     visible = position[:, None] >= position[None, :]
-    small = jnp.concatenate([norm_gains, router.transpose(0, 2, 1)], 1)
-    small = lax.all_gather(small, ("seq", "fsdp"), axis=2, tiled=True)
+    small = jnp.concatenate([norm_gains, router.transpose(0, 2, 1)], 1).reshape(12, 48)
+    shards = {
+        "small": jnp.pad(small, ((0, 4), (0, 80))),
+        "attn_qkv": attn_qkv.reshape(LAYERS, 48, 3, SEQ, COLS)
+        .transpose(0, 3, 1, 2, 4)
+        .reshape(LAYERS, SEQ, 48, 3 * COLS),
+        "attn_out": attn_out,
+        "shared_in": shared_in,
+        "shared_out": shared_out,
+        "expert_in": expert_in,
+        "expert_out": expert_out,
+    }
+    h = inputs[0].astype(f32)
+    kept_layers = []
+    _, (small, *attn) = call(
+        prologue_kernel, [], [], [], [(SmallJob, 0), (AttnJob, 0)], shards, 11
+    )
+    small = small.reshape(16, 16, 128)[:, :12, :48].transpose(1, 0, 2).reshape(LAYERS, 6, D)
     gains = small[:, :2].astype(f32)
     routers = small[:, 2:].transpose(0, 2, 1)
-    h = inputs[0].astype(f32)
-    kept_layers = []
+    branch = None
     for layer in range(LAYERS):
-        dense = fetch_dense(attn_qkv[layer], attn_out[layer], shared_in[layer], shared_out[layer])
-        expert = fetch_expert(expert_in[layer], expert_out[layer], s)
+        first = layer == 0
         routes = routing(expert_choice[layer, 0], pair_order[layer, 0, 0])
-        h, stored = layer_forward(
-            layer, h, dense, expert, gains[layer], routers[layer], expert_choice[layer, 0], routes,
-            cosine, sine, visible,
+        onehot = expert_choice[layer, 0].T[..., None] == jnp.arange(128, dtype=jnp.int32)
+        onehot = onehot.astype(f32)
+        w_qkv, w_out = attn[0].reshape(D, 3 * COLS), attn[1].reshape(COLS, D)
+        jobs = [(ExpertJob, layer)] + ([(SharedJob, layer)] if first else [])
+        (middle, second, every_one, queries, keys, values, attended, totals), fetched = attn_forward(
+            h, gains[layer], w_qkv, w_out, table_cos, table_sin, jobs, shards, 12 + layer
         )
+        w1, w2 = fetched[0].reshape(2, 2, D, FF_DEV), fetched[1].reshape(FF_CORE, D)
+        if first:
+            branch = fetched[2:]
+        w_in, w_so = branch[0].reshape(2, D, FF_DEV), branch[1].reshape(FF_DEV, D)
+        router_pad = jnp.pad(routers[layer], ((0, 0), (0, 124)))
+        jobs = [(AttnJob, 1), (SharedJob, 1)] if first else []
+        outs, fetched = ffn_forward(
+            second, middle, router_pad, onehot, routes[1], w_in, w_so, w1, w2, jobs, shards,
+            14 + layer,
+        )
+        if first:
+            attn, branch = fetched[:2], fetched[2:]
+        result, gates, gathered, every_two, joint, hidden, rows, joint_e, hidden_e = outs
+        dense = (
+            w_qkv, jnp.concatenate([w_in[0], w_in[1]], 1), w_out, w_so,
+        )
+        expert = (
+            jnp.concatenate([w1[0, 0], w1[1, 0], w1[0, 1], w1[1, 1]], 1), w2,
+        )
+        heads = lambda x: x.reshape(HEADS_DEV, -1, HEAD_DIM).transpose(1, 0, 2)
+        stored = (
+            h, rms_rows(h), every_one.reshape(-1, D), heads(queries), heads(keys), heads(values),
+            totals[..., :1].reshape(HEADS_DEV, -1, 1), heads(attended),
+            heads(attended).reshape(-1, COLS).astype(bf16), middle, rms_rows(middle), second,
+            gates[:, :2], onehot.transpose(1, 0, 2)[..., :EXPERTS], every_two.reshape(-1, D),
+            joint.transpose(1, 2, 0, 3).reshape(-1, 2 * FF_DEV).astype(f32),
+            hidden.reshape(-1, FF_DEV), rows.reshape(-1, D),
+            joint_e.transpose(0, 3, 2, 1, 4).reshape(2 * SLOTS, -1).astype(f32),
+            hidden_e.transpose(0, 2, 1, 3).reshape(2 * SLOTS, -1), gathered.astype(f32),
+        )
+        h = result
         kept_layers.append((dense, expert, routes, stored))
     output = h.astype(bf16)[None]
     grad = cotangent[0].astype(f32)
@@ -418,7 +915,7 @@
     for layer in reversed(range(LAYERS)):
         dense, expert, routes, stored = kept_layers[layer]
         grad, d_dense, d_expert, smalls[layer] = layer_backward(
-            layer, grad, dense, expert, gains[layer], routers[layer], routes, stored, cosine, sine,
+            layer, s, grad, dense, expert, gains[layer], routers[layer], routes, stored, cosine, sine,
             visible,
         )
         grads[layer] = return_dense(*d_dense, s, z, r, reps) + return_expert(*d_expert, s, r, reps)

time: 1280 us -> 1350 us (1.055)
  Pallas kernels: 181 us -> 524 us
  blocking collectives: 152 us -> 42.6 us
  matrix products: 180 us -> 121 us
  waiting for transfers between devices: 264 us -> 211 us
  starting transfers between devices: 107 us -> 57.7 us
  other arithmetic: 157 us -> 129 us
  local copies, waits for them, and re-layouts: 211 us -> 236 us
    pallas_call x0 -> x5, Pallas kernels: none -> 431 us  [call(): pl.pallas_call(body, out_shape=[jax.ShapeDtypeStruct(shape, kind) for sha...]
    all_gather x1 -> x0, blocking collectives: 95.7 us -> none  [local(): small = lax.all_gather(small, ('seq', 'fsdp'), axis=2, tiled=True)]
    pallas_call x8 -> x4, Pallas kernels: 181 us -> 93.1 us  [exchange(): pl.pallas_call(exchange_kernel, out_shape=jax.ShapeDtypeStruct(x.shape, x...]
    convert_element_type x0 -> x10, local copies, waits for them, and re-layouts: none -> 75.3 us  [the longest x4 57.1 us: local(): joint_e.transpose(0, 3, 2, 1, 4).reshape(2 * SLOTS, -1).astype(f32)]
    dot_general x22 -> x6, matrix products: 37.6 us -> 2.7 us  [dot(): return jnp.dot(a, b, preferred_element_type=f32)]
    ppermute x14 -> x4, waiting for transfers between devices: 32.6 us -> 0.01 us  [the longest x2 0.01 us: layer_backward(): lax.ppermute(lax.dynamic_index_in_dim(back, 1 - core, 0, False).astype(bf...]
    all_to_all x5 -> x0, starting transfers between devices: 32.1 us -> none  [the longest x2 15.2 us: fetch_expert(): lax.all_to_all(first, 'fsdp', split_axis=0, concat_axis=0, tiled=True)]
    all_to_all x5 -> x0, waiting for transfers between devices: 31.3 us -> none  [the longest x2 15.7 us: fetch_expert(): lax.all_to_all(first, 'fsdp', split_axis=0, concat_axis=0, tiled=True)]
  transfers between devices with their start and end apart: 87 -> 51, of which waited for: 23 -> 18; matrix products, arithmetic and copies ran while one was open for 38% -> 31% of each run, Pallas kernels for 14% -> 5%
where the time goes in v2:
time: 1350 us; the launch traced here: 1340 us
  Pallas kernels  524 us (39%)
  local copies, waits for them, and re-layouts  236 us (17%)
  waiting for transfers between devices  211 us (16%)
  other arithmetic  129 us (10%)
  matrix products  121 us (9%)
  starting transfers between devices  57.7 us (4%)
  blocking collectives  42.6 us (3%)
  between operations  16.8 us (1%)
    pallas_call x5, Pallas kernels, call(): pl.pallas_call(body, out_shape=[jax.ShapeDtypeStruct(shape, kind) for sha...  431 us
    ppermute x8, waiting for transfers between devices, scatter_rep(): got = lax.ppermute(other, 'rep', rep_pairs(reps))  121 us
    pallas_call x4, Pallas kernels, exchange(): pl.pallas_call(exchange_kernel, out_shape=jax.ShapeDtypeStruct(x.shape, x...  93.1 us
    convert_element_type x4, local copies, waits for them, and re-layouts, local(): joint_e.transpose(0, 3, 2, 1, 4).reshape(2 * SLOTS, -1).astype(f32)  57.1 us
    unnamed x329, local copies, waits for them, and re-layouts  43.3 us
    dot_general x18, matrix products, dot_tn(): lax.dot_general(a, b, (((0,), (0,)), ((), ())), preferred_element_type=f32)  42.8 us
    psum x1, blocking collectives, local(): total = lax.psum(jnp.stack(smalls), ('rep', 'seq', 'fsdp'))  42.6 us
    dot_general x14, matrix products, dot_nt(): lax.dot_general(a, b, (((1,), (1,)), ((), ())), preferred_element_type=f32)  38.3 us
  transfers between devices with their start and end apart: 51, of which 18 were waited for; matrix products, arithmetic and copies ran while one was open for 31% of the time, Pallas kernels for 5%

profile of v2, /device:TPU:8, one launch (start us, length us, event | category | flops | bytes accessed | tf_op | source)
XLA Modules:
  0.0 1337.6 jit_solution(11455452703465955593)
XLA Ops:
  11.9 34.8 %shard_map.195 = (bf16[4,4,16,128]{3,2,1,0:T(8,128)(2,1)}, bf16[4,4,48,576]{3,2,1,0:T(8,128)(2,1)}, bf16[4,48,768]{2,1,0:T(8,128)(2,1)}) custom-call(bf16[16,128]{1,0:T(8,128)(2,1)} %pad.11.refs_0_, bf16[2,4,48,576]{3,2,1,0:T(8,128)(2,1)} %reshape.691.refs_1_.refs_9_, bf16[2,48,768]{2,1,0:T(8,128)(2,1)} %refs_10_.1), custom_call_target="tpu_custom_call" | custom-call | bytes 1048576 | tf_op jit(solution)/shard_map/pallas_call | solution.py:526
  61.5 119.5 %shard_map.196 = (f32[256,768]{1,0:T(8,128)}, bf16[256,768]{1,0:T(8,128)(2,1)}, bf16[4,256,768]{2,1,0:T(8,128)(2,1)}, bf16[3,4,256,64]{3,2,1,0:T(8,128)(2,1)}, b...) custom-call(f32[256,768]{1,0:T(8,128)} %bitcast_convert_fusion.2.ref, ...), custom_call_target="tpu_custom_call" | custom-call | bytes 1048576 | tf_op jit(solution)/shard_map/pallas_call | solution.py:526
  181.0 125.1 %shard_map.197 = (f32[256,768]{1,0:T(8,128)}, f32[256,128]{1,0:T(8,128)}, bf16[512,768]{1,0:T(8,128)(2,1)}, bf16[4,256,768]{2,1,0:T(8,128)(2,1)}, bf16[2,4,256,5...) custom-call(bf16[256,768]{1,0:T(8,128)(2,1)} %get-tuple-element.60.r, ...), custom_call_target="tpu_custom_call" | custom-call | bytes 1048576 | tf_op jit(solution)/shard_map/pallas_call | solution.py:526
  306.1 88.7 %shard_map.198 = (f32[256,768]{1,0:T(8,128)}, bf16[256,768]{1,0:T(8,128)(2,1)}, bf16[4,256,768]{2,1,0:T(8,128)(2,1)}, bf16[3,4,256,64]{3,2,1,0:T(8,128)(2,1)}, b...) custom-call(f32[256,768]{1,0:T(8,128)} %get-tuple-element.66.refs_0_, ...), custom_call_target="tpu_custom_call" | custom-call | bytes 1048576 | tf_op jit(solution)/shard_map/pallas_call | solution.py:526
  394.8 62.4 %shard_map.199 = (f32[256,768]{1,0:T(8,128)}, f32[256,128]{1,0:T(8,128)}, bf16[512,768]{1,0:T(8,128)(2,1)}, bf16[4,256,768]{2,1,0:T(8,128)(2,1)}, bf16[2,4,256,5...) custom-call(bf16[256,768]{1,0:T(8,128)(2,1)} %get-tuple-element.69.r, ...), custom_call_target="tpu_custom_call" | custom-call | bytes 1048576 | tf_op jit(solution)/shard_map/pallas_call | solution.py:526
  461.7 21.8 %shard_map.200 = bf16[4,144,768]{2,1,0:T(8,128)(2,1)S(1)} custom-call(bf16[4,144,768]{2,1,0:T(8,128)(2,1)S(1)} %bitcast.600), custom_call_target="tpu_custom_call" | custom-call | tf_op jit(solution)/shard_map/pallas_call | solution.py:75
  501.3 7.3 convert_bitcast_fusion.1
  508.6 16.0 %copy.451 = f32[2,576,2,2,512]{1,0,4,3,2:T(2,128)} copy(f32[2,576,2,2,512]{4,1,2,3,0:T(8,128)} %convert_bitcast_fusion.1) | data formatting | bytes 18874368 | tf_op jit(solution)/shard_map/convert_element_type | solution.py:906
  524.6 12.5 reshape.784
  562.5 7.3 convert_bitcast_fusion
  569.7 16.0 %copy.455 = f32[2,576,2,2,512]{1,0,4,3,2:T(2,128)} copy(f32[2,576,2,2,512]{4,1,2,3,0:T(8,128)} %convert_bitcast_fusion) | data formatting | bytes 18874368 | tf_op jit(solution)/shard_map/convert_element_type | solution.py:906
  585.8 12.6 reshape.786
  652.1 6.4 fusion.162
  658.5 6.4 fusion.156
  673.7 6.5 fusion.13
  686.2 7.0 convolution_convert_fusion
  698.4 8.2 constant_dynamic-slice_fusion.2
  727.4 34.6 %collective-permute-done.39 = bf16[2,4,64,768]{3,2,1,0:T(8,128)(2,1)S(1)} collective-permute-done((bf16[2,4,64,768]{3,2,1,0:T(8,128)(2,1)S(1)}, bf16[2,4,64,768]{3,2,1,0:T(8,128)(2,1)S(1)}, u32[]{:S(2)}, u32[]{:S(2)}) %collective-permute-start.39) | collective-permute-done | bytes 786464 | tf_op jit(solution)/shard_map/ppermute | solution.py:121
  766.8 20.8 %shard_map.201 = bf16[4,144,768]{2,1,0:T(8,128)(2,1)S(1)} custom-call(bf16[4,144,768]{2,1,0:T(8,128)(2,1)S(1)} %bitcast.596), custom_call_target="tpu_custom_call" | custom-call | tf_op jit(solution)/shard_map/pallas_call | solution.py:75
  813.9 9.3 collective-permute-done.33
  863.4 30.0 %collective-permute-done.26 = bf16[4,88,768]{2,1,0:T(8,128)(2,1)} collective-permute-done((bf16[4,88,768]{2,1,0:T(8,128)(2,1)}, bf16[4,88,768]{2,1,0:T(8,128)(2,1)}, u32[]{:S(2)}, u32[]{:S(2)}) %collective-permute-start.26) | collective-permute-done | bytes 540704 | tf_op jit(solution)/shard_map/ppermute | solution.py:121
  900.5 29.6 %shard_map.202 = bf16[4,144,768]{2,1,0:T(8,128)(2,1)S(1)} custom-call(bf16[4,144,768]{2,1,0:T(8,128)(2,1)S(1)} %bitcast.601), custom_call_target="tpu_custom_call" | custom-call | tf_op jit(solution)/shard_map/pallas_call | solution.py:75
  951.4 6.3 fusion.10
  963.7 7.0 convolution_convert_fusion.1
  975.7 10.0 constant_dynamic-slice_fusion.4
  1013.9 35.9 %collective-permute-done.36 = bf16[2,4,64,768]{3,2,1,0:T(8,128)(2,1)S(1)} collective-permute-done((bf16[2,4,64,768]{3,2,1,0:T(8,128)(2,1)S(1)}, bf16[2,4,64,768]{3,2,1,0:T(8,128)(2,1)S(1)}, u32[]{:S(2)}, u32[]{:S(2)}) %collective-permute-start.36) | collective-permute-done | bytes 786464 | tf_op jit(solution)/shard_map/ppermute | solution.py:121
  1054.6 21.0 %shard_map.203 = bf16[4,144,768]{2,1,0:T(8,128)(2,1)S(1)} custom-call(bf16[4,144,768]{2,1,0:T(8,128)(2,1)S(1)} %bitcast.597), custom_call_target="tpu_custom_call" | custom-call | tf_op jit(solution)/shard_map/pallas_call | solution.py:75
  1104.3 8.5 collective-permute-done.29
  1169.0 14.5 %collective-permute-done.20 = bf16[4,4,24,1600]{3,2,0,1:T(8,128)(2,1)} collective-permute-done((bf16[4,4,24,1600]{3,2,0,1:T(8,128)(2,1)}, bf16[4,4,24,1600]{3,2,0,1:T(8,128)(2,1)}, u32[]{:S(2)}, u32[]{:S(2)}) %collective-permute-start.20) | collective-permute-done | bytes 1228832 | tf_op jit(solution)/shard_map/ppermute | solution.py:121
  1187.2 42.6 %psum.7 = f32[2,6,768]{2,1,0:T(8,128)S(1)} all-reduce(f32[2,6,768]{2,1,0:T(8,128)S(1)} %pad_maximum_fusion.50), channel_id=1, replica_groups=mesh['rep'=2,'seq'=4,'fsdp'=4] {'rep','seq','fsdp'}, use_global_device_ids=true, to_apply=%region_24.25 | all-reduce | flops 9216 | bytes 73728 | tf_op jit(solution)/shard_map/psum | solution.py:922
  1240.6 12.5 collective-permute-done.31
  1260.2 31.2 %all-reduce.8.cloned.1.call-done = (bf16[4,4,24,1600]{3,2,0,1:T(8,128)(2,1)}, bf16[4,4,24,1600]{3,2,0,1:T(8,128)(2,1)}) async-done(((bf16[4,4,24,1600]{3,2,0,1:T(8,128)(2,1)}, bf16[4,4,24,1600]{3,2,0,1:T(8,128)(2,1)}), (bf16[4,4,24,1600]{3,2,0,1:T(8,128)(2,1)}, bf16[4,4,24,1600]{3,2,0,1:T(8,128)(2,1)})) %all-reduce.8.cloned.1.call-update) | async-done | bytes 2457616
  (728 shorter events, 448.4 us)
Async XLA Ops:
  483.5 188.7 %collective-permute-start.4 = (bf16[576,768]{1,0:T(8,128)(2,1)S(1)}, bf16[576,768]{1,0:T(8,128)(2,1)}, u32[]{:S(2)}, u32[]{:S(2)}) collective-permute-start(bf16[576,768]{1,0:T(8,128)(2,1)S(1)} %bitcast.594), channel_id=1, source_target_pairs={{0,4},{4,0},{8,12},{12,8},{1,5},{5,1},{9,13},{13,9},{2,6},{6,2},{1... | collective-permute-start | bytes 2654216 | tf_op jit(solution)/shard_map/ppermute | solution.py:788
  483.5 186.5 %collective-permute-start = (bf16[256,768]{1,0:T(8,128)(2,1)S(1)}, bf16[256,768]{1,0:T(8,128)(2,1)}, u32[]{:S(2)}, u32[]{:S(2)}) collective-permute-start(bf16[256,768]{1,0:T(8,128)(2,1)S(1)} %bitcast.619), channel_id=1, source_target_pairs={{0,8},{4,12},{8,0},{12,4},{1,9},{5,13},{9,1},{13,5},{2,10},{6,14},... | collective-permute-start | bytes 1179656 | tf_op jit(solution)/shard_map/ppermute | solution.py:92
  672.0 40.8 %collective-permute-start.1 = (bf16[2,256,768]{2,1,0:T(8,128)(2,1)}, bf16[2,256,768]{2,1,0:T(8,128)(2,1)}, u32[]{:S(2)}, u32[]{:S(2)}) collective-permute-start(bf16[2,256,768]{2,1,0:T(8,128)(2,1)} %pad_maximum_fusion.32), channel_id=1, source_target_pairs={{0,4},{4,0},{8,12},{12,8},{1,5},{5,1},{9,13},{13,9},{2,6},{6,2},{1... | collective-permute-start | bytes 2359304 | tf_op jit(solution)/shard_map/ppermute | solution.py:93
  685.2 80.1 %collective-permute-start.5 = (bf16[576,768]{1,0:T(8,128)(2,1)}, bf16[576,768]{1,0:T(8,128)(2,1)}, u32[]{:S(2)}, u32[]{:S(2)}) collective-permute-start(bf16[576,768]{1,0:T(8,128)(2,1)} %fusion.100), channel_id=1, source_target_pairs={{0,4},{4,0},{8,12},{12,8},{1,5},{5,1},{9,13},{13,9},{2,6},{6,2},{1... | collective-permute-start | bytes 2654216 | tf_op jit(solution)/shard_map/ppermute | solution.py:797
  708.2 89.5 %collective-permute-start.32 = (bf16[2,2,4,48,2,512]{5,3,4,2,1,0:T(8,128)(2,1)}, bf16[2,2,4,48,2,512]{5,3,4,2,1,0:T(8,128)(2,1)}, u32[]{:S(2)}, u32[]{:S(2)}) collective-permute-start(bf16[2,2,4,48,2,512]{5,3,4,2,1,0:T(8,128)(2,1)} %bitcast.589), channel_id=1, source_target_pairs={{0,16},{16,0},{1,17},{17,1},{2,18},{18,2},{3,19},{19,3},{4,20},{20... | collective-permute-start | bytes 4718600 | tf_op jit(solution)/shard_map/ppermute | solution.py:121
  711.7 50.3 %collective-permute-start.39 = (bf16[2,4,64,768]{3,2,1,0:T(8,128)(2,1)S(1)}, bf16[2,4,64,768]{3,2,1,0:T(8,128)(2,1)S(1)}, u32[]{:S(2)}, u32[]{:S(2)}) collective-permute-start(bf16[2,4,64,768]{3,2,1,0:T(8,128)(2,1)S(1)} %dynamic-slice_bitcast_fusion), channel_id=1, source_target_pairs={{0,16},{16,0},{1,17},{17,1},{2,18},{18,2},{3,19},{19,3},{4,20},{20... | collective-permute-start | bytes 2359304 | tf_op jit(solution)/shard_map/ppermute | solution.py:121
  722.1 41.7 %collective-permute-start.2 = (bf16[2,256,768]{2,1,0:T(8,128)(2,1)S(1)}, bf16[2,256,768]{2,1,0:T(8,128)(2,1)S(1)}, u32[]{:S(2)}, u32[]{:S(2)}) collective-permute-start(bf16[2,256,768]{2,1,0:T(8,128)(2,1)S(1)} %pad_maximum_fusion.33), channel_id=1, source_target_pairs={{0,4},{4,0},{8,12},{12,8},{1,5},{5,1},{9,13},{13,9},{2,6},{6,2},{1... | collective-permute-start | bytes 2359304 | tf_op jit(solution)/shard_map/ppermute | solution.py:100
  762.2 25.3 %collective-permute-start.40 = (bf16[4,64,768]{2,1,0:T(8,128)(2,1)S(1)}, bf16[4,64,768]{2,1,0:T(8,128)(2,1)S(1)}, u32[]{:S(2)}, u32[]{:S(2)}) collective-permute-start(bf16[4,64,768]{2,1,0:T(8,128)(2,1)S(1)} %dynamic-slice_bitcast_fusion.6), channel_id=1, source_target_pairs={{0,8},{4,12},{8,0},{12,4},{1,9},{5,13},{9,1},{13,5},{2,10},{6,14},... | collective-permute-start | bytes 1179656 | tf_op jit(solution)/shard_map/ppermute | solution.py:174
  764.9 27.6 %collective-permute-start.3 = (bf16[256,768]{1,0:T(8,128)(2,1)}, bf16[256,768]{1,0:T(8,128)(2,1)}, u32[]{:S(2)}, u32[]{:S(2)}) collective-permute-start(bf16[256,768]{1,0:T(8,128)(2,1)} %fusion.146), channel_id=1, source_target_pairs={{0,8},{4,12},{8,0},{12,4},{1,9},{5,13},{9,1},{13,5},{2,10},{6,14},... | collective-permute-start | bytes 1179656 | tf_op jit(solution)/shard_map/ppermute | solution.py:102
  800.8 22.4 %collective-permute-start.33 = (bf16[2,4,48,2,512]{4,2,3,1,0:T(8,128)(2,1)}, bf16[2,4,48,2,512]{4,2,3,1,0:T(8,128)(2,1)}, u32[]{:S(2)}, u32[]{:S(2)}) collective-permute-start(bf16[2,4,48,2,512]{4,2,3,1,0:T(8,128)(2,1)} %dynamic-slice_bitcast_fusion.2), channel_id=1, source_target_pairs={{0,8},{4,12},{8,0},{12,4},{1,9},{5,13},{9,1},{13,5},{2,10},{6,14},... | collective-permute-start | bytes 2359304 | tf_op jit(solution)/shard_map/ppermute | solution.py:163
  808.3 17.0 %collective-permute-start.7 = (bf16[2,256,768]{2,1,0:T(8,128)(2,1)S(1)}, bf16[2,256,768]{2,1,0:T(8,128)(2,1)S(1)}, u32[]{:S(2)}, u32[]{:S(2)}) collective-permute-start(bf16[2,256,768]{2,1,0:T(8,128)(2,1)S(1)} %pad_maximum_fusion.34), channel_id=1, source_target_pairs={{0,4},{4,0},{8,12},{12,8},{1,5},{5,1},{9,13},{13,9},{2,6},{6,2},{1... | collective-permute-start | bytes 2359304 | tf_op jit(solution)/shard_map/ppermute | solution.py:93
  825.3 31.7 %collective-permute-start.34 = (bf16[4,48,2,512]{3,1,2,0:T(8,128)(2,1)}, bf16[4,48,2,512]{3,1,2,0:T(8,128)(2,1)}, u32[]{:S(2)}, u32[]{:S(2)}) collective-permute-start(bf16[4,48,2,512]{3,1,2,0:T(8,128)(2,1)} %dynamic-slice_bitcast_fusion.8), channel_id=1, source_target_pairs={{0,4},{4,0},{8,12},{12,8},{1,5},{5,1},{9,13},{13,9},{2,6},{6,2},{1... | collective-permute-start | bytes 1179656 | tf_op jit(solution)/shard_map/ppermute | solution.py:166
  851.1 89.7 %collective-permute-start.22 = (bf16[4,4,24,1600]{3,2,0,1:T(8,128)(2,1)}, bf16[4,4,24,1600]{3,2,0,1:T(8,128)(2,1)}, u32[]{:S(2)}, u32[]{:S(2)}) collective-permute-start(bf16[4,4,24,1600]{3,2,0,1:T(8,128)(2,1)} %fusion.67), channel_id=1, source_target_pairs={{0,16},{16,0},{1,17},{17,1},{2,18},{18,2},{3,19},{19,3},{4,20},{20... | collective-permute-start | bytes 3686408 | tf_op jit(solution)/shard_map/ppermute | solution.py:121
  853.0 40.4 %collective-permute-start.26 = (bf16[4,88,768]{2,1,0:T(8,128)(2,1)}, bf16[4,88,768]{2,1,0:T(8,128)(2,1)}, u32[]{:S(2)}, u32[]{:S(2)}) collective-permute-start(bf16[4,88,768]{2,1,0:T(8,128)(2,1)} %dynamic-slice_bitcast_fusion.4), channel_id=1, source_target_pairs={{0,16},{16,0},{1,17},{17,1},{2,18},{18,2},{3,19},{19,3},{4,20},{20... | collective-permute-start | bytes 1622024 | tf_op jit(solution)/shard_map/ppermute | solution.py:121
  855.5 39.9 %collective-permute-start.9 = (bf16[256,768]{1,0:T(8,128)(2,1)}, bf16[256,768]{1,0:T(8,128)(2,1)}, u32[]{:S(2)}, u32[]{:S(2)}) collective-permute-start(bf16[256,768]{1,0:T(8,128)(2,1)} %fusion.147), channel_id=1, source_target_pairs={{0,8},{4,12},{8,0},{12,4},{1,9},{5,13},{9,1},{13,5},{2,10},{6,14},... | collective-permute-start | bytes 1179656 | tf_op jit(solution)/shard_map/ppermute | solution.py:102
  859.1 84.7 %all-to-all-start.3 = ((bf16[4,48,2,2,512]{4,1,3,2,0:T(8,128)(2,1)}), bf16[4,48,2,2,512]{4,1,3,2,0:T(8,128)(2,1)}, u32[]{:S(2)}, u32[]{:S(2)}) async-start(bf16[4,48,2,2,512]{4,1,3,2,0:T(8,128)(2,1)} %pad_maximum_fusion.41), calls=%async_computation.5 | async-start | bytes 1572864 | tf_op jit(solution)/shard_map/all_to_all | solution.py:168
  863.4 76.2 %reduce-scatter.7.cloned.1.call-start = ((), (), s32[]{:S(2)}) async-start(), calls=%async_computation.9 | async-start | bytes 675840 | tf_op jit(solution)/shard_map/reduce_scatter | solution.py:146
  930.0 19.7 %collective-permute-start.14 = (bf16[576,768]{1,0:T(8,128)(2,1)S(1)}, bf16[576,768]{1,0:T(8,128)(2,1)}, u32[]{:S(2)}, u32[]{:S(2)}) collective-permute-start(bf16[576,768]{1,0:T(8,128)(2,1)S(1)} %bitcast.595), channel_id=1, source_target_pairs={{0,4},{4,0},{8,12},{12,8},{1,5},{5,1},{9,13},{13,9},{2,6},{6,2},{1... | collective-permute-start | bytes 2654216 | tf_op jit(solution)/shard_map/ppermute | solution.py:788
  943.8 41.9 %collective-permute-start.35 = (bf16[4,48,2,2,512]{4,1,3,2,0:T(8,128)(2,1)}, bf16[4,48,2,2,512]{4,1,3,2,0:T(8,128)(2,1)}, u32[]{:S(2)}, u32[]{:S(2)}) collective-permute-start(bf16[4,48,2,2,512]{4,1,3,2,0:T(8,128)(2,1)} %all-to-all-done.3), channel_id=1, source_target_pairs={{0,16},{16,0},{1,17},{17,1},{2,18},{18,2},{3,19},{19,3},{4,20},{20... | collective-permute-start | bytes 2359304 | tf_op jit(solution)/shard_map/ppermute | solution.py:127
  948.6 52.0 %collective-permute-start.11 = (bf16[2,256,768]{2,1,0:T(8,128)(2,1)}, bf16[2,256,768]{2,1,0:T(8,128)(2,1)}, u32[]{:S(2)}, u32[]{:S(2)}) collective-permute-start(bf16[2,256,768]{2,1,0:T(8,128)(2,1)} %pad_maximum_fusion.36), channel_id=1, source_target_pairs={{0,4},{4,0},{8,12},{12,8},{1,5},{5,1},{9,13},{13,9},{2,6},{6,2},{1... | collective-permute-start | bytes 2359304 | tf_op jit(solution)/shard_map/ppermute | solution.py:93
  962.7 90.4 %collective-permute-start.15 = (bf16[576,768]{1,0:T(8,128)(2,1)}, bf16[576,768]{1,0:T(8,128)(2,1)}, u32[]{:S(2)}, u32[]{:S(2)}) collective-permute-start(bf16[576,768]{1,0:T(8,128)(2,1)} %fusion.101), channel_id=1, source_target_pairs={{0,4},{4,0},{8,12},{12,8},{1,5},{5,1},{9,13},{13,9},{2,6},{6,2},{1... | collective-permute-start | bytes 2654216 | tf_op jit(solution)/shard_map/ppermute | solution.py:797
  995.9 91.1 %collective-permute-start.28 = (bf16[2,2,4,48,2,512]{5,3,4,2,1,0:T(8,128)(2,1)}, bf16[2,2,4,48,2,512]{5,3,4,2,1,0:T(8,128)(2,1)}, u32[]{:S(2)}, u32[]{:S(2)}) collective-permute-start(bf16[2,2,4,48,2,512]{5,3,4,2,1,0:T(8,128)(2,1)} %bitcast.590), channel_id=1, source_target_pairs={{0,16},{16,0},{1,17},{17,1},{2,18},{18,2},{3,19},{19,3},{4,20},{20... | collective-permute-start | bytes 4718600 | tf_op jit(solution)/shard_map/ppermute | solution.py:121
  999.5 50.3 %collective-permute-start.36 = (bf16[2,4,64,768]{3,2,1,0:T(8,128)(2,1)S(1)}, bf16[2,4,64,768]{3,2,1,0:T(8,128)(2,1)S(1)}, u32[]{:S(2)}, u32[]{:S(2)}) collective-permute-start(bf16[2,4,64,768]{3,2,1,0:T(8,128)(2,1)S(1)} %dynamic-slice_bitcast_fusion.1), channel_id=1, source_target_pairs={{0,16},{16,0},{1,17},{17,1},{2,18},{18,2},{3,19},{19,3},{4,20},{20... | collective-permute-start | bytes 2359304 | tf_op jit(solution)/shard_map/ppermute | solution.py:121
  1009.7 41.9 %collective-permute-start.12 = (bf16[2,256,768]{2,1,0:T(8,128)(2,1)S(1)}, bf16[2,256,768]{2,1,0:T(8,128)(2,1)S(1)}, u32[]{:S(2)}, u32[]{:S(2)}) collective-permute-start(bf16[2,256,768]{2,1,0:T(8,128)(2,1)S(1)} %pad_maximum_fusion.37), channel_id=1, source_target_pairs={{0,4},{4,0},{8,12},{12,8},{1,5},{5,1},{9,13},{13,9},{2,6},{6,2},{1... | collective-permute-start | bytes 2359304 | tf_op jit(solution)/shard_map/ppermute | solution.py:100
  1050.1 25.5 %collective-permute-start.37 = (bf16[4,64,768]{2,1,0:T(8,128)(2,1)S(1)}, bf16[4,64,768]{2,1,0:T(8,128)(2,1)S(1)}, u32[]{:S(2)}, u32[]{:S(2)}) collective-permute-start(bf16[4,64,768]{2,1,0:T(8,128)(2,1)S(1)} %dynamic-slice_bitcast_fusion.7), channel_id=1, source_target_pairs={{0,8},{4,12},{8,0},{12,4},{1,9},{5,13},{9,1},{13,5},{2,10},{6,14},... | collective-permute-start | bytes 1179656 | tf_op jit(solution)/shard_map/ppermute | solution.py:174
  1052.7 28.2 %collective-permute-start.13 = (bf16[256,768]{1,0:T(8,128)(2,1)}, bf16[256,768]{1,0:T(8,128)(2,1)}, u32[]{:S(2)}, u32[]{:S(2)}) collective-permute-start(bf16[256,768]{1,0:T(8,128)(2,1)} %fusion.148), channel_id=1, source_target_pairs={{0,8},{4,12},{8,0},{12,4},{1,9},{5,13},{9,1},{13,5},{2,10},{6,14},... | collective-permute-start | bytes 1179656 | tf_op jit(solution)/shard_map/ppermute | solution.py:102
  1080.5 150.6 %reduce-scatter.5.cloned.1.call-start = ((), (), s32[]{:S(2)}) async-start(), calls=%async_computation.8 | async-start | bytes 675840 | tf_op jit(solution)/shard_map/reduce_scatter | solution.py:146
  1090.2 22.6 %collective-permute-start.29 = (bf16[2,4,48,2,512]{4,2,3,1,0:T(8,128)(2,1)}, bf16[2,4,48,2,512]{4,2,3,1,0:T(8,128)(2,1)}, u32[]{:S(2)}, u32[]{:S(2)}) collective-permute-start(bf16[2,4,48,2,512]{4,2,3,1,0:T(8,128)(2,1)} %dynamic-slice_bitcast_fusion.3), channel_id=1, source_target_pairs={{0,8},{4,12},{8,0},{12,4},{1,9},{5,13},{9,1},{13,5},{2,10},{6,14},... | collective-permute-start | bytes 2359304 | tf_op jit(solution)/shard_map/ppermute | solution.py:163
  1147.1 36.3 %collective-permute-start.20 = (bf16[4,4,24,1600]{3,2,0,1:T(8,128)(2,1)}, bf16[4,4,24,1600]{3,2,0,1:T(8,128)(2,1)}, u32[]{:S(2)}, u32[]{:S(2)}) collective-permute-start(bf16[4,4,24,1600]{3,2,0,1:T(8,128)(2,1)} %fusion.71), channel_id=1, source_target_pairs={{0,16},{16,0},{1,17},{17,1},{2,18},{18,2},{3,19},{19,3},{4,20},{20... | collective-permute-start | bytes 3686408 | tf_op jit(solution)/shard_map/ppermute | solution.py:121
  1161.0 73.6 %all-to-all-start.2 = ((bf16[4,48,2,2,512]{4,1,3,2,0:T(8,128)(2,1)}), bf16[4,48,2,2,512]{4,1,3,2,0:T(8,128)(2,1)}, u32[]{:S(2)}, u32[]{:S(2)}) async-start(bf16[4,48,2,2,512]{4,1,3,2,0:T(8,128)(2,1)} %pad_maximum_fusion.40), calls=%async_computation.4 | async-start | bytes 1572864 | tf_op jit(solution)/shard_map/all_to_all | solution.py:168
  1165.2 126.3 %all-reduce.8.cloned.1.call-start = ((), (), s32[]{:S(2)}) async-start(), calls=%async_computation.10 | async-start | bytes 5111808
  1234.6 18.5 %collective-permute-start.31 = (bf16[4,48,2,2,512]{4,1,3,2,0:T(8,128)(2,1)}, bf16[4,48,2,2,512]{4,1,3,2,0:T(8,128)(2,1)S(1)}, u32[]{:S(2)}, u32[]{:S(2)}) collective-permute-start(bf16[4,48,2,2,512]{4,1,3,2,0:T(8,128)(2,1)} %all-to-all-done.2), channel_id=1, source_target_pairs={{0,16},{16,0},{1,17},{17,1},{2,18},{18,2},{3,19},{19,3},{4,20},{20... | collective-permute-start | bytes 2359304 | tf_op jit(solution)/shard_map/ppermute | solution.py:127
  (176 other events, 2699.2 us)
Sparse Core Ops, SparseCore 0:
  895.5 29.9 reduce-scatter.6
  1158.9 27.7 reduce-scatter.4
  1189.7 101.6 all-reduce.7

commit v3 on v2

v3 whole, which is shorter than its diff:
```python
import functools

import jax
import jax.numpy as jnp
from jax import lax
from jax.experimental import pallas as pl
from jax.experimental.pallas import tpu as pltpu
from jax.sharding import PartitionSpec as P

D = 768
HEADS = 12
HEAD_DIM = 64
FF = 2048
EXPERTS = 4
LAYERS = 2
CAP = 144
EPS = 1e-06
MASKED = -1e30
SEQ = 4
FSDP = 4
HEADS_DEV = HEADS // SEQ
COLS = HEADS_DEV * HEAD_DIM
FF_DEV = FF // SEQ
FF_CORE = FF // 2
SLOTS = EXPERTS * CAP
bf16 = jnp.bfloat16
f32 = jnp.float32
MESH = pl.DeviceIdType.MESH


def dot(a, b):
    return jnp.dot(a, b, preferred_element_type=f32)


def dot_nt(a, b):
    return lax.dot_general(a, b, (((1,), (1,)), ((), ())), preferred_element_type=f32)


def dot_tn(a, b):
    return lax.dot_general(a, b, (((0,), (0,)), ((), ())), preferred_element_type=f32)


def rep_rest(x, reps):
    bit = 2
    while bit < reps:
        x = x + lax.ppermute(x, "rep", [(i, i ^ bit) for i in range(reps)])
        bit *= 2
    return x


def routing(choices, order):
    tokens = choices.shape[0]
    pairs = 2 * tokens
    flat = choices.reshape(-1)
    ids = jnp.arange(pairs, dtype=jnp.int32)
    place = (order[:, None] == ids[None, :]).astype(bf16)
    experts = (flat[:, None] == jnp.arange(EXPERTS, dtype=jnp.int32)[None, :]).astype(bf16)
    placed = dot(place, experts).astype(bf16)
    lower = (ids[:, None] > ids[None, :]).astype(bf16)
    slot_placed = jnp.minimum(jnp.sum(dot(lower, placed) * placed.astype(f32), 1), float(CAP))
    slot = dot_tn(place, slot_placed[:, None].astype(bf16))[:, 0].astype(jnp.int32)
    kept = slot < CAP
    target = jnp.where(kept, flat * CAP + slot, SLOTS).reshape(tokens, 2)
    target = target.T.reshape(-1)
    chosen = (target[None, :] == jnp.arange(SLOTS, dtype=jnp.int32)[:, None]).astype(bf16)
    return kept.reshape(tokens, 2).astype(f32), chosen


class Net:
    def __init__(self, send, recv, local_sems):
        self.send, self.recv, self.local_sems = send, recv, local_sems
        self.count = 0
        self.local_count = 0
        self.r, self.s, self.z = (lax.axis_index(a) for a in ("rep", "seq", "fsdp"))
        self.half = lax.rem(self.r, 2)
        self.core = lax.rem(self.s, 2)
        self.far = self.s // 2
        self.partner = self.r + 1 - 2 * self.half

    def seq(self, d):
        core = self.core if d % 2 == 0 else 1 - self.core
        far = self.far if d < 2 else 1 - self.far
        return far * 2 + core

    def plane(self, k):
        return lax.rem(self.z + k, FSDP)

    def copy(self, src, dst, **device):
        k = self.count
        self.count += 1
        out = pltpu.make_async_remote_copy(
            src_ref=src, dst_ref=dst, send_sem=self.send.at[k], recv_sem=self.recv.at[k],
            device_id=device, device_id_type=MESH,
        )
        out.start()
        return out

    def move(self, src, dst):
        k = self.local_count
        self.local_count += 1
        out = pltpu.make_async_copy(src, dst, self.local_sems.at[k])
        out.start()
        return out

    def greet(self, devices):
        self.barrier = pltpu.get_barrier_semaphore()
        for device in devices:
            pl.semaphore_signal(self.barrier, inc=1, device_id=device, device_id_type=MESH)
        self.greeted = len(devices)

    def met(self):
        pl.semaphore_wait(self.barrier, self.greeted)

    def everyone(self):
        seqs = [{"seq": self.seq(d)} for d in (1, 2, 3)]
        planes = [{"fsdp": self.plane(k)} for k in (1, 2, 3)]
        both = [{"seq": self.seq(1), "fsdp": self.plane(k)} for k in (1, 2, 3)]
        return seqs + planes + both + [{"rep": self.partner}]


def columns(start, size):
    return pl.ds(pl.multiple_of(start, 128), size)


def wait_all(copies):
    for copy in copies:
        copy.wait()


class Job:
    space = pl.ANY
    out_space = pl.ANY
    scratch = ()
    kind = bf16

    def __init__(self, net, layer, ins, outs, scratch):
        self.net, self.layer = net, layer
        self.bind(ins, outs, scratch)


class ExpertPlane(Job):
    inputs = ("expert_in", "expert_out")
    shapes = ((2, 2, 4, 48, FF_DEV), (4, 128, 384))

    def bind(self, ins, outs, scratch):
        self.first, self.second = ins
        self.p1, self.p2 = outs

    def stages(self):
        return [self.plane_begin, self.plane_finish]

    def plane_begin(self):
        n = self.net
        self.copies = []
        for k in (2, 1, 3, 0):
            e = n.plane(k)
            for d in (0, 1):
                core = n.core if d == 0 else 1 - n.core
                for gu in (0, 1):
                    src = self.first.at[
                        self.layer, e, :, columns(gu * FF + n.half * FF_CORE + core * FF_DEV, FF_DEV)
                    ]
                    dst = self.p1.at[gu, n.core, n.z]
                    if k == 0 and d == 0:
                        self.copies.append(n.move(src, dst))
                    else:
                        self.copies.append(n.copy(src, dst, seq=n.seq(d), fsdp=e))
            src = self.second.at[self.layer, e, :, columns(n.half * 384, 384)]
            dst = self.p2.at[n.z]
            self.copies.append(n.move(src, dst) if k == 0 else n.copy(src, dst, fsdp=e))

    def plane_finish(self):
        wait_all(self.copies)


class ExpertSides(Job):
    inputs = ("p1", "p2")
    shapes = ((2, 2, 4, 4, 48, FF_DEV), (2, 4, 128, D))

    def bind(self, ins, outs, scratch):
        self.p1, self.p2 = ins
        self.w1, self.w2 = outs

    def stages(self):
        return [self.sides_begin, self.sides_second, self.sides_finish]

    def quarter(self, half, far):
        return self.w1.at[half, :, pl.ds(2 * far, 2)]

    def corner(self, half, far, zs):
        return self.w2.at[far, zs, :, columns(half * 384, 384)]

    def sides_begin(self):
        n = self.net
        own, corner = self.quarter(n.half, n.far), self.corner(n.half, n.far, pl.ds(0, 4))
        self.across = [n.copy(self.p1, own, rep=n.partner), n.copy(self.p2, corner, rep=n.partner)]
        self.along = [n.copy(self.p1, own, seq=n.seq(2)), n.copy(self.p2, corner, seq=n.seq(2))]
        self.kept = [n.move(self.p1, own), n.move(self.p2, corner)]

    def sides_second(self):
        n = self.net
        wait_all(self.along)
        part = self.w1.at[n.half, 0, pl.ds(2 * (1 - n.far), 2)]
        corner = self.corner(n.half, 1 - n.far, pl.ds(0, 2))
        self.along = [n.copy(part, part, rep=n.partner), n.copy(corner, corner, rep=n.partner)]
        wait_all(self.across)
        part = self.w1.at[1 - n.half, 1, pl.ds(2 * n.far, 2)]
        corner = self.corner(1 - n.half, n.far, pl.ds(2, 2))
        self.across = [n.copy(part, part, seq=n.seq(2)), n.copy(corner, corner, seq=n.seq(2))]

    def sides_finish(self):
        wait_all(self.across + self.along + self.kept)


class ExpertFetch(ExpertPlane, ExpertSides):
    inputs = ExpertPlane.inputs
    shapes = ExpertSides.shapes
    scratch = ExpertPlane.shapes

    def bind(self, ins, outs, scratch):
        ExpertPlane.bind(self, ins, scratch, ())
        ExpertSides.bind(self, scratch, outs, ())

    def stages(self):
        def turn_over():
            self.plane_finish()
            self.sides_begin()

        return [self.plane_begin, turn_over, self.sides_second, self.sides_finish]


class SharedFetch(Job):
    inputs = ("shared_in", "shared_out")
    shapes = ((2, 4, 4, 48, FF_DEV), (4, 128, D))

    def bind(self, ins, outs, scratch):
        self.first, self.second = ins
        self.w_in, self.w_out = outs

    def stages(self):
        return [self.begin, self.second_hop, self.third_hop, self.finish]

    def begin(self):
        n = self.net
        self.firsts, self.seconds = [], []
        for d in (3, 2, 1, 0):
            src = self.first.at[self.layer, :, columns(n.half * FF + n.seq(d) * FF_DEV, FF_DEV)]
            dst = self.w_in.at[n.half, n.s, n.z]
            self.firsts.append(n.move(src, dst) if d == 0 else n.copy(src, dst, seq=n.seq(d)))
        for k in (2, 1, 3, 0):
            src = self.second.at[self.layer, :, columns(n.half * 384, 384)]
            dst = self.w_out.at[n.z, :, columns(n.half * 384, 384)]
            self.seconds.append(n.move(src, dst) if k == 0 else n.copy(src, dst, fsdp=n.plane(k)))

    def second_hop(self):
        n = self.net
        wait_all(self.firsts)
        part = self.w_in.at[n.half, :, n.z]
        self.firsts = [n.copy(part, part, fsdp=n.plane(k)) for k in (2, 1, 3)]
        self.across = [n.copy(part, part, rep=n.partner)]
        wait_all(self.seconds)
        part = self.w_out.at[:, :, columns(n.half * 384, 384)]
        self.across.append(n.copy(part, part, rep=n.partner))

    def third_hop(self):
        n = self.net
        for copy, k in zip(self.firsts[1:] + self.firsts[:1], (1, 3, 2)):
            copy.wait()
            part = self.w_in.at[n.half, :, n.plane(FSDP - k)]
            self.across.append(n.copy(part, part, rep=n.partner))

    def finish(self):
        wait_all(self.across)


class AttnFetch(Job):
    inputs = ("attn_qkv", "attn_out")
    shapes = ((4, 4, 48, 3 * COLS), (4, 48, D))

    def bind(self, ins, outs, scratch):
        self.qkv, self.out = ins
        self.w_qkv, self.w_out = outs

    def stages(self):
        return [self.begin, self.second_hop, self.third_hop, self.finish]

    def begin(self):
        n = self.net
        self.firsts, self.seconds = [], []
        for d in (3, 2, 1, 0):
            src, dst = self.qkv.at[self.layer, n.seq(d)], self.w_qkv.at[n.s, n.z]
            self.firsts.append(n.move(src, dst) if d == 0 else n.copy(src, dst, seq=n.seq(d)))
        for k in (2, 1, 3, 0):
            src = self.out.at[self.layer, :, columns(n.half * 384, 384)]
            dst = self.w_out.at[n.z, :, columns(n.half * 384, 384)]
            self.seconds.append(n.move(src, dst) if k == 0 else n.copy(src, dst, fsdp=n.plane(k)))

    def second_hop(self):
        n = self.net
        wait_all(self.firsts)
        part = self.w_qkv.at[pl.ds(2 * n.half, 2), n.z]
        self.firsts = [n.copy(part, part, fsdp=n.plane(k)) for k in (2, 1, 3)]
        wait_all(self.seconds)
        part = self.w_out.at[:, :, columns(n.half * 384, 384)]
        self.across = [n.copy(part, part, rep=n.partner)]

    def third_hop(self):
        n = self.net
        for copy, k in zip(self.firsts[1:] + self.firsts[:1], (1, 3, 2)):
            copy.wait()
            part = self.w_qkv.at[pl.ds(2 * n.half, 2), n.plane(FSDP - k)]
            self.across.append(n.copy(part, part, rep=n.partner))

    def finish(self):
        wait_all(self.across)


class AttnFetchHere(AttnFetch):
    out_space = pltpu.VMEM


class SmallFetch(Job):
    inputs = ("small",)
    shapes = ((4, 4, 16, 128),)

    def bind(self, ins, outs, scratch):
        (self.src,), (self.dst,) = ins, outs

    def stages(self):
        return [self.begin, self.second_hop, self.finish]

    def begin(self):
        n = self.net
        dst = self.dst.at[n.s, n.z]
        self.copies = [n.copy(self.src, dst, seq=n.seq(d)) for d in (3, 2, 1)]
        self.copies.append(n.move(self.src, dst))

    def second_hop(self):
        n = self.net
        wait_all(self.copies)
        part = self.dst.at[:, n.z]
        self.copies = [n.copy(part, part, fsdp=n.plane(k)) for k in (2, 1, 3)]

    def finish(self):
        wait_all(self.copies)


def total(*parts):
    out = parts[0].astype(f32)
    for part in parts[1:]:
        out = out + part.astype(f32)
    return out.astype(bf16)


class ExpertSidesReturn(Job):
    space = pltpu.VMEM
    out_space = pltpu.VMEM
    inputs = ("d_w1", "d_w2")
    shapes = ((2, 2, 4, 48, FF_DEV), (4, 128, 384))
    scratch = (
        (4, 4, 48, FF_DEV), (2, 2, 4, 48, FF_DEV), (2, 2, 128, 384), (2, 128, D),
    )

    def bind(self, ins, outs, scratch):
        self.d1, self.d2 = ins
        self.q1, self.q2 = outs
        self.ra, self.rb, self.rc, self.rd = scratch[:4]

    def stages(self):
        return [self.sides_begin, self.sides_second, self.sides_finish]

    def sides_begin(self):
        n = self.net
        other, half_cols = 1 - n.far, columns((1 - n.half) * 384, 384)
        self.across = [
            n.copy(self.d1.at[1 - n.half, 0], self.ra, rep=n.partner),
            n.copy(self.d2.at[:, pl.ds(0, 2), :, half_cols], self.rc, rep=n.partner),
        ]
        self.along = [
            n.copy(self.d1.at[:, 1, pl.ds(2 * other, 2)], self.rb, seq=n.seq(2)),
            n.copy(self.d2.at[other, pl.ds(2, 2)], self.rd, seq=n.seq(2)),
        ]

    def sides_second(self):
        n = self.net
        other, far = 1 - n.far, n.far
        wait_all(self.along)
        rows = pl.ds(2 * far, 2)
        self.rb[1 - n.half] = total(self.rb[1 - n.half], self.d1[1 - n.half, 1, rows])
        mine, rest = columns(n.half * 384, 384), columns((1 - n.half) * 384, 384)
        self.rd[...] = total(self.rd[...], self.d2[far, pl.ds(2, 2)])
        self.along = [
            n.copy(self.rb.at[1 - n.half], self.q1.at[1], rep=n.partner),
            n.copy(self.rd.at[:, :, rest], self.q2.at[pl.ds(2, 2)], rep=n.partner),
        ]
        wait_all(self.across)
        rows = pl.ds(2 * other, 2)
        self.ra[rows] = total(self.ra[rows], self.d1[n.half, 0, rows])
        self.rc[other] = total(self.rc[other], self.d2[other, pl.ds(0, 2), :, mine])
        self.across = [
            n.copy(self.ra.at[rows], self.q1.at[0], seq=n.seq(2)),
            n.copy(self.rc.at[other], self.q2.at[pl.ds(0, 2)], seq=n.seq(2)),
        ]
        rows = pl.ds(2 * far, 2)
        self.rb[n.half] = total(self.rb[n.half], self.d1[n.half, 1, rows])
        self.ra[rows] = total(self.ra[rows], self.d1[n.half, 0, rows])
        self.rc[far] = total(self.rc[far], self.d2[far, pl.ds(0, 2), :, mine])

    def sides_finish(self):
        n = self.net
        wait_all(self.across + self.along)
        self.q1[0] = total(self.q1[0], self.ra[pl.ds(2 * n.far, 2)])
        self.q1[1] = total(self.q1[1], self.rb[n.half])
        self.q2[0:2] = total(self.q2[0:2], self.rc[n.far])
        self.q2[2:4] = total(self.q2[2:4], self.rd[:, :, columns(n.half * 384, 384)])


class ExpertPlaneReturn(Job):
    space = pltpu.VMEM
    inputs = ("q1", "q2")
    shapes = ((EXPERTS, 48, 2 * FF), (EXPERTS, 128, D))

    def bind(self, ins, outs, scratch):
        self.q1, self.q2 = ins
        self.o1, self.o2 = outs

    def stages(self):
        return [self.plane_begin, self.plane_second, self.plane_finish]

    def plane_begin(self):
        n = self.net
        self.firsts, self.seconds = [], []
        for k in (2, 1, 3, 0):
            for d in (1, 0):
                core = n.core if d == 0 else 1 - n.core
                for gu in (0, 1):
                    src = self.q1.at[gu, core, n.plane(k)]
                    dst = self.o1.at[
                        n.z, :, columns(gu * FF + n.half * FF_CORE + n.core * FF_DEV, FF_DEV)
                    ]
                    if k == 0 and d == 0:
                        self.firsts.append(n.move(src, dst))
                    else:
                        self.firsts.append(n.copy(src, dst, seq=n.seq(d), fsdp=n.plane(k)))
            src = self.q2.at[n.plane(k)]
            dst = self.o2.at[n.z, :, columns(n.half * 384, 384)]
            self.seconds.append(n.move(src, dst) if k == 0 else n.copy(src, dst, fsdp=n.plane(k)))

    def plane_second(self):
        n = self.net
        wait_all(self.seconds)
        part = self.o2.at[:, :, columns(n.half * 384, 384)]
        self.seconds = [n.copy(part, part, rep=n.partner)]
        wait_all(self.firsts)
        self.firsts = []
        for gu in (0, 1):
            part = self.o1.at[:, :, columns(gu * FF + n.half * FF_CORE, FF_CORE)]
            self.firsts.append(n.copy(part, part, rep=n.partner))

    def plane_finish(self):
        wait_all(self.firsts + self.seconds)


class ExpertReturn(ExpertSidesReturn, ExpertPlaneReturn):
    out_space = pl.ANY
    inputs = ExpertSidesReturn.inputs
    shapes = ExpertPlaneReturn.shapes
    scratch = ExpertSidesReturn.scratch + ExpertSidesReturn.shapes

    def bind(self, ins, outs, scratch):
        ExpertSidesReturn.bind(self, ins, scratch[4:], scratch[:4])
        ExpertPlaneReturn.bind(self, scratch[4:], outs, ())

    def stages(self):
        def turn_over():
            self.sides_finish()
            self.plane_begin()

        return [
            self.sides_begin, self.sides_second, turn_over, self.plane_second, self.plane_finish,
        ]


class SharedReturn(Job):
    space = pltpu.VMEM
    inputs = ("d_w_in", "d_w_so")
    shapes = ((48, 2 * FF), (128, D))
    scratch = (
        (4, 4, 48, FF_DEV), (3, 4, 48, FF_DEV), (4, 48, FF_DEV), (4, 128, 384), (3, 128, 384),
        (128, 384),
    )

    def bind(self, ins, outs, scratch):
        self.d1, self.d2 = ins
        self.o1, self.o2 = outs
        self.r1, self.r1z, self.s1, self.r2, self.r2z, self.s2 = scratch

    def stages(self):
        return [self.begin, self.second_hop, self.third_hop, self.fourth_hop, self.finish]

    def begin(self):
        n = self.net
        self.firsts = [n.copy(self.d1.at[1 - n.half], self.r1, rep=n.partner)]
        part = self.d2.at[:, :, columns((1 - n.half) * 384, 384)]
        self.seconds = [n.copy(part, self.r2, rep=n.partner)]

    def second_hop(self):
        n = self.net
        wait_all(self.firsts)
        self.r1[...] = total(self.r1[...], self.d1[n.half])
        self.firsts = [
            n.copy(self.r1.at[:, n.plane(k)], self.r1z.at[k - 1], fsdp=n.plane(k))
            for k in (2, 1, 3)
        ]
        wait_all(self.seconds)
        self.r2[...] = total(self.r2[...], self.d2[:, :, columns(n.half * 384, 384)])
        self.seconds = [
            n.copy(self.r2.at[n.plane(k)], self.r2z.at[k - 1], fsdp=n.plane(k)) for k in (2, 1, 3)
        ]

    def third_hop(self):
        n = self.net
        wait_all(self.firsts + self.seconds)
        self.s1[...] = total(self.r1[:, n.z], self.r1z[0], self.r1z[1], self.r1z[2])
        self.firsts = []
        for d in (3, 2, 1, 0):
            src = self.s1.at[n.seq(d)]
            dst = self.o1.at[:, columns(n.half * FF + n.s * FF_DEV, FF_DEV)]
            self.firsts.append(n.move(src, dst) if d == 0 else n.copy(src, dst, seq=n.seq(d)))
        self.s2[...] = total(self.r2[n.z], self.r2z[0], self.r2z[1], self.r2z[2])
        dst = self.o2.at[:, columns(n.half * 384, 384)]
        self.seconds = [n.copy(self.s2, dst, rep=n.partner), n.move(self.s2, dst)]

    def fourth_hop(self):
        n = self.net
        wait_all(self.firsts)
        part = self.o1.at[:, columns(n.half * FF, FF)]
        self.firsts = [n.copy(part, part, rep=n.partner)]

    def finish(self):
        wait_all(self.firsts + self.seconds)


class AttnReturn(Job):
    space = pltpu.VMEM
    inputs = ("d_w_qkv", "d_w_out")
    shapes = ((4, 48, 3 * COLS), (48, D))
    scratch = (
        (2, 4, 48, 3 * COLS), (3, 2, 48, 3 * COLS), (4, 48, 3 * COLS), (4, 48, 384), (3, 48, 384),
        (48, 384),
    )

    def bind(self, ins, outs, scratch):
        self.d1, self.d2 = ins
        self.o1, self.o2 = outs
        self.r1, self.r1z, self.s1, self.r2, self.r2z, self.s2 = scratch

    def stages(self):
        return [self.begin, self.second_hop, self.third_hop, self.fourth_hop, self.finish]

    def begin(self):
        n = self.net
        self.firsts = [n.copy(self.d1.at[pl.ds(2 * (1 - n.half), 2)], self.r1, rep=n.partner)]
        part = self.d2.at[:, :, columns((1 - n.half) * 384, 384)]
        self.seconds = [n.copy(part, self.r2, rep=n.partner)]

    def second_hop(self):
        n = self.net
        wait_all(self.firsts)
        self.r1[...] = total(self.r1[...], self.d1[pl.ds(2 * n.half, 2)])
        self.firsts = [
            n.copy(self.r1.at[:, n.plane(k)], self.r1z.at[k - 1], fsdp=n.plane(k))
            for k in (2, 1, 3)
        ]
        wait_all(self.seconds)
        self.r2[...] = total(self.r2[...], self.d2[:, :, columns(n.half * 384, 384)])
        self.seconds = [
            n.copy(self.r2.at[n.plane(k)], self.r2z.at[k - 1], fsdp=n.plane(k)) for k in (2, 1, 3)
        ]

    def third_hop(self):
        n = self.net
        wait_all(self.firsts + self.seconds)
        pair = pl.ds(2 * n.half, 2)
        self.s1[pair] = total(self.r1[:, n.z], self.r1z[0], self.r1z[1], self.r1z[2])
        self.firsts = [n.copy(self.s1.at[pair], self.s1.at[pair], rep=n.partner)]
        self.s2[...] = total(self.r2[n.z], self.r2z[0], self.r2z[1], self.r2z[2])
        dst = self.o2.at[:, columns(n.half * 384, 384)]
        self.seconds = [n.copy(self.s2, dst, rep=n.partner), n.move(self.s2, dst)]

    def fourth_hop(self):
        n = self.net
        wait_all(self.firsts)
        self.firsts = []
        for d in (3, 2, 1, 0):
            src, dst = self.s1.at[n.seq(d)], self.o1.at[n.s]
            self.firsts.append(n.move(src, dst) if d == 0 else n.copy(src, dst, seq=n.seq(d)))

    def finish(self):
        wait_all(self.firsts + self.seconds)


class AttnReturnHere(AttnReturn):
    inputs = ()
    own = (2, 3)


class SmallReturnHere(Job):
    inputs = ("small_rows",)
    space = pltpu.VMEM
    out_space = pltpu.VMEM
    kind = f32
    own = (1,)
    shapes = ((16, D),)
    scratch = ((16, D), (16, D), (3, 16, D), (3, 16, D))

    def bind(self, ins, outs, scratch):
        self.rows, self.gain = ins
        (self.out,) = outs
        self.acc, self.rx, self.rz, self.rs = scratch

    def stages(self):
        return [self.begin, self.second_hop, self.third_hop, self.finish]

    def begin(self):
        n = self.net
        self.acc[...] = self.rows[...]
        self.acc[0:8] += self.gain[...]
        self.copies = [n.copy(self.acc, self.rx, rep=n.partner)]

    def second_hop(self):
        n = self.net
        wait_all(self.copies)
        self.rx[...] = self.acc[...] + self.rx[...]
        self.copies = [n.copy(self.rx, self.rz.at[k - 1], fsdp=n.plane(k)) for k in (2, 1, 3)]

    def third_hop(self):
        n = self.net
        wait_all(self.copies)
        self.acc[...] = self.rx[...] + self.rz[0] + self.rz[1] + self.rz[2]
        self.copies = [n.copy(self.acc, self.rs.at[d - 1], seq=n.seq(d)) for d in (3, 2, 1)]

    def finish(self):
        wait_all(self.copies)
        self.out[...] = self.acc[...] + self.rs[0] + self.rs[1] + self.rs[2]


class Background:
    def __init__(self, net, jobs, ins, own_outs, outs, scratch):
        self.queues, self.made = [], []
        for job, layer, points in jobs:
            a, b, c = len(job.inputs), len(job.shapes), len(job.scratch)
            given = list(ins[:a]) + [own_outs[i] for i in getattr(job, "own", ())]
            made = job(net, layer, given, outs[:b], scratch[:c])
            self.made.append((made, outs[:b]))
            stages = made.stages()
            last = points[-1]
            points = tuple(points) + (last,) * (len(stages) - len(points))
            self.queues.append(list(zip(points, stages)))
            ins, outs, scratch = ins[a:], outs[b:], scratch[c:]

    def at(self, point):
        for queue in self.queues:
            while queue and queue[0][0] <= point:
                queue.pop(0)[1]()

    def drain(self):
        while any(self.queues):
            for queue in self.queues:
                if queue:
                    queue.pop(0)[1]()


COPIES = 112


def call(kernel, inputs, outputs, scratch, jobs, shards, cid):
    given = [shards[name] for job, *_ in jobs for name in job.inputs]
    results = [
        (jax.ShapeDtypeStruct(shape, job.kind), job.out_space)
        for job, *_ in jobs
        for shape in job.shapes
    ]
    vmem = pl.BlockSpec(memory_space=pltpu.VMEM)
    job_scratch = [pltpu.VMEM(shape, job.kind) for job, *_ in jobs for shape in job.scratch]

    def body(*refs):
        a = len(inputs)
        b = a + len(given)
        c = b + len(outputs)
        d = c + len(results)
        e = d + len(scratch)
        f = e + len(job_scratch)
        net = Net(*refs[f:])
        ground = Background(net, jobs, refs[a:b], refs[b:c], refs[c:d], refs[e:f])
        kernel(net, ground, *refs[:a], *refs[b:c], *refs[d:e])

    made = pl.pallas_call(
        body,
        out_shape=[jax.ShapeDtypeStruct(shape, kind) for shape, kind in outputs]
        + [shape for shape, _ in results],
        in_specs=[vmem] * len(inputs)
        + [pl.BlockSpec(memory_space=job.space) for job, *_ in jobs for _ in job.inputs],
        out_specs=[vmem] * len(outputs) + [pl.BlockSpec(memory_space=where) for _, where in results],
        scratch_shapes=[pltpu.VMEM(shape, kind) for shape, kind in scratch]
        + job_scratch
        + [
            pltpu.SemaphoreType.DMA((COPIES,)),
            pltpu.SemaphoreType.DMA((COPIES,)),
            pltpu.SemaphoreType.DMA((32,)),
        ],
        compiler_params=pltpu.CompilerParams(
            collective_id=cid, has_side_effects=True, vmem_limit_bytes=60 << 20
        ),
        cost_estimate=pl.CostEstimate(flops=0, bytes_accessed=1 << 20, transcendentals=0),
    )(*inputs, *given)
    return made[: len(outputs)], made[len(outputs) :]


def prologue_kernel(net, ground):
    net.greet(net.everyone())
    net.met()
    ground.drain()


def rms_rows(x):
    return lax.rsqrt(jnp.mean(x * x, -1, keepdims=True) + EPS)


def turn(x, cosine, sine):
    half = HEAD_DIM // 2
    return x * cosine + jnp.concatenate([x[:, half:], x[:, :half]], 1) * sine


def attn_forward_kernel(
    here, net, ground, h, gains, cosine, sine, *refs
):
    if here:
        w_qkv, w_out = ground.made[0][1]
    else:
        w_qkv, w_out, *refs = refs
    (
        middle, second, every, queries, keys, values, attended, totals,
        near_out, near_in, away_out, away_in,
    ) = refs
    net.greet(net.everyone())
    x = h[...]
    every[net.s] = (x * rms_rows(x) * gains[0:1, :]).astype(bf16)
    net.met()
    ground.at(0)
    far = net.copy(every.at[net.s], every.at[net.s], seq=net.seq(2))
    near = net.copy(every.at[net.s], every.at[net.s], seq=net.seq(1))
    ground.at(1)

    def project(b):
        joint = dot(every[b], w_qkv[...].reshape(D, 3 * COLS))
        c, sn = cosine[b], sine[b]
        for i in range(HEADS_DEV):
            at = i * HEAD_DIM
            queries[i, b] = turn(joint[:, at : at + HEAD_DIM], c, sn).astype(bf16)
            at += COLS
            keys[i, b] = turn(joint[:, at : at + HEAD_DIM], c, sn).astype(bf16)
            at += COLS
            values[i, b] = joint[:, at : at + HEAD_DIM].astype(bf16)

    if not here:
        project(net.s)
    near.wait_recv()
    ground.at(2)
    if not here:
        project(net.seq(1))
    far.wait_recv()
    passed = net.copy(every.at[net.seq(2)], every.at[net.seq(2)], seq=net.seq(1))
    ground.at(3)
    if here:
        project(net.s)
        project(net.seq(1))
    project(net.seq(2))
    passed.wait_recv()
    project(net.seq(3))
    ground.at(4)
    tokens = h.shape[0]

    def head(i):
        for b in range(SEQ):
            size = (b + 1) * tokens
            scores = dot_nt(queries[i, b], keys[i, : b + 1].reshape(size, HEAD_DIM))
            row = lax.broadcasted_iota(jnp.int32, (tokens, size), 0) + b * tokens
            col = lax.broadcasted_iota(jnp.int32, (tokens, size), 1)
            scores = jnp.where(row >= col, scores * HEAD_DIM**-0.5, MASKED)
            top = jnp.max(scores, -1, keepdims=True)
            weights = jnp.exp(scores - top)
            total = jnp.sum(weights, -1, keepdims=True)
            weights = (weights * (1.0 / total)).astype(bf16)
            attended[i, b] = dot(weights, values[i, : b + 1].reshape(size, HEAD_DIM))
            totals[i, b] = jnp.broadcast_to(top + jnp.log(total), (tokens, 128))

    for i in range(HEADS_DEV):
        head(i)
        ground.at(5 + i)

    def part(b):
        low = jnp.concatenate([attended[i, b].astype(bf16) for i in range(HEADS_DEV)], 1)
        return dot(low, w_out[...].reshape(COLS, D))

    near_out[0] = part(net.seq(1)).astype(bf16)
    near_out[1] = part(net.seq(3)).astype(bf16)
    near_sum = net.copy(near_out, near_in, seq=net.seq(1))
    away = part(net.seq(2))
    own = part(net.s)
    near_sum.wait_recv()
    away_out[...] = (away + near_in[1].astype(f32)).astype(bf16)
    away_sum = net.copy(away_out, away_in, seq=net.seq(2))
    own = h[...] + own + near_in[0].astype(f32)
    ground.at(8)
    away_sum.wait_recv()
    own = own + away_in[...].astype(f32)
    middle[...] = own
    second[...] = (own * rms_rows(own) * gains[1:2, :]).astype(bf16)
    for copy in (far, near, passed, near_sum, away_sum):
        copy.wait_send()
    ground.drain()


def attn_forward(h, gains, weights, tables, jobs, shards, cid):
    t = h.shape[0]
    head = (HEADS_DEV, SEQ, t, HEAD_DIM)
    return call(
        functools.partial(attn_forward_kernel, not weights),
        [h, gains, *tables, *weights],
        [
            ((t, D), f32), ((t, D), bf16), ((SEQ, t, D), bf16), (head, bf16), (head, bf16),
            (head, bf16), (head, f32), ((HEADS_DEV, SEQ, t, 128), f32),
        ],
        [((2, t, D), bf16), ((2, t, D), bf16), ((t, D), bf16), ((t, D), bf16)],
        jobs, shards, cid,
    )


def silu_gate(g, u):
    return g / (1.0 + jnp.exp(-g)) * u


def ffn_forward_kernel(
    net, ground, second, middle, router, onehot, chosen, w_in, w_so, w1, w2,
    result, gates, gathered, every, joint, hidden, rows, joint_e, hidden_e,
    rows_out, prod_out, prod_in, prod_own, back_out, yields, near_out, near_in, away_out, away_in,
):
    t = second.shape[0]
    net.greet(net.everyone())
    picked = chosen[:, :t] + chosen[:, t:]
    rows_out[...] = dot(picked, second[...]).astype(bf16).reshape(EXPERTS, CAP, D)
    every[net.s] = second[...]
    net.met()
    sent = {}
    for k in (2, 1, 3):
        e = net.plane(k)
        sent[k] = net.copy(rows_out.at[e], rows.at[net.core, net.z], fsdp=e)
    far = net.copy(every.at[net.s], every.at[net.s], seq=net.seq(2))
    near = net.copy(every.at[net.s], every.at[net.s], seq=net.seq(1))
    rows[net.core, net.z] = rows_out[net.z]
    passed = []

    def pass_rows(k):
        if k:
            sent[k].wait_recv()
        part = rows.at[net.core, net.plane(FSDP - k)]
        passed.append(net.copy(part, part, seq=net.seq(1)))

    pass_rows(0)
    ground.at(0)
    logits = dot(second[...], router[...])
    l0 = jnp.sum(onehot[0] * logits, -1, keepdims=True)
    l1 = jnp.sum(onehot[1] * logits, -1, keepdims=True)
    top = jnp.maximum(l0, l1)
    e0, e1 = jnp.exp(l0 - top), jnp.exp(l1 - top)
    g0, g1 = e0 / (e0 + e1), e1 / (e0 + e1)
    lane = lax.broadcasted_iota(jnp.int32, (t, 128), 1)
    gates[...] = jnp.where(lane == 0, g0, jnp.where(lane == 1, g1, 0.0))

    def shared(b):
        g, u = dot(every[b], w_in[0]), dot(every[b], w_in[1])
        joint[0, b] = g.astype(bf16)
        joint[1, b] = u.astype(bf16)
        low = silu_gate(g, u).astype(bf16)
        hidden[b] = low
        return dot(low, w_so[...])

    own_part = shared(net.s)
    ground.at(1)
    near.wait_recv()
    near_out[0] = shared(net.seq(1)).astype(bf16)
    pass_rows(1)
    pass_rows(3)
    far.wait_recv()
    passed_far = net.copy(every.at[net.seq(2)], every.at[net.seq(2)], seq=net.seq(1))
    far_part = shared(net.seq(2))
    pass_rows(2)
    ground.at(2)
    passed_far.wait_recv()
    near_out[1] = shared(net.seq(3)).astype(bf16)
    near_sum = net.copy(near_out, near_in, seq=net.seq(1))
    ground.at(3)

    def expert(core):
        x = rows[core].reshape(SLOTS, D)
        total = None
        for half in (0, 1):
            g, u = dot(x, w1[half, 0]), dot(x, w1[half, 1])
            joint_e[core, half, 0] = g.astype(bf16)
            joint_e[core, half, 1] = u.astype(bf16)
            low = silu_gate(g, u).astype(bf16)
            hidden_e[core, half] = low
            new = dot(low, w2[half * FF_DEV : (half + 1) * FF_DEV, :])
            total = new if total is None else total + new
        return total

    for copy in passed:
        copy.wait_recv()
    prod_out[...] = expert(1 - net.core).astype(bf16)
    prod_sum = net.copy(prod_out, prod_in, seq=net.seq(1))
    near_sum.wait_recv()
    away_out[...] = (far_part + near_in[1].astype(f32)).astype(bf16)
    away_sum = net.copy(away_out, away_in, seq=net.seq(2))
    ground.at(4)
    prod_own[...] = expert(net.core)
    ground.at(5)
    prod_sum.wait_recv()
    back_out[...] = (prod_own[...] + prod_in[...].astype(f32)).astype(bf16).reshape(EXPERTS, CAP, D)
    returned = []
    for k in (2, 1, 3):
        e = net.plane(k)
        returned.append(net.copy(back_out.at[e], yields.at[net.z], fsdp=e))
    yields[net.z] = back_out[net.z]
    ground.at(6)
    away_sum.wait_recv()
    base = middle[...] + own_part + near_in[0].astype(f32) + away_in[...].astype(f32)
    for copy in returned:
        copy.wait_recv()
    got = dot_tn(chosen[...], yields[...].reshape(SLOTS, D))
    gathered[...] = got.astype(bf16)
    result[...] = base + g0 * got[:t] + g1 * got[t:]
    for copy in [far, near, passed_far, near_sum, prod_sum, away_sum, *passed, *sent.values(), *returned]:
        copy.wait_send()
    ground.drain()


def ffn_forward(second, middle, router, onehot, chosen, w_in, w_so, w1, w2, jobs, shards, cid):
    t = second.shape[0]
    return call(
        ffn_forward_kernel,
        [second, middle, router, onehot, chosen, w_in, w_so, w1, w2],
        [
            ((t, D), f32), ((t, 128), f32), ((2 * t, D), bf16), ((SEQ, t, D), bf16),
            ((2, SEQ, t, FF_DEV), bf16), ((SEQ, t, FF_DEV), bf16), ((2, EXPERTS, CAP, D), bf16),
            ((2, 2, 2, SLOTS, FF_DEV), bf16), ((2, 2, SLOTS, FF_DEV), bf16),
        ],
        [
            ((EXPERTS, CAP, D), bf16), ((SLOTS, D), bf16), ((SLOTS, D), bf16), ((SLOTS, D), f32),
            ((EXPERTS, CAP, D), bf16), ((EXPERTS, CAP, D), bf16), ((2, t, D), bf16),
            ((2, t, D), bf16), ((t, D), bf16), ((t, D), bf16),
        ],
        jobs, shards, cid,
    )


def norm_back(x, gain, gradient):
    factor = rms_rows(x)
    weighted = gradient * gain
    inner = jnp.mean(weighted * x, -1, keepdims=True)
    d_x = factor * weighted - x * (factor * factor * factor) * inner
    return d_x, jnp.sum(gradient * x * factor, 0, keepdims=True)


def gate_back(g, u, gradient):
    sig = 1.0 / (1.0 + jnp.exp(-g))
    d_g = gradient * u * sig * (1.0 + g * (1.0 - sig))
    return d_g.astype(bf16), (gradient * g * sig).astype(bf16)


def ffn_backward_kernel(
    net, ground, grad, gates, onehot, chosen, gathered, middle, second, gains, router, every,
    joint, hidden, rows, joint_e, hidden_e, w_in, w_so, w1, w2,
    d_middle, small, d_w1, d_w2, d_w_in, d_w_so,
    every_g, d_joint, rows_out, d_rows, d_joint_e, prod_out, prod_in, prod_own, back_out, back_in,
    near_out, near_in, away_out, away_in,
):
    t = grad.shape[0]
    net.greet(net.everyone())
    g0, g1 = gates[:, 0:1], gates[:, 1:2]
    up = grad[...]
    pairs = jnp.concatenate([(up * g0).astype(bf16), (up * g1).astype(bf16)], 0)
    rows_out[...] = dot(chosen[...], pairs).astype(bf16).reshape(EXPERTS, CAP, D)
    every_g[net.s] = up.astype(bf16)
    net.met()
    sent = {}
    for k in (2, 1, 3):
        e = net.plane(k)
        sent[k] = net.copy(rows_out.at[e], d_rows.at[net.core, net.z], fsdp=e)
    far = net.copy(every_g.at[net.s], every_g.at[net.s], seq=net.seq(2))
    near = net.copy(every_g.at[net.s], every_g.at[net.s], seq=net.seq(1))
    d_rows[net.core, net.z] = rows_out[net.z]
    passed = []

    def pass_rows(k):
        if k:
            sent[k].wait_recv()
        part = d_rows.at[net.core, net.plane(FSDP - k)]
        passed.append(net.copy(part, part, seq=net.seq(1)))

    pass_rows(0)
    ground.at(0)
    d0 = jnp.sum(up * gathered[:t].astype(f32), -1, keepdims=True)
    d1 = jnp.sum(up * gathered[t:].astype(f32), -1, keepdims=True)
    mean = g0 * d0 + g1 * d1
    d_logits = (g0 * (d0 - mean) * onehot[0] + g1 * (d1 - mean) * onehot[1]).astype(bf16)
    small[8:16, :] = dot_tn(d_logits, second[...])[:8]
    local = dot_nt(d_logits, router[...])

    def shared(b):
        d_hidden = dot_nt(every_g[b], w_so[...])
        d_g, d_u = gate_back(joint[0, b].astype(f32), joint[1, b].astype(f32), d_hidden)
        d_joint[0, b] = d_g
        d_joint[1, b] = d_u
        return dot_nt(d_g, w_in[0]) + dot_nt(d_u, w_in[1])

    local = local + shared(net.s)
    ground.at(1)
    near.wait_recv()
    near_out[0] = shared(net.seq(1)).astype(bf16)
    pass_rows(1)
    pass_rows(3)
    far.wait_recv()
    passed_far = net.copy(every_g.at[net.seq(2)], every_g.at[net.seq(2)], seq=net.seq(1))
    far_part = shared(net.seq(2))
    pass_rows(2)
    ground.at(2)
    passed_far.wait_recv()
    near_out[1] = shared(net.seq(3)).astype(bf16)
    near_sum = net.copy(near_out, near_in, seq=net.seq(1))
    ground.at(3)

    def expert(core):
        x = d_rows[core].reshape(SLOTS, D)
        out = None
        for half in (0, 1):
            d_hidden = dot_nt(x, w2[half * FF_DEV : (half + 1) * FF_DEV, :])
            d_g, d_u = gate_back(
                joint_e[core, half, 0].astype(f32), joint_e[core, half, 1].astype(f32), d_hidden
            )
            d_joint_e[half, 0, core] = d_g
            d_joint_e[half, 1, core] = d_u
            new = dot_nt(d_g, w1[half, 0]) + dot_nt(d_u, w1[half, 1])
            out = new if out is None else out + new
        return out

    for copy in passed:
        copy.wait_recv()
    prod_out[...] = expert(1 - net.core).astype(bf16)
    prod_sum = net.copy(prod_out, prod_in, seq=net.seq(1))
    near_sum.wait_recv()
    away_out[...] = (far_part + near_in[1].astype(f32)).astype(bf16)
    away_sum = net.copy(away_out, away_in, seq=net.seq(2))
    ground.at(4)
    prod_own[...] = expert(net.core)
    ground.at(5)
    prod_sum.wait_recv()
    back_out[...] = (prod_own[...] + prod_in[...].astype(f32)).astype(bf16).reshape(EXPERTS, CAP, D)
    returned = []
    for k in (2, 1, 3):
        e = net.plane(k)
        returned.append(net.copy(back_out.at[e], back_in.at[net.z], fsdp=e))
    back_in[net.z] = back_out[net.z]
    ground.at(6)
    rows_all = rows[...].reshape(2 * SLOTS, D)
    d_rows_all = d_rows[...].reshape(2 * SLOTS, D)
    for half in (0, 1):
        for gu in (0, 1):
            d_w1[half, gu] = dot_tn(rows_all, d_joint_e[half, gu].reshape(2 * SLOTS, FF_DEV)).astype(
                bf16
            )
        low = jnp.concatenate([hidden_e[0, half], hidden_e[1, half]], 0)
        d_w2[half] = dot_tn(low, d_rows_all).astype(bf16)
        ground.at(6 + half)
    ground.at(8)
    tokens = every[...].reshape(SEQ * t, D)
    for gu in (0, 1):
        d_w_in[gu] = dot_tn(tokens, d_joint[gu].reshape(SEQ * t, FF_DEV)).astype(bf16)
    ground.at(9)
    d_w_so[...] = dot_tn(hidden[...].reshape(SEQ * t, FF_DEV), every_g[...].reshape(SEQ * t, D)).astype(
        bf16
    )
    away_sum.wait_recv()
    for copy in returned:
        copy.wait_recv()
    picked = chosen[:, :t] + chosen[:, t:]
    d_normed = local + near_in[0].astype(f32) + away_in[...].astype(f32)
    d_normed = d_normed + dot_tn(picked, back_in[...].reshape(SLOTS, D))
    d_x, d_gain = norm_back(middle[...], gains[1:2, :], d_normed)
    d_middle[...] = up + d_x
    small[0:8, :] = jnp.broadcast_to(d_gain, (8, D))
    for copy in [far, near, passed_far, near_sum, prod_sum, away_sum, *passed, *sent.values(), *returned]:
        copy.wait_send()
    ground.drain()


def ffn_backward(grad, saved, gains, router, weights, jobs, shards, cid):
    t = grad.shape[0]
    gates, onehot, chosen, gathered, middle, second, every, joint, hidden, rows, joint_e, hidden_e = saved
    slots = (EXPERTS, CAP, D)
    return call(
        ffn_backward_kernel,
        [
            grad, gates, onehot, chosen, gathered, middle, second, gains, router, every, joint,
            hidden, rows, joint_e, hidden_e, *weights,
        ],
        [
            ((t, D), f32), ((16, D), f32), ((2, 2, D, FF_DEV), bf16), ((2, FF_DEV, D), bf16),
            ((2, D, FF_DEV), bf16), ((FF_DEV, D), bf16),
        ],
        [
            ((SEQ, t, D), bf16), ((2, SEQ, t, FF_DEV), bf16), (slots, bf16), ((2, *slots), bf16),
            ((2, 2, 2, SLOTS, FF_DEV), bf16), ((SLOTS, D), bf16), ((SLOTS, D), bf16),
            ((SLOTS, D), f32), (slots, bf16), (slots, bf16), ((2, t, D), bf16), ((2, t, D), bf16),
            ((t, D), bf16), ((t, D), bf16),
        ],
        jobs, shards, cid,
    )


def attn_backward_kernel(
    net, ground, d_middle, h, gains, every, queries, keys, values, attended, totals, w_qkv, w_out,
    cosine, sine,
    grad, d_gain, d_w_qkv, d_w_out,
    every_m, d_att, d_q, d_k, d_v, d_joint, near_out, near_in, away_out, away_in,
):
    t = h.shape[0]
    net.greet(net.everyone())
    up = d_middle[...]
    every_m[net.s] = up.astype(bf16)
    net.met()
    far = net.copy(every_m.at[net.s], every_m.at[net.s], seq=net.seq(2))
    near = net.copy(every_m.at[net.s], every_m.at[net.s], seq=net.seq(1))
    ground.at(0)

    def project(b):
        d = dot_nt(every_m[b], w_out[...].reshape(COLS, D)).astype(bf16)
        for i in range(HEADS_DEV):
            d_att[i, b] = d[:, i * HEAD_DIM : (i + 1) * HEAD_DIM]

    project(net.s)
    near.wait_recv()
    project(net.seq(1))
    far.wait_recv()
    passed = net.copy(every_m.at[net.seq(2)], every_m.at[net.seq(2)], seq=net.seq(1))
    project(net.seq(2))
    passed.wait_recv()
    project(net.seq(3))
    ground.at(1)
    tokens = every_m[...].reshape(SEQ * t, D)
    low = jnp.concatenate(
        [attended[i].reshape(SEQ * t, HEAD_DIM).astype(bf16) for i in range(HEADS_DEV)], 1
    )
    d_w_out[...] = dot_tn(low, tokens).astype(bf16).reshape(SEQ, 48, D)
    scale = HEAD_DIM**-0.5

    def head(i):
        d_k[i] = jnp.zeros_like(d_k[i])
        d_v[i] = jnp.zeros_like(d_v[i])
        for b in range(SEQ):
            size = (b + 1) * t
            q, d = queries[i, b], d_att[i, b]
            k = keys[i, : b + 1].reshape(size, HEAD_DIM)
            v = values[i, : b + 1].reshape(size, HEAD_DIM)
            delta = jnp.sum(d.astype(f32) * attended[i, b], -1, keepdims=True)
            row = lax.broadcasted_iota(jnp.int32, (t, size), 0) + b * t
            col = lax.broadcasted_iota(jnp.int32, (t, size), 1)
            scores = jnp.where(row >= col, dot_nt(q, k) * scale, MASKED)
            weights = jnp.exp(scores - totals[i, b][:, 0:1])
            d_scores = (weights * (dot_nt(d, v) - delta)).astype(bf16)
            d_q[i, b] = dot(d_scores, k) * scale
            shape = (b + 1, t, HEAD_DIM)
            d_k[i, : b + 1] += (dot_tn(d_scores, q) * scale).reshape(shape)
            d_v[i, : b + 1] += dot_tn(weights.astype(bf16), d).reshape(shape)

    for i in range(HEADS_DEV):
        head(i)
        ground.at(2 + i)

    def part(b):
        c, sn = cosine[b], -sine[b]
        pieces = [turn(d_q[i, b], c, sn) for i in range(HEADS_DEV)]
        pieces += [turn(d_k[i, b], c, sn) for i in range(HEADS_DEV)]
        pieces += [d_v[i, b] for i in range(HEADS_DEV)]
        d = jnp.concatenate(pieces, 1).astype(bf16)
        d_joint[b] = d
        return dot_nt(d, w_qkv[...].reshape(D, 3 * COLS))

    near_out[0] = part(net.seq(1)).astype(bf16)
    near_out[1] = part(net.seq(3)).astype(bf16)
    near_sum = net.copy(near_out, near_in, seq=net.seq(1))
    away = part(net.seq(2))
    own = part(net.s)
    near_sum.wait_recv()
    away_out[...] = (away + near_in[1].astype(f32)).astype(bf16)
    away_sum = net.copy(away_out, away_in, seq=net.seq(2))
    own = own + near_in[0].astype(f32)
    ground.at(5)
    d_w = dot_tn(every[...].reshape(SEQ * t, D), d_joint[...].reshape(SEQ * t, 3 * COLS))
    d_w_qkv[...] = d_w.astype(bf16).reshape(4, 4, 48, 3 * COLS)
    ground.at(6)
    away_sum.wait_recv()
    d_x, gain = norm_back(h[...], gains[0:1, :], own + away_in[...].astype(f32))
    grad[...] = up + d_x
    row = lax.broadcasted_iota(jnp.int32, (8, D), 0)
    d_gain[...] = jnp.where(row == 0, gain, 0.0)
    ground.at(7)
    for copy in (far, near, passed, near_sum, away_sum):
        copy.wait_send()
    ground.drain()


def attn_backward(d_middle, saved, gains, weights, tables, jobs, shards, cid):
    t = d_middle.shape[0]
    h, every, queries, keys, values, attended, totals = saved
    head = (HEADS_DEV, SEQ, t, HEAD_DIM)
    return call(
        attn_backward_kernel,
        [d_middle, h, gains, every, queries, keys, values, attended, totals, *weights, *tables],
        [((t, D), f32), ((8, D), f32), ((4, 4, 48, 3 * COLS), bf16), ((4, 48, D), bf16)],
        [
            ((SEQ, t, D), bf16), (head, bf16), (head, f32), (head, f32), (head, f32),
            ((SEQ, t, 3 * COLS), bf16), ((2, t, D), bf16), ((2, t, D), bf16), ((t, D), bf16),
            ((t, D), bf16),
        ],
        jobs, shards, cid,
    )


FORWARD_ATTN_FIRST = (
    (AttnFetchHere, 0, (0, 1, 3, 3)),
    (ExpertFetch, 0, (1, 4, 6, 9)),
    (SharedFetch, 0, (2, 4, 7, 9)),
    (AttnFetch, 1, (4, 7, 8, 9)),
)
FORWARD_FFN_FIRST = ((ExpertPlane, 1, (3, 9)),)
FORWARD_ATTN = ((ExpertSides, 1, (1, 5, 9)), (SharedFetch, 1, (1, 2, 5, 9)))
BACKWARD_FFN = ((ExpertPlaneReturn, 1, (3, 6, 9)), (AttnReturn, 1, (0, 3, 6, 8, 9)))
BACKWARD_ATTN = ((ExpertSidesReturn, 1, (0, 4, 9)), (SharedReturn, 1, (0, 3, 5, 9)))
BACKWARD_ATTN_LAST = (
    (ExpertReturn, 0, (0, 3, 5, 9)),
    (SharedReturn, 0, (0, 3, 5, 9)),
    (AttnReturnHere, 0, (6, 9)),
    (SmallReturnHere, 0, (7, 9)),
)


def local(
    reps, inputs, expert_choice, pair_order, norm_gains, attn_qkv, attn_out, router, shared_in,
    shared_out, expert_in, expert_out, cotangent,
):
    r, s, z = lax.axis_index("rep"), lax.axis_index("seq"), lax.axis_index("fsdp")
    tokens = inputs.shape[1]
    position = jnp.arange(SEQ * tokens, dtype=jnp.int32)
    half = HEAD_DIM // 2
    inverse = jnp.exp(-jnp.log(10000.0) * jnp.arange(half, dtype=f32) * 2.0 / HEAD_DIM)
    angle = position.astype(f32)[:, None] * inverse[None, :]
    cosine, sine = jnp.cos(angle)[:, None, :], jnp.sin(angle)[:, None, :]
    table_cos = jnp.concatenate([cosine, cosine], -1).reshape(SEQ, tokens, HEAD_DIM)
    table_sin = jnp.concatenate([-sine, sine], -1).reshape(SEQ, tokens, HEAD_DIM)
    small = jnp.concatenate([norm_gains, router.transpose(0, 2, 1)], 1).reshape(12, 48)
    shards = {
        "small": jnp.pad(small, ((0, 4), (0, 80))),
        "attn_qkv": attn_qkv.reshape(LAYERS, 48, 3, SEQ, COLS)
        .transpose(0, 3, 1, 2, 4)
        .reshape(LAYERS, SEQ, 48, 3 * COLS),
        "attn_out": attn_out,
        "shared_in": shared_in,
        "shared_out": shared_out,
        "expert_in": expert_in,
        "expert_out": expert_out,
    }
    h = inputs[0].astype(f32)
    kept_layers = []
    _, (small,) = call(prologue_kernel, [], [], [], [(SmallFetch, 0, (0,))], shards, 11)
    small = small.reshape(16, 16, 128)[:, :12, :48].transpose(1, 0, 2).reshape(LAYERS, 6, D)
    gains = small[:, :2].astype(f32)
    routers = small[:, 2:].transpose(0, 2, 1)
    tables = (table_cos, table_sin)
    attn = ()
    for layer in range(LAYERS):
        first = layer == 0
        routes = routing(expert_choice[layer, 0], pair_order[layer, 0, 0])
        onehot = expert_choice[layer, 0].T[..., None] == jnp.arange(128, dtype=jnp.int32)
        onehot = onehot.astype(f32)
        if first:
            jobs = FORWARD_ATTN_FIRST
        else:
            jobs = FORWARD_ATTN
        (middle, second, every_one, queries, keys, values, attended, totals), fetched = attn_forward(
            h, gains[layer], attn, tables, jobs, shards, 12 + layer
        )
        if first:
            attn, fetched, next_attn = fetched[:2], fetched[2:6], fetched[6:]
        w_qkv, w_out = attn
        w1, w2 = fetched[0].reshape(2, 2, D, FF_DEV), fetched[1].reshape(FF_CORE, D)
        w_in, w_so = fetched[2].reshape(2, D, FF_DEV), fetched[3].reshape(FF_DEV, D)
        router_pad = jnp.pad(routers[layer], ((0, 0), (0, 124)))
        outs, fetched = ffn_forward(
            second, middle, router_pad, onehot, routes[1], w_in, w_so, w1, w2,
            FORWARD_FFN_FIRST if first else (), shards, 14 + layer,
        )
        attn_weights, ffn_weights = attn, (w_in, w_so, w1, w2)
        if first:
            attn = next_attn
            shards["p1"], shards["p2"] = fetched
        result, gates, gathered, every_two, joint, hidden, rows, joint_e, hidden_e = outs
        attn_saved = (h, every_one, queries, keys, values, attended, totals)
        ffn_saved = (
            gates, onehot, routes[1], gathered, middle, second, every_two, joint, hidden, rows,
            joint_e, hidden_e,
        )
        h = result
        kept_layers.append((attn_weights, ffn_weights, attn_saved, ffn_saved, router_pad))
    output = h.astype(bf16)[None]
    grad = cotangent[0].astype(f32)
    smalls = [None] * LAYERS
    returned = {}
    grads = {}
    for layer in reversed(range(LAYERS)):
        last = layer == 0
        attn_weights, ffn_weights, attn_saved, ffn_saved, router_pad = kept_layers[layer]
        (d_middle, small, d_w1, d_w2, d_w_in, d_w_so), done = ffn_backward(
            grad, ffn_saved, gains[layer], router_pad, ffn_weights, BACKWARD_FFN if last else (),
            grads, 18 + layer,
        )
        if last:
            returned["d_expert", 1], returned["d_attn", 1] = done[:2], done[2:]
        grads["d_w1"] = d_w1.reshape(2, 2, 4, 4, 48, FF_DEV)
        grads["d_w2"] = d_w2.reshape(2, 4, 128, D)
        grads["d_w_in"] = d_w_in.reshape(2, 4, 4, 48, FF_DEV)
        grads["d_w_so"] = d_w_so.reshape(4, 128, D)
        smalls[layer] = jnp.concatenate([small[:1], small[8:12]], 0)
        if last:
            rows = jnp.concatenate([jnp.zeros((1, D), f32), smalls[0], d_gain[:1], smalls[1]], 0)
            grads["small_rows"] = jnp.pad(rows, ((0, 4), (0, 0)))
        (grad, d_gain, d_w_qkv, d_w_out), done = attn_backward(
            d_middle, attn_saved, gains[layer], attn_weights, tables,
            BACKWARD_ATTN_LAST if last else BACKWARD_ATTN, grads, 16 + layer,
        )
        if last:
            returned["d_expert", 0], returned["d_shared", 0] = done[:2], done[2:4]
            returned["d_attn", 0], total_small = done[4:6], done[6]
        else:
            grads["q1"], grads["q2"] = done[:2]
            returned["d_shared", 1] = done[2:]
            grads["d_w_qkv"], grads["d_w_out"] = d_w_qkv, d_w_out
    total_small = rep_rest(total_small, reps)[:12].reshape(LAYERS, 6, D)
    total_small = lax.dynamic_slice_in_dim(total_small, (s * FSDP + z) * 48, 48, 2)

    def stack(name, k):
        return jnp.stack([rep_rest(returned[name, i][k], reps) for i in range(LAYERS)]).astype(f32)

    d_qkv = stack("d_attn", 0).reshape(LAYERS, SEQ, 48, 3, COLS).transpose(0, 2, 3, 1, 4)
    return (
        output, grad[None], total_small[:, :2], d_qkv.reshape(LAYERS, 48, 3 * D),
        stack("d_attn", 1), total_small[:, 2:].transpose(0, 2, 1), stack("d_shared", 0),
        stack("d_shared", 1), stack("d_expert", 0), stack("d_expert", 1),
    )


def solution(mesh):
    tokens = P(("rep", "fsdp"), "seq", None)
    routes = P(None, ("rep", "fsdp"), "seq", None)
    gains = P(None, None, ("seq", "fsdp"))
    dense = P(None, ("seq", "fsdp"), None)
    expert = P(None, None, ("seq", "fsdp"), None)
    in_specs = (
        tokens, routes, routes, gains, dense, dense, dense, dense, dense, expert, expert, tokens,
    )
    out_specs = (tokens, tokens, gains, dense, dense, dense, dense, dense, expert, expert)
    return jax.shard_map(
        functools.partial(local, mesh.shape["rep"]),
        mesh=mesh, in_specs=in_specs, out_specs=out_specs, check_vma=False,
    )
```

time: 1350 us -> 872 us (0.65)
  Pallas kernels: 524 us -> 820 us
  local copies, waits for them, and re-layouts: 236 us -> 19 us
  waiting for transfers between devices: 211 us -> 0 us
  matrix products: 121 us -> 2.09 us
  other arithmetic: 129 us -> 21 us
  starting transfers between devices: 57.7 us -> 0 us
  blocking collectives: 42.6 us -> 0 us
  between operations: 16.8 us -> 1.35 us
    pallas_call x5 -> x9, Pallas kernels: 431 us -> 820 us  [call(): pl.pallas_call(body, out_shape=[jax.ShapeDtypeStruct(shape, kind) for sha...]
    ppermute x42 -> x0, waiting for transfers between devices: 173 us -> none  [the longest x8 121 us: scatter_rep(): got = lax.ppermute(other, 'rep', rep_pairs(reps))]
    pallas_call x4 -> x0, Pallas kernels: 93.1 us -> none  [exchange(): pl.pallas_call(exchange_kernel, out_shape=jax.ShapeDtypeStruct(x.shape, x...]
    convert_element_type x24 -> x0, local copies, waits for them, and re-layouts: 85.6 us -> none  [the longest x4 57.1 us: local(): joint_e.transpose(0, 3, 2, 1, 4).reshape(2 * SLOTS, -1).astype(f32)]
    dot_general x24 -> x0, matrix products: 75.1 us -> none  [the longest x14 38.3 us: dot_nt(): lax.dot_general(a, b, (((1,), (1,)), ((), ())), preferred_element_type=f32)]
    psum x1 -> x0, blocking collectives: 42.6 us -> none  [local(): total = lax.psum(jnp.stack(smalls), ('rep', 'seq', 'fsdp'))]
    dot_general x18 -> x2, matrix products: 42.8 us -> 0.67 us  [dot_tn(): lax.dot_general(a, b, (((0,), (0,)), ((), ())), preferred_element_type=f32)]
    convert_element_type x28 -> x6, other arithmetic: 50.4 us -> 8.83 us  [the longest x5 7.9 us: stack(): jnp.stack([rep_rest(returned[name, i][k], reps) for i in range(LAYERS)])]
  transfers between devices with their start and end apart: 51 -> 0, of which waited for: 18 -> 0; matrix products, arithmetic and copies ran while one was open for 31% -> 0% of each run, Pallas kernels for 5% -> 0%
where the time goes in v3:
time: 872 us; the launch traced here: 863 us
  Pallas kernels  820 us (94%)
  other arithmetic  21 us (2%)
  local copies, waits for them, and re-layouts  19 us (2%)
    pallas_call x9, Pallas kernels, call(): pl.pallas_call(body, out_shape=[jax.ShapeDtypeStruct(shape, kind) for sha...  820 us

profile of v3, /device:TPU:8, one launch (start us, length us, event | category | flops | bytes accessed | tf_op | source)
XLA Modules:
  0.0 863.0 jit_solution(15674362539895548408)
XLA Ops:
  0.6 1.9 bitcast_convert_fusion.1.refs_0_.refs_1_
  3.9 12.0 %shard_map.195 = bf16[4,4,16,128]{3,2,1,0:T(8,128)(2,1)} custom-call(bf16[16,128]{1,0:T(8,128)(2,1)} %pad.15.refs_0_), custom_call_target="tpu_custom_call" | custom-call | bytes 1048576 | tf_op jit(solution)/shard_map/pallas_call | solution.py:698
  15.9 0.9 copy.55
  17.5 1.9 fusion.12
  19.4 1.3 pad_maximum_fusion
  21.6 1.4 reshape.189.refs_4_.refs_10_
  23.0 139.3 %shard_map.196 = (f32[256,768]{1,0:T(8,128)}, bf16[256,768]{1,0:T(8,128)(2,1)}, bf16[4,256,768]{2,1,0:T(8,128)(2,1)}, bf16[3,4,256,64]{3,2,1,0:T(8,128)(2,1)}, b...) custom-call(f32[256,768]{1,0:T(8,128)} %bitcast_convert_fusion.1.ref, ...), custom_call_target="tpu_custom_call" | custom-call | bytes 1048576 | tf_op jit(solution)/shard_map/pallas_call | solution.py:698
  163.6 0.9 fusion.10.refs_3_.refs_2_
  166.0 1.0 fusion.refs_4_.refs_3_
  167.0 80.2 %shard_map.197 = (f32[256,768]{1,0:T(8,128)}, f32[256,128]{1,0:T(8,128)}, bf16[512,768]{1,0:T(8,128)(2,1)}, bf16[4,256,768]{2,1,0:T(8,128)(2,1)}, bf16[2,4,256,5...) custom-call(bf16[256,768]{1,0:T(8,128)(2,1)} %get-tuple-element.90.r, ...), custom_call_target="tpu_custom_call" | custom-call | bytes 1048576 | tf_op jit(solution)/shard_map/pallas_call | solution.py:698
  247.1 87.6 %shard_map.198 = (f32[256,768]{1,0:T(8,128)}, bf16[256,768]{1,0:T(8,128)(2,1)}, bf16[4,256,768]{2,1,0:T(8,128)(2,1)}, bf16[3,4,256,64]{3,2,1,0:T(8,128)(2,1)}, b...) custom-call(f32[256,768]{1,0:T(8,128)} %get-tuple-element.96.refs_0_, ...), custom_call_target="tpu_custom_call" | custom-call | bytes 1048576 | tf_op jit(solution)/shard_map/pallas_call | solution.py:698
  335.7 0.9 fusion.11.refs_3_.refs_2_
  338.1 1.0 fusion.1.refs_4_.refs_3_
  339.1 63.0 %shard_map.199 = (f32[256,768]{1,0:T(8,128)}, f32[256,128]{1,0:T(8,128)}, bf16[512,768]{1,0:T(8,128)(2,1)}, bf16[4,256,768]{2,1,0:T(8,128)(2,1)}, bf16[2,4,256,5...) custom-call(bf16[256,768]{1,0:T(8,128)(2,1)} %get-tuple-element.101., ...), custom_call_target="tpu_custom_call" | custom-call | bytes 1048576 | tf_op jit(solution)/shard_map/pallas_call | solution.py:698
  402.0 1.9 convert_bitcast_fusion.1
  404.0 0.9 bitcast_convert_fusion.refs_0_
  404.9 64.9 %shard_map.200 = (f32[256,768]{1,0:T(8,128)}, f32[16,768]{1,0:T(8,128)}, bf16[2,2,768,512]{3,2,1,0:T(8,128)(2,1)}, bf16[2,512,768]{2,1,0:T(8,128)(2,1)}, bf16[2,...) custom-call(f32[256,768]{1,0:T(8,128)} %bitcast_convert_fusion.refs_0_, f32[256,128]{1,0:T(8,128)} %get-tuple-element.108.refs_1_, ...), custom_call_target="tpu_custom_call" | custom-call | bytes 1048576 | tf_op jit(solution)/shard_map/pallas_call | solution.py:698
  469.8 98.7 %shard_map.201 = (f32[256,768]{1,0:T(8,128)}, f32[8,768]{1,0:T(8,128)}, bf16[4,4,48,576]{3,2,1,0:T(8,128)(2,1)}, bf16[4,48,768]{2,1,0:T(8,128)(2,1)}, bf16[2,2,4...) custom-call(f32[256,768]{1,0:T(8,128)} %get-tuple-element.116.refs_0, ...), custom_call_target="tpu_custom_call" | custom-call | bytes 1048576 | tf_op jit(solution)/shard_map/pallas_call | solution.py:698
  568.5 117.3 %shard_map.202 = (f32[256,768]{1,0:T(8,128)}, f32[16,768]{1,0:T(8,128)}, bf16[2,2,768,512]{3,2,1,0:T(8,128)(2,1)}, bf16[2,512,768]{2,1,0:T(8,128)(2,1)}, bf16[2,...) custom-call(f32[256,768]{1,0:T(8,128)} %get-tuple-element.127.refs_0, ...), custom_call_target="tpu_custom_call" | custom-call | bytes 1048576 | tf_op jit(solution)/shard_map/pallas_call | solution.py:698
  685.8 0.7 slice.74
  686.6 0.7 slice.75
  688.8 0.7 slice.78
  690.2 156.5 %shard_map.203 = (f32[256,768]{1,0:T(8,128)}, f32[8,768]{1,0:T(8,128)}, bf16[4,4,48,576]{3,2,1,0:T(8,128)(2,1)}, bf16[4,48,768]{2,1,0:T(8,128)(2,1)}, bf16[4,48,...) custom-call(f32[256,768]{1,0:T(8,128)} %get-tuple-element.140.refs_0, ...), custom_call_target="tpu_custom_call" | custom-call | bytes 1048576 | tf_op jit(solution)/shard_map/pallas_call | solution.py:698
  846.8 0.8 reshape.206
  848.4 1.1 stack.54
  850.1 0.8 copy.45
  850.9 1.7 reshape.212
  854.0 1.2 maximum_convert_fusion.2
  855.3 0.9 maximum_convert_fusion.3
  856.7 3.1 maximum_convert_fusion
  859.8 1.9 maximum_convert_fusion.1
  861.7 0.9 copy.57
  (85 shorter events, 13.5 us)
Async XLA Ops:
  19.4 1.3 copy-start.5
  162.3 1.1 copy-start.14
  162.3 2.2 copy-start.15
  339.0 64.9 %copy-start.8 = (bf16[1,256,768]{2,1,0:T(8,128)(2,1)S(1)}, bf16[1,256,768]{2,1,0:T(8,128)(2,1)}, u32[]{:S(2)}) copy-start(bf16[1,256,768]{2,1,0:T(8,128)(2,1)} %param.23) | copy-start | bytes 1179652
  690.2 158.0 %copy-start.9 = (bf16[4,48,576]{2,1,0:T(8,128)(2,1)S(1)}, bf16[4,48,576]{2,1,0:T(8,128)(2,1)}, u32[]{:S(2)}) copy-start(bf16[4,48,576]{2,1,0:T(8,128)(2,1)} %get-tuple-element.159) | copy-start | bytes 663556
  850.9 1.7 copy-start.12
  850.9 1.7 copy-start.13
  850.9 3.1 copy-start.6
  850.9 3.1 copy-start.7
  852.6 2.7 copy-start.10
  852.6 2.7 copy-start.11
  854.0 2.2 copy-start
  854.0 2.7 copy-start.1
  856.7 3.1 copy-start.2
  856.7 3.1 copy-start.3
  859.8 1.9 copy-start.4

commit v4 on v3

--- a/solution.py
+++ b/solution.py
@@ -102,6 +102,14 @@
         out.start()
         return out
 
+    def need(self, *refs):
+        for ref in refs:
+            self.coming.pop(id(ref)).wait()
+
+    def done(self, *refs):
+        for ref in refs:
+            self.going.append(self.move(ref, self.there.pop(id(ref))))
+
     def greet(self, devices):
         self.barrier = pltpu.get_barrier_semaphore()
         for device in devices:
@@ -173,60 +181,85 @@
         wait_all(self.copies)
 
 
-class ExpertSides(Job):
-    inputs = ("p1", "p2")
-    shapes = ((2, 2, 4, 4, 48, FF_DEV), (2, 4, 128, D))
+class ExpertFetch(ExpertPlane):
+    shapes = ExpertPlane.shapes + ((2, 2, 4, 48, FF_DEV), (2, 2, 4, 48, FF_DEV)) + (
+        (4, 128, 384), (4, 128, 384),
+    )
 
     def bind(self, ins, outs, scratch):
-        self.p1, self.p2 = ins
-        self.w1, self.w2 = outs
-
-    def stages(self):
-        return [self.sides_begin, self.sides_second, self.sides_finish]
-
-    def quarter(self, half, far):
-        return self.w1.at[half, :, pl.ds(2 * far, 2)]
-
-    def corner(self, half, far, zs):
-        return self.w2.at[far, zs, :, columns(half * 384, 384)]
-
-    def sides_begin(self):
-        n = self.net
-        own, corner = self.quarter(n.half, n.far), self.corner(n.half, n.far, pl.ds(0, 4))
-        self.across = [n.copy(self.p1, own, rep=n.partner), n.copy(self.p2, corner, rep=n.partner)]
-        self.along = [n.copy(self.p1, own, seq=n.seq(2)), n.copy(self.p2, corner, seq=n.seq(2))]
-        self.kept = [n.move(self.p1, own), n.move(self.p2, corner)]
-
-    def sides_second(self):
-        n = self.net
-        wait_all(self.along)
-        part = self.w1.at[n.half, 0, pl.ds(2 * (1 - n.far), 2)]
-        corner = self.corner(n.half, 1 - n.far, pl.ds(0, 2))
-        self.along = [n.copy(part, part, rep=n.partner), n.copy(corner, corner, rep=n.partner)]
-        wait_all(self.across)
-        part = self.w1.at[1 - n.half, 1, pl.ds(2 * n.far, 2)]
-        corner = self.corner(1 - n.half, n.far, pl.ds(2, 2))
-        self.across = [n.copy(part, part, seq=n.seq(2)), n.copy(corner, corner, seq=n.seq(2))]
-
-    def sides_finish(self):
-        wait_all(self.across + self.along + self.kept)
-
-
-class ExpertFetch(ExpertPlane, ExpertSides):
-    inputs = ExpertPlane.inputs
-    shapes = ExpertSides.shapes
-    scratch = ExpertPlane.shapes
-
-    def bind(self, ins, outs, scratch):
-        ExpertPlane.bind(self, ins, scratch, ())
-        ExpertSides.bind(self, scratch, outs, ())
+        ExpertPlane.bind(self, ins, outs[:2], ())
+        self.ax, self.ay, self.bx, self.by = outs[2:]
 
     def stages(self):
         def turn_over():
             self.plane_finish()
-            self.sides_begin()
-
-        return [self.plane_begin, turn_over, self.sides_second, self.sides_finish]
+            self.near_begin()
+
+        return [self.plane_begin, turn_over, self.near_finish]
+
+    def near_begin(self):
+        n = self.net
+        self.sides = [
+            n.copy(self.p1, self.ax, rep=n.partner), n.copy(self.p1, self.ay, seq=n.seq(2)),
+            n.copy(self.p2, self.bx, rep=n.partner), n.copy(self.p2, self.by, seq=n.seq(2)),
+        ]
+
+    def near_finish(self):
+        wait_all(self.sides)
+
+
+class ExpertNear(ExpertFetch):
+    inputs = ("p1", "p2")
+    shapes = ExpertFetch.shapes[2:]
+
+    def bind(self, ins, outs, scratch):
+        self.p1, self.p2 = ins
+        self.ax, self.ay, self.bx, self.by = outs
+
+    def stages(self):
+        return [self.near_begin, self.near_finish]
+
+
+class ExpertJoin(Job):
+    inputs = ("p1", "p2", "ax", "ay", "bx", "by")
+    shapes = ((2, 2, 4, 4, 48, FF_DEV), (2, 4, 128, D))
+    scratch = shapes
+
+    def bind(self, ins, outs, scratch):
+        self.p1, self.p2, self.ax, self.ay, self.bx, self.by = ins
+        self.outs = outs
+        self.w1, self.w2 = scratch
+
+    def stages(self):
+        return [self.begin, self.finish, self.written]
+
+    def begin(self):
+        n = self.net
+        here, there = pl.ds(2 * n.far, 2), pl.ds(2 * (1 - n.far), 2)
+        mine, rest = columns(n.half * 384, 384), columns((1 - n.half) * 384, 384)
+        low, high = pl.ds(0, 2), pl.ds(2, 2)
+        w1, w2 = self.w1, self.w2
+        self.copies = [
+            n.copy(self.ay.at[0], w1.at[n.half, 0, there], rep=n.partner),
+            n.copy(self.ax.at[1], w1.at[1 - n.half, 1, here], seq=n.seq(2)),
+            n.copy(self.by.at[low], w2.at[1 - n.far, low, :, mine], rep=n.partner),
+            n.copy(self.bx.at[high], w2.at[n.far, high, :, rest], seq=n.seq(2)),
+            n.move(self.p1, w1.at[n.half, :, here]),
+            n.move(self.ax, w1.at[1 - n.half, :, here]),
+            n.move(self.ay, w1.at[n.half, :, there]),
+            n.move(self.p2, w2.at[n.far, :, :, mine]),
+            n.move(self.bx, w2.at[n.far, :, :, rest]),
+            n.move(self.by, w2.at[1 - n.far, :, :, mine]),
+        ]
+
+    def finish(self):
+        wait_all(self.copies)
+        self.copies = [
+            self.net.move(self.w1, self.outs[0]), self.net.move(self.w2, self.outs[1])
+        ]
+
+    def written(self):
+        wait_all(self.copies)
 
 
 class SharedFetch(Job):
@@ -352,124 +385,90 @@
     return out.astype(bf16)
 
 
-class ExpertSidesReturn(Job):
-    space = pltpu.VMEM
+class FirstSides(Job):
+    inputs = ("d_w1",)
     out_space = pltpu.VMEM
-    inputs = ("d_w1", "d_w2")
-    shapes = ((2, 2, 4, 48, FF_DEV), (4, 128, 384))
-    scratch = (
-        (4, 4, 48, FF_DEV), (2, 2, 4, 48, FF_DEV), (2, 2, 128, 384), (2, 128, D),
-    )
+    shapes = ((2, 4, 48, FF_DEV),)
+    scratch = ((2, 2, 4, 48, FF_DEV), (2, 2, 4, 48, FF_DEV))
 
     def bind(self, ins, outs, scratch):
-        self.d1, self.d2 = ins
-        self.q1, self.q2 = outs
-        self.ra, self.rb, self.rc, self.rd = scratch[:4]
+        (self.d,), (self.q,) = ins, outs
+        self.own, self.got = scratch
 
     def stages(self):
         return [self.sides_begin, self.sides_second, self.sides_finish]
 
     def sides_begin(self):
         n = self.net
-        other, half_cols = 1 - n.far, columns((1 - n.half) * 384, 384)
-        self.across = [
-            n.copy(self.d1.at[1 - n.half, 0], self.ra, rep=n.partner),
-            n.copy(self.d2.at[:, pl.ds(0, 2), :, half_cols], self.rc, rep=n.partner),
-        ]
-        self.along = [
-            n.copy(self.d1.at[:, 1, pl.ds(2 * other, 2)], self.rb, seq=n.seq(2)),
-            n.copy(self.d2.at[other, pl.ds(2, 2)], self.rd, seq=n.seq(2)),
-        ]
+        if self.gu == 0:
+            src = [self.d.at[1 - n.half, 0, pl.ds(2 * f, 2)] for f in (0, 1)]
+            kept = [self.d.at[n.half, 0, pl.ds(2 * f, 2)] for f in (0, 1)]
+            device = {"rep": n.partner}
+        else:
+            src = [self.d.at[h, 1, pl.ds(2 * (1 - n.far), 2)] for h in (0, 1)]
+            kept = [self.d.at[h, 1, pl.ds(2 * n.far, 2)] for h in (0, 1)]
+            device = {"seq": n.seq(2)}
+        self.sent = [n.copy(src[i], self.got.at[i], **device) for i in (0, 1)]
+        self.sent += [n.move(kept[i], self.own.at[i]) for i in (0, 1)]
 
     def sides_second(self):
         n = self.net
-        other, far = 1 - n.far, n.far
-        wait_all(self.along)
-        rows = pl.ds(2 * far, 2)
-        self.rb[1 - n.half] = total(self.rb[1 - n.half], self.d1[1 - n.half, 1, rows])
-        mine, rest = columns(n.half * 384, 384), columns((1 - n.half) * 384, 384)
-        self.rd[...] = total(self.rd[...], self.d2[far, pl.ds(2, 2)])
-        self.along = [
-            n.copy(self.rb.at[1 - n.half], self.q1.at[1], rep=n.partner),
-            n.copy(self.rd.at[:, :, rest], self.q2.at[pl.ds(2, 2)], rep=n.partner),
-        ]
-        wait_all(self.across)
-        rows = pl.ds(2 * other, 2)
-        self.ra[rows] = total(self.ra[rows], self.d1[n.half, 0, rows])
-        self.rc[other] = total(self.rc[other], self.d2[other, pl.ds(0, 2), :, mine])
-        self.across = [
-            n.copy(self.ra.at[rows], self.q1.at[0], seq=n.seq(2)),
-            n.copy(self.rc.at[other], self.q2.at[pl.ds(0, 2)], seq=n.seq(2)),
-        ]
-        rows = pl.ds(2 * far, 2)
-        self.rb[n.half] = total(self.rb[n.half], self.d1[n.half, 1, rows])
-        self.ra[rows] = total(self.ra[rows], self.d1[n.half, 0, rows])
-        self.rc[far] = total(self.rc[far], self.d2[far, pl.ds(0, 2), :, mine])
+        wait_all(self.sent)
+        stays = n.far if self.gu == 0 else n.half
+        device = {"seq": n.seq(2)} if self.gu == 0 else {"rep": n.partner}
+        goes = 1 - stays
+        self.got[goes] = total(self.got[goes], self.own[goes])
+        self.sent = [n.copy(self.got.at[goes], self.q, **device)]
+        self.got[stays] = total(self.got[stays], self.own[stays])
 
     def sides_finish(self):
         n = self.net
-        wait_all(self.across + self.along)
-        self.q1[0] = total(self.q1[0], self.ra[pl.ds(2 * n.far, 2)])
-        self.q1[1] = total(self.q1[1], self.rb[n.half])
-        self.q2[0:2] = total(self.q2[0:2], self.rc[n.far])
-        self.q2[2:4] = total(self.q2[2:4], self.rd[:, :, columns(n.half * 384, 384)])
-
-
-class ExpertPlaneReturn(Job):
+        wait_all(self.sent)
+        self.q[...] = total(self.q[...], self.got[n.far if self.gu == 0 else n.half])
+
+
+class FirstPlane(Job):
     space = pltpu.VMEM
-    inputs = ("q1", "q2")
-    shapes = ((EXPERTS, 48, 2 * FF), (EXPERTS, 128, D))
+    shapes = ((EXPERTS, 48, FF),)
 
     def bind(self, ins, outs, scratch):
-        self.q1, self.q2 = ins
-        self.o1, self.o2 = outs
+        (self.q,), (self.o,) = ins, outs
 
     def stages(self):
         return [self.plane_begin, self.plane_second, self.plane_finish]
 
     def plane_begin(self):
         n = self.net
-        self.firsts, self.seconds = [], []
+        self.sent = []
+        dst = self.o.at[n.z, :, columns(n.half * FF_CORE + n.core * FF_DEV, FF_DEV)]
         for k in (2, 1, 3, 0):
             for d in (1, 0):
                 core = n.core if d == 0 else 1 - n.core
-                for gu in (0, 1):
-                    src = self.q1.at[gu, core, n.plane(k)]
-                    dst = self.o1.at[
-                        n.z, :, columns(gu * FF + n.half * FF_CORE + n.core * FF_DEV, FF_DEV)
-                    ]
-                    if k == 0 and d == 0:
-                        self.firsts.append(n.move(src, dst))
-                    else:
-                        self.firsts.append(n.copy(src, dst, seq=n.seq(d), fsdp=n.plane(k)))
-            src = self.q2.at[n.plane(k)]
-            dst = self.o2.at[n.z, :, columns(n.half * 384, 384)]
-            self.seconds.append(n.move(src, dst) if k == 0 else n.copy(src, dst, fsdp=n.plane(k)))
+                src = self.q.at[core, n.plane(k)]
+                if k == 0 and d == 0:
+                    self.sent.append(n.move(src, dst))
+                else:
+                    self.sent.append(n.copy(src, dst, seq=n.seq(d), fsdp=n.plane(k)))
 
     def plane_second(self):
         n = self.net
-        wait_all(self.seconds)
-        part = self.o2.at[:, :, columns(n.half * 384, 384)]
-        self.seconds = [n.copy(part, part, rep=n.partner)]
-        wait_all(self.firsts)
-        self.firsts = []
-        for gu in (0, 1):
-            part = self.o1.at[:, :, columns(gu * FF + n.half * FF_CORE, FF_CORE)]
-            self.firsts.append(n.copy(part, part, rep=n.partner))
+        wait_all(self.sent)
+        part = self.o.at[:, :, columns(n.half * FF_CORE, FF_CORE)]
+        self.sent = [n.copy(part, part, rep=n.partner)]
 
     def plane_finish(self):
-        wait_all(self.firsts + self.seconds)
-
-
-class ExpertReturn(ExpertSidesReturn, ExpertPlaneReturn):
+        wait_all(self.sent)
+
+
+class FirstReturn(FirstSides, FirstPlane):
+    space = pl.ANY
     out_space = pl.ANY
-    inputs = ExpertSidesReturn.inputs
-    shapes = ExpertPlaneReturn.shapes
-    scratch = ExpertSidesReturn.scratch + ExpertSidesReturn.shapes
+    shapes = FirstPlane.shapes
+    scratch = FirstSides.scratch + FirstSides.shapes
 
     def bind(self, ins, outs, scratch):
-        ExpertSidesReturn.bind(self, ins, scratch[4:], scratch[:4])
-        ExpertPlaneReturn.bind(self, scratch[4:], outs, ())
+        FirstSides.bind(self, ins, scratch[2:], scratch[:2])
+        FirstPlane.bind(self, scratch[2:], outs, ())
 
     def stages(self):
         def turn_over():
@@ -481,39 +480,154 @@
         ]
 
 
+class GateSides(FirstSides):
+    gu = 0
+
+
+class UpSides(FirstSides):
+    gu = 1
+
+
+class GatePlane(FirstPlane):
+    inputs = ("q_gate",)
+
+
+class UpPlane(FirstPlane):
+    inputs = ("q_up",)
+
+
+class GateReturn(FirstReturn):
+    gu = 0
+
+
+class UpReturn(FirstReturn):
+    gu = 1
+
+
+class SecondSides(Job):
+    inputs = ("d_w2",)
+    out_space = pltpu.VMEM
+    shapes = ((4, 128, 384),)
+    scratch = ((2, 4, 128, 384), (2, 4, 128, 384))
+
+    def bind(self, ins, outs, scratch):
+        (self.d,), (self.q,) = ins, outs
+        self.own, self.got = scratch
+
+    def stages(self):
+        return [self.sides_begin, self.sides_second, self.sides_finish]
+
+    def sides_begin(self):
+        n = self.net
+        src = self.d.at[:, :, :, columns((1 - n.half) * 384, 384)]
+        kept = self.d.at[:, :, :, columns(n.half * 384, 384)]
+        self.sent = [n.copy(src, self.got, rep=n.partner), n.move(kept, self.own)]
+
+    def sides_second(self):
+        n = self.net
+        wait_all(self.sent)
+        goes = 1 - n.far
+        self.got[goes] = total(self.got[goes], self.own[goes])
+        self.sent = [n.copy(self.got.at[goes], self.q, seq=n.seq(2))]
+        self.got[n.far] = total(self.got[n.far], self.own[n.far])
+
+    def sides_finish(self):
+        n = self.net
+        wait_all(self.sent)
+        self.q[...] = total(self.q[...], self.got[n.far])
+
+
+class SecondPlane(Job):
+    space = pltpu.VMEM
+    inputs = ("q_second",)
+    shapes = ((EXPERTS, 128, D),)
+
+    def bind(self, ins, outs, scratch):
+        (self.q,), (self.o,) = ins, outs
+
+    def stages(self):
+        return [self.plane_begin, self.plane_second, self.plane_finish]
+
+    def plane_begin(self):
+        n = self.net
+        self.sent = []
+        dst = self.o.at[n.z, :, columns(n.half * 384, 384)]
+        for k in (2, 1, 3, 0):
+            src = self.q.at[n.plane(k)]
+            self.sent.append(n.move(src, dst) if k == 0 else n.copy(src, dst, fsdp=n.plane(k)))
+
+    def plane_second(self):
+        n = self.net
+        wait_all(self.sent)
+        part = self.o.at[:, :, columns(n.half * 384, 384)]
+        self.sent = [n.copy(part, part, rep=n.partner)]
+
+    def plane_finish(self):
+        wait_all(self.sent)
+
+
+class SecondReturn(SecondSides, SecondPlane):
+    space = pl.ANY
+    out_space = pl.ANY
+    inputs = SecondSides.inputs
+    shapes = SecondPlane.shapes
+    scratch = SecondSides.scratch + SecondSides.shapes
+
+    def bind(self, ins, outs, scratch):
+        SecondSides.bind(self, ins, scratch[2:], scratch[:2])
+        SecondPlane.bind(self, scratch[2:], outs, ())
+
+    stages = FirstReturn.stages
+
+
+class SharedAcross(Job):
+    inputs = ()
+    own = (-2, -1)
+    out_space = pltpu.VMEM
+    shapes = ((4, 4, 48, FF_DEV), (4, 128, 384))
+
+    def bind(self, ins, outs, scratch):
+        self.d1, self.d2 = ins
+        self.r1, self.r2 = outs
+
+    def stages(self):
+        return [self.begin, self.finish]
+
+    def begin(self):
+        n = self.net
+        part = self.d2.at[:, :, columns((1 - n.half) * 384, 384)]
+        self.sent = [
+            n.copy(self.d1.at[1 - n.half], self.r1, rep=n.partner),
+            n.copy(part, self.r2, rep=n.partner),
+        ]
+
+    def finish(self):
+        n = self.net
+        wait_all(self.sent)
+        self.r1[...] = total(self.r1[...], self.d1[n.half])
+        self.r2[...] = total(self.r2[...], self.d2[:, :, columns(n.half * 384, 384)])
+
+
 class SharedReturn(Job):
     space = pltpu.VMEM
-    inputs = ("d_w_in", "d_w_so")
+    inputs = ("r1", "r2")
     shapes = ((48, 2 * FF), (128, D))
-    scratch = (
-        (4, 4, 48, FF_DEV), (3, 4, 48, FF_DEV), (4, 48, FF_DEV), (4, 128, 384), (3, 128, 384),
-        (128, 384),
-    )
+    scratch = ((3, 4, 48, FF_DEV), (4, 48, FF_DEV), (3, 128, 384), (128, 384))
 
     def bind(self, ins, outs, scratch):
-        self.d1, self.d2 = ins
+        self.r1, self.r2 = ins
         self.o1, self.o2 = outs
-        self.r1, self.r1z, self.s1, self.r2, self.r2z, self.s2 = scratch
+        self.r1z, self.s1, self.r2z, self.s2 = scratch
 
     def stages(self):
-        return [self.begin, self.second_hop, self.third_hop, self.fourth_hop, self.finish]
-
-    def begin(self):
-        n = self.net
-        self.firsts = [n.copy(self.d1.at[1 - n.half], self.r1, rep=n.partner)]
-        part = self.d2.at[:, :, columns((1 - n.half) * 384, 384)]
-        self.seconds = [n.copy(part, self.r2, rep=n.partner)]
+        return [self.second_hop, self.third_hop, self.fourth_hop, self.finish]
 
     def second_hop(self):
         n = self.net
-        wait_all(self.firsts)
-        self.r1[...] = total(self.r1[...], self.d1[n.half])
         self.firsts = [
             n.copy(self.r1.at[:, n.plane(k)], self.r1z.at[k - 1], fsdp=n.plane(k))
             for k in (2, 1, 3)
         ]
-        wait_all(self.seconds)
-        self.r2[...] = total(self.r2[...], self.d2[:, :, columns(n.half * 384, 384)])
         self.seconds = [
             n.copy(self.r2.at[n.plane(k)], self.r2z.at[k - 1], fsdp=n.plane(k)) for k in (2, 1, 3)
         ]
@@ -674,6 +788,11 @@
 COPIES = 112
 
 
+class Late:
+    def __init__(self, array):
+        self.array = array
+
+
 def call(kernel, inputs, outputs, scratch, jobs, shards, cid):
     given = [shards[name] for job, *_ in jobs for name in job.inputs]
     results = [
@@ -681,8 +800,13 @@
         for job, *_ in jobs
         for shape in job.shapes
     ]
-    vmem = pl.BlockSpec(memory_space=pltpu.VMEM)
+    vmem, anywhere = pl.BlockSpec(memory_space=pltpu.VMEM), pl.BlockSpec(memory_space=pl.ANY)
     job_scratch = [pltpu.VMEM(shape, job.kind) for job, *_ in jobs for shape in job.scratch]
+    late_in = [i for i, x in enumerate(inputs) if isinstance(x, Late)]
+    arrays = [x.array if isinstance(x, Late) else x for x in inputs]
+    late_out = [i for i, x in enumerate(outputs) if len(x) == 3]
+    late = [pltpu.VMEM(arrays[i].shape, arrays[i].dtype) for i in late_in]
+    late += [pltpu.VMEM(outputs[i][0], outputs[i][1]) for i in late_out]
 
     def body(*refs):
         a = len(inputs)
@@ -691,29 +815,43 @@
         d = c + len(results)
         e = d + len(scratch)
         f = e + len(job_scratch)
-        net = Net(*refs[f:])
-        ground = Background(net, jobs, refs[a:b], refs[b:c], refs[c:d], refs[e:f])
-        kernel(net, ground, *refs[:a], *refs[b:c], *refs[d:e])
+        g = f + len(late)
+        net = Net(*refs[g:])
+        ins, outs = list(refs[:a]), list(refs[b:c])
+        net.coming, net.going = {}, []
+        for i, ref in zip(late_in, refs[f:]):
+            net.coming[id(ref)] = net.move(ins[i], ref)
+            ins[i] = ref
+        there = {}
+        for i, ref in zip(late_out, refs[f + len(late_in) : g]):
+            there[id(ref)] = outs[i]
+            outs[i] = ref
+        net.there = there
+        ground = Background(net, jobs, refs[a:b], outs + list(refs[d:e]), refs[c:d], refs[e:f])
+        kernel(net, ground, *ins, *outs, *refs[d:e])
+        assert not net.coming and not there
+        wait_all(net.going)
 
     made = pl.pallas_call(
         body,
-        out_shape=[jax.ShapeDtypeStruct(shape, kind) for shape, kind in outputs]
-        + [shape for shape, _ in results],
-        in_specs=[vmem] * len(inputs)
+        out_shape=[jax.ShapeDtypeStruct(x[0], x[1]) for x in outputs] + [shape for shape, _ in results],
+        in_specs=[anywhere if i in late_in else vmem for i in range(len(inputs))]
         + [pl.BlockSpec(memory_space=job.space) for job, *_ in jobs for _ in job.inputs],
-        out_specs=[vmem] * len(outputs) + [pl.BlockSpec(memory_space=where) for _, where in results],
+        out_specs=[anywhere if i in late_out else vmem for i in range(len(outputs))]
+        + [pl.BlockSpec(memory_space=where) for _, where in results],
         scratch_shapes=[pltpu.VMEM(shape, kind) for shape, kind in scratch]
         + job_scratch
+        + late
         + [
             pltpu.SemaphoreType.DMA((COPIES,)),
             pltpu.SemaphoreType.DMA((COPIES,)),
-            pltpu.SemaphoreType.DMA((32,)),
+            pltpu.SemaphoreType.DMA((56,)),
         ],
         compiler_params=pltpu.CompilerParams(
             collective_id=cid, has_side_effects=True, vmem_limit_bytes=60 << 20
         ),
         cost_estimate=pl.CostEstimate(flops=0, bytes_accessed=1 << 20, transcendentals=0),
-    )(*inputs, *given)
+    )(*arrays, *given)
     return made[: len(outputs)], made[len(outputs) :]
 
 
@@ -778,6 +916,7 @@
     project(net.seq(2))
     passed.wait_recv()
     project(net.seq(3))
+    net.done(every, queries, keys, values)
     ground.at(4)
     tokens = h.shape[0]
 
@@ -798,6 +937,7 @@
     for i in range(HEADS_DEV):
         head(i)
         ground.at(5 + i)
+    net.done(attended, totals)
 
     def part(b):
         low = jnp.concatenate([attended[i, b].astype(bf16) for i in range(HEADS_DEV)], 1)
@@ -829,8 +969,8 @@
         functools.partial(attn_forward_kernel, not weights),
         [h, gains, *tables, *weights],
         [
-            ((t, D), f32), ((t, D), bf16), ((SEQ, t, D), bf16), (head, bf16), (head, bf16),
-            (head, bf16), (head, f32), ((HEADS_DEV, SEQ, t, 128), f32),
+            ((t, D), f32), ((t, D), bf16), ((SEQ, t, D), bf16, 1), (head, bf16, 1), (head, bf16, 1),
+            (head, bf16, 1), (head, f32, 1), ((HEADS_DEV, SEQ, t, 128), f32, 1),
         ],
         [((2, t, D), bf16), ((2, t, D), bf16), ((t, D), bf16), ((t, D), bf16)],
         jobs, shards, cid,
@@ -841,33 +981,88 @@
     return g / (1.0 + jnp.exp(-g)) * u
 
 
+CHUNKS = ((0, 80), (80, 64))
+
+
+class SlotTrip:
+    def __init__(self, net, out, into):
+        self.net, self.into = net, into
+        self.sent, self.passed = {}, {}
+        for c, (at, size) in enumerate(CHUNKS):
+            for k in (2, 1, 3):
+                e = net.plane(k)
+                self.sent[c, k] = net.copy(
+                    out.at[e, pl.ds(at, size)], into.at[net.core, net.z, pl.ds(at, size)], fsdp=e
+                )
+        into[net.core, net.z] = out[net.z]
+
+    def hand_on(self, c):
+        net, (at, size) = self.net, CHUNKS[c]
+        self.passed[c] = []
+        for k in (0, 1, 3, 2):
+            if k:
+                self.sent[c, k].wait_recv()
+            part = self.into.at[net.core, net.plane(FSDP - k), pl.ds(at, size)]
+            self.passed[c].append(net.copy(part, part, seq=net.seq(1)))
+
+    def here(self, c):
+        for copy in self.passed[c]:
+            copy.wait_recv()
+
+    def close(self):
+        for copy in [*self.sent.values(), *self.passed[0], *self.passed[1]]:
+            copy.wait_send()
+
+
+class SlotReturn:
+    def __init__(self, net, out, into, own, back, home):
+        self.net, self.out, self.into, self.own = net, out, into, own
+        self.back, self.home = back, home
+        self.near, self.sent = {}, []
+
+    def other(self, c, rows):
+        at, size = CHUNKS[c]
+        self.out[:, at : at + size] = rows.astype(bf16).reshape(EXPERTS, size, D)
+        part = pl.ds(at, size)
+        self.near[c] = self.net.copy(self.out.at[:, part], self.into.at[:, part], seq=self.net.seq(1))
+
+    def mine(self, c, rows):
+        net, (at, size) = self.net, CHUNKS[c]
+        self.own[0 : EXPERTS * size] = rows
+        self.near[c].wait_recv()
+        got = self.into[:, at : at + size].astype(f32).reshape(EXPERTS * size, D)
+        both = (self.own[0 : EXPERTS * size] + got).astype(bf16)
+        self.back[:, at : at + size] = both.reshape(EXPERTS, size, D)
+        for k in (2, 1, 3):
+            e = net.plane(k)
+            part = pl.ds(at, size)
+            self.sent.append(net.copy(self.back.at[e, part], self.home.at[net.z, part], fsdp=e))
+        self.home[net.z, at : at + size] = self.back[net.z, at : at + size]
+
+    def wait(self):
+        for copy in self.sent:
+            copy.wait_recv()
+
+    def close(self):
+        for copy in [*self.sent, *self.near.values()]:
+            copy.wait_send()
+
+
 def ffn_forward_kernel(
-    net, ground, second, middle, router, onehot, chosen, w_in, w_so, w1, w2,
+    net, ground, second, middle, router, onehot, chosen, w_in, w_so,
     result, gates, gathered, every, joint, hidden, rows, joint_e, hidden_e,
     rows_out, prod_out, prod_in, prod_own, back_out, yields, near_out, near_in, away_out, away_in,
 ):
     t = second.shape[0]
+    w1, w2 = ground.made[0][0].w1, ground.made[0][0].w2
     net.greet(net.everyone())
     picked = chosen[:, :t] + chosen[:, t:]
     rows_out[...] = dot(picked, second[...]).astype(bf16).reshape(EXPERTS, CAP, D)
     every[net.s] = second[...]
     net.met()
-    sent = {}
-    for k in (2, 1, 3):
-        e = net.plane(k)
-        sent[k] = net.copy(rows_out.at[e], rows.at[net.core, net.z], fsdp=e)
+    trip = SlotTrip(net, rows_out, rows)
     far = net.copy(every.at[net.s], every.at[net.s], seq=net.seq(2))
     near = net.copy(every.at[net.s], every.at[net.s], seq=net.seq(1))
-    rows[net.core, net.z] = rows_out[net.z]
-    passed = []
-
-    def pass_rows(k):
-        if k:
-            sent[k].wait_recv()
-        part = rows.at[net.core, net.plane(FSDP - k)]
-        passed.append(net.copy(part, part, seq=net.seq(1)))
-
-    pass_rows(0)
     ground.at(0)
     logits = dot(second[...], router[...])
     l0 = jnp.sum(onehot[0] * logits, -1, keepdims=True)
@@ -877,6 +1072,7 @@
     g0, g1 = e0 / (e0 + e1), e1 / (e0 + e1)
     lane = lax.broadcasted_iota(jnp.int32, (t, 128), 1)
     gates[...] = jnp.where(lane == 0, g0, jnp.where(lane == 1, g1, 0.0))
+    net.need(w_in, w_so)
 
     def shared(b):
         g, u = dot(every[b], w_in[0]), dot(every[b], w_in[1])
@@ -890,75 +1086,79 @@
     ground.at(1)
     near.wait_recv()
     near_out[0] = shared(net.seq(1)).astype(bf16)
-    pass_rows(1)
-    pass_rows(3)
     far.wait_recv()
     passed_far = net.copy(every.at[net.seq(2)], every.at[net.seq(2)], seq=net.seq(1))
-    far_part = shared(net.seq(2))
-    pass_rows(2)
+    away_out[...] = shared(net.seq(2)).astype(bf16)
+    trip.hand_on(0)
     ground.at(2)
     passed_far.wait_recv()
     near_out[1] = shared(net.seq(3)).astype(bf16)
     near_sum = net.copy(near_out, near_in, seq=net.seq(1))
-    ground.at(3)
-
-    def expert(core):
-        x = rows[core].reshape(SLOTS, D)
+    net.done(every, joint, hidden)
+
+    def expert(core, c):
+        at, size = CHUNKS[c]
+        part = slice(at, at + size)
+        x = rows[core, :, part].reshape(EXPERTS * size, D)
         total = None
         for half in (0, 1):
-            g, u = dot(x, w1[half, 0]), dot(x, w1[half, 1])
-            joint_e[core, half, 0] = g.astype(bf16)
-            joint_e[core, half, 1] = u.astype(bf16)
+            g = dot(x, w1[half, 0].reshape(D, FF_DEV))
+            u = dot(x, w1[half, 1].reshape(D, FF_DEV))
+            shape = (EXPERTS, size, FF_DEV)
+            joint_e[core, half, 0, :, part] = g.astype(bf16).reshape(shape)
+            joint_e[core, half, 1, :, part] = u.astype(bf16).reshape(shape)
             low = silu_gate(g, u).astype(bf16)
-            hidden_e[core, half] = low
-            new = dot(low, w2[half * FF_DEV : (half + 1) * FF_DEV, :])
+            hidden_e[core, half, :, part] = low.reshape(shape)
+            new = dot(low, w2[half].reshape(FF_DEV, D))
             total = new if total is None else total + new
         return total
 
-    for copy in passed:
-        copy.wait_recv()
-    prod_out[...] = expert(1 - net.core).astype(bf16)
-    prod_sum = net.copy(prod_out, prod_in, seq=net.seq(1))
+    trip.here(0)
+    ground.at(3)
+    back = SlotReturn(net, prod_out, prod_in, prod_own, back_out, yields)
+    back.other(0, expert(1 - net.core, 0))
+    trip.hand_on(1)
     near_sum.wait_recv()
-    away_out[...] = (far_part + near_in[1].astype(f32)).astype(bf16)
+    away_out[...] = (away_out[...].astype(f32) + near_in[1].astype(f32)).astype(bf16)
     away_sum = net.copy(away_out, away_in, seq=net.seq(2))
     ground.at(4)
-    prod_own[...] = expert(net.core)
+    back.mine(0, expert(net.core, 0))
     ground.at(5)
-    prod_sum.wait_recv()
-    back_out[...] = (prod_own[...] + prod_in[...].astype(f32)).astype(bf16).reshape(EXPERTS, CAP, D)
-    returned = []
-    for k in (2, 1, 3):
-        e = net.plane(k)
-        returned.append(net.copy(back_out.at[e], yields.at[net.z], fsdp=e))
-    yields[net.z] = back_out[net.z]
+    trip.here(1)
+    back.other(1, expert(1 - net.core, 1))
+    back.mine(1, expert(net.core, 1))
+    net.done(rows, joint_e, hidden_e)
     ground.at(6)
+    net.need(middle)
     away_sum.wait_recv()
     base = middle[...] + own_part + near_in[0].astype(f32) + away_in[...].astype(f32)
-    for copy in returned:
-        copy.wait_recv()
+    back.wait()
     got = dot_tn(chosen[...], yields[...].reshape(SLOTS, D))
     gathered[...] = got.astype(bf16)
     result[...] = base + g0 * got[:t] + g1 * got[t:]
-    for copy in [far, near, passed_far, near_sum, prod_sum, away_sum, *passed, *sent.values(), *returned]:
+    for copy in [far, near, passed_far, near_sum, away_sum]:
         copy.wait_send()
+    trip.close()
+    back.close()
     ground.drain()
 
 
-def ffn_forward(second, middle, router, onehot, chosen, w_in, w_so, w1, w2, jobs, shards, cid):
+def ffn_forward(second, middle, router, onehot, chosen, w_in, w_so, jobs, shards, cid):
     t = second.shape[0]
+    slots = (EXPERTS, CAP, FF_DEV)
     return call(
         ffn_forward_kernel,
-        [second, middle, router, onehot, chosen, w_in, w_so, w1, w2],
+        [second, Late(middle), router, onehot, chosen, Late(w_in), Late(w_so)],
         [
-            ((t, D), f32), ((t, 128), f32), ((2 * t, D), bf16), ((SEQ, t, D), bf16),
-            ((2, SEQ, t, FF_DEV), bf16), ((SEQ, t, FF_DEV), bf16), ((2, EXPERTS, CAP, D), bf16),
-            ((2, 2, 2, SLOTS, FF_DEV), bf16), ((2, 2, SLOTS, FF_DEV), bf16),
+            ((t, D), f32), ((t, 128), f32), ((2 * t, D), bf16), ((SEQ, t, D), bf16, 1),
+            ((2, SEQ, t, FF_DEV), bf16, 1), ((SEQ, t, FF_DEV), bf16, 1),
+            ((2, EXPERTS, CAP, D), bf16, 1), ((2, 2, 2, *slots), bf16, 1), ((2, 2, *slots), bf16, 1),
         ],
         [
-            ((EXPERTS, CAP, D), bf16), ((SLOTS, D), bf16), ((SLOTS, D), bf16), ((SLOTS, D), f32),
-            ((EXPERTS, CAP, D), bf16), ((EXPERTS, CAP, D), bf16), ((2, t, D), bf16),
-            ((2, t, D), bf16), ((t, D), bf16), ((t, D), bf16),
+            ((EXPERTS, CAP, D), bf16), ((EXPERTS, CAP, D), bf16), ((EXPERTS, CAP, D), bf16),
+            ((EXPERTS * CHUNKS[0][1], D), f32), ((EXPERTS, CAP, D), bf16),
+            ((EXPERTS, CAP, D), bf16), ((2, t, D), bf16), ((2, t, D), bf16), ((t, D), bf16),
+            ((t, D), bf16),
         ],
         jobs, shards, cid,
     )
@@ -981,9 +1181,9 @@
 def ffn_backward_kernel(
     net, ground, grad, gates, onehot, chosen, gathered, middle, second, gains, router, every,
     joint, hidden, rows, joint_e, hidden_e, w_in, w_so, w1, w2,
-    d_middle, small, d_w1, d_w2, d_w_in, d_w_so,
+    d_middle, small, d_w1, d_w2,
     every_g, d_joint, rows_out, d_rows, d_joint_e, prod_out, prod_in, prod_own, back_out, back_in,
-    near_out, near_in, away_out, away_in,
+    near_out, near_in, away_out, away_in, d_w_in, d_w_so,
 ):
     t = grad.shape[0]
     net.greet(net.everyone())
@@ -993,29 +1193,11 @@
     rows_out[...] = dot(chosen[...], pairs).astype(bf16).reshape(EXPERTS, CAP, D)
     every_g[net.s] = up.astype(bf16)
     net.met()
-    sent = {}
-    for k in (2, 1, 3):
-        e = net.plane(k)
-        sent[k] = net.copy(rows_out.at[e], d_rows.at[net.core, net.z], fsdp=e)
+    trip = SlotTrip(net, rows_out, d_rows)
     far = net.copy(every_g.at[net.s], every_g.at[net.s], seq=net.seq(2))
     near = net.copy(every_g.at[net.s], every_g.at[net.s], seq=net.seq(1))
-    d_rows[net.core, net.z] = rows_out[net.z]
-    passed = []
-
-    def pass_rows(k):
-        if k:
-            sent[k].wait_recv()
-        part = d_rows.at[net.core, net.plane(FSDP - k)]
-        passed.append(net.copy(part, part, seq=net.seq(1)))
-
-    pass_rows(0)
     ground.at(0)
-    d0 = jnp.sum(up * gathered[:t].astype(f32), -1, keepdims=True)
-    d1 = jnp.sum(up * gathered[t:].astype(f32), -1, keepdims=True)
-    mean = g0 * d0 + g1 * d1
-    d_logits = (g0 * (d0 - mean) * onehot[0] + g1 * (d1 - mean) * onehot[1]).astype(bf16)
-    small[8:16, :] = dot_tn(d_logits, second[...])[:8]
-    local = dot_nt(d_logits, router[...])
+    net.need(w_so, joint, w_in)
 
     def shared(b):
         d_hidden = dot_nt(every_g[b], w_so[...])
@@ -1024,105 +1206,126 @@
         d_joint[1, b] = d_u
         return dot_nt(d_g, w_in[0]) + dot_nt(d_u, w_in[1])
 
-    local = local + shared(net.s)
+    local = shared(net.s)
     ground.at(1)
     near.wait_recv()
     near_out[0] = shared(net.seq(1)).astype(bf16)
-    pass_rows(1)
-    pass_rows(3)
     far.wait_recv()
     passed_far = net.copy(every_g.at[net.seq(2)], every_g.at[net.seq(2)], seq=net.seq(1))
-    far_part = shared(net.seq(2))
-    pass_rows(2)
+    away_out[...] = shared(net.seq(2)).astype(bf16)
+    trip.hand_on(0)
     ground.at(2)
     passed_far.wait_recv()
     near_out[1] = shared(net.seq(3)).astype(bf16)
     near_sum = net.copy(near_out, near_in, seq=net.seq(1))
-    ground.at(3)
-
-    def expert(core):
-        x = d_rows[core].reshape(SLOTS, D)
+    net.need(every, hidden)
+    tokens = every[...].reshape(SEQ * t, D)
+    for gu in (0, 1):
+        d_w = dot_tn(tokens, d_joint[gu].reshape(SEQ * t, FF_DEV))
+        d_w_in[gu] = d_w.astype(bf16).reshape(4, 4, 48, FF_DEV)
+    d_w = dot_tn(hidden[...].reshape(SEQ * t, FF_DEV), every_g[...].reshape(SEQ * t, D))
+    d_w_so[...] = d_w.astype(bf16).reshape(4, 128, D)
+    net.need(w2, w1, joint_e)
+
+    def expert(core, c):
+        at, size = CHUNKS[c]
+        part = slice(at, at + size)
+        x = d_rows[core, :, part].reshape(EXPERTS * size, D)
         out = None
         for half in (0, 1):
-            d_hidden = dot_nt(x, w2[half * FF_DEV : (half + 1) * FF_DEV, :])
-            d_g, d_u = gate_back(
-                joint_e[core, half, 0].astype(f32), joint_e[core, half, 1].astype(f32), d_hidden
-            )
-            d_joint_e[half, 0, core] = d_g
-            d_joint_e[half, 1, core] = d_u
-            new = dot_nt(d_g, w1[half, 0]) + dot_nt(d_u, w1[half, 1])
+            d_hidden = dot_nt(x, w2[half].reshape(FF_DEV, D))
+            flat, shape = (EXPERTS * size, FF_DEV), (EXPERTS, size, FF_DEV)
+            g = joint_e[core, half, 0, :, part].astype(f32).reshape(flat)
+            u = joint_e[core, half, 1, :, part].astype(f32).reshape(flat)
+            d_g, d_u = gate_back(g, u, d_hidden)
+            d_joint_e[half, 0, core, :, part] = d_g.reshape(shape)
+            d_joint_e[half, 1, core, :, part] = d_u.reshape(shape)
+            new = dot_nt(d_g, w1[half, 0].reshape(D, FF_DEV))
+            new = new + dot_nt(d_u, w1[half, 1].reshape(D, FF_DEV))
             out = new if out is None else out + new
         return out
 
-    for copy in passed:
-        copy.wait_recv()
-    prod_out[...] = expert(1 - net.core).astype(bf16)
-    prod_sum = net.copy(prod_out, prod_in, seq=net.seq(1))
+    trip.here(0)
+    ground.at(3)
+    back = SlotReturn(net, prod_out, prod_in, prod_own, back_out, back_in)
+    back.other(0, expert(1 - net.core, 0))
+    trip.hand_on(1)
     near_sum.wait_recv()
-    away_out[...] = (far_part + near_in[1].astype(f32)).astype(bf16)
+    away_out[...] = (away_out[...].astype(f32) + near_in[1].astype(f32)).astype(bf16)
     away_sum = net.copy(away_out, away_in, seq=net.seq(2))
     ground.at(4)
-    prod_own[...] = expert(net.core)
+    back.mine(0, expert(net.core, 0))
     ground.at(5)
-    prod_sum.wait_recv()
-    back_out[...] = (prod_own[...] + prod_in[...].astype(f32)).astype(bf16).reshape(EXPERTS, CAP, D)
-    returned = []
-    for k in (2, 1, 3):
-        e = net.plane(k)
-        returned.append(net.copy(back_out.at[e], back_in.at[net.z], fsdp=e))
-    back_in[net.z] = back_out[net.z]
+    trip.here(1)
+    back.other(1, expert(1 - net.core, 1))
+    back.mine(1, expert(net.core, 1))
     ground.at(6)
-    rows_all = rows[...].reshape(2 * SLOTS, D)
-    d_rows_all = d_rows[...].reshape(2 * SLOTS, D)
+    net.need(rows, hidden_e)
     for half in (0, 1):
+        d_rows_all = d_rows[...].reshape(2 * SLOTS, D)
         for gu in (0, 1):
-            d_w1[half, gu] = dot_tn(rows_all, d_joint_e[half, gu].reshape(2 * SLOTS, FF_DEV)).astype(
-                bf16
+            d_w = dot_tn(
+                rows[...].reshape(2 * SLOTS, D), d_joint_e[half, gu].reshape(2 * SLOTS, FF_DEV)
             )
-        low = jnp.concatenate([hidden_e[0, half], hidden_e[1, half]], 0)
-        d_w2[half] = dot_tn(low, d_rows_all).astype(bf16)
-        ground.at(6 + half)
-    ground.at(8)
-    tokens = every[...].reshape(SEQ * t, D)
-    for gu in (0, 1):
-        d_w_in[gu] = dot_tn(tokens, d_joint[gu].reshape(SEQ * t, FF_DEV)).astype(bf16)
-    ground.at(9)
-    d_w_so[...] = dot_tn(hidden[...].reshape(SEQ * t, FF_DEV), every_g[...].reshape(SEQ * t, D)).astype(
-        bf16
-    )
+            d_w1[half, gu] = d_w.astype(bf16).reshape(4, 4, 48, FF_DEV)
+        low = jnp.concatenate(
+            [hidden_e[core, half].reshape(SLOTS, FF_DEV) for core in (0, 1)], 0
+        )
+        d_w2[half] = dot_tn(low, d_rows_all).astype(bf16).reshape(4, 128, D)
+        ground.at(7 + half)
+    net.done(d_w1, d_w2)
+    net.need(gathered, onehot, second, router, middle)
+    d0 = jnp.sum(up * gathered[:t].astype(f32), -1, keepdims=True)
+    d1 = jnp.sum(up * gathered[t:].astype(f32), -1, keepdims=True)
+    mean = g0 * d0 + g1 * d1
+    d_logits = (g0 * (d0 - mean) * onehot[0] + g1 * (d1 - mean) * onehot[1]).astype(bf16)
+    small[8:16, :] = dot_tn(d_logits, second[...])[:8]
+    local = local + dot_nt(d_logits, router[...])
     away_sum.wait_recv()
-    for copy in returned:
-        copy.wait_recv()
+    local = local + near_in[0].astype(f32) + away_in[...].astype(f32)
+    back.wait()
     picked = chosen[:, :t] + chosen[:, t:]
-    d_normed = local + near_in[0].astype(f32) + away_in[...].astype(f32)
-    d_normed = d_normed + dot_tn(picked, back_in[...].reshape(SLOTS, D))
+    d_normed = local + dot_tn(picked, back_in[...].reshape(SLOTS, D))
     d_x, d_gain = norm_back(middle[...], gains[1:2, :], d_normed)
     d_middle[...] = up + d_x
     small[0:8, :] = jnp.broadcast_to(d_gain, (8, D))
-    for copy in [far, near, passed_far, near_sum, prod_sum, away_sum, *passed, *sent.values(), *returned]:
+    for copy in [far, near, passed_far, near_sum, away_sum]:
         copy.wait_send()
+    trip.close()
+    back.close()
     ground.drain()
 
 
 def ffn_backward(grad, saved, gains, router, weights, jobs, shards, cid):
     t = grad.shape[0]
     gates, onehot, chosen, gathered, middle, second, every, joint, hidden, rows, joint_e, hidden_e = saved
+    w_in, w_so, w1, w2 = weights
     slots = (EXPERTS, CAP, D)
+    late = {}
+    for name, x in (
+        ("w_so", w_so), ("joint", joint), ("w_in", w_in), ("every", every), ("hidden", hidden),
+        ("w2", w2), ("joint_e", joint_e), ("w1", w1), ("rows", rows), ("hidden_e", hidden_e),
+        ("gathered", gathered), ("onehot", onehot), ("second", second), ("router", router),
+        ("middle", middle),
+    ):
+        late[name] = Late(x)
     return call(
         ffn_backward_kernel,
         [
-            grad, gates, onehot, chosen, gathered, middle, second, gains, router, every, joint,
-            hidden, rows, joint_e, hidden_e, *weights,
+            grad, gates, late["onehot"], chosen, late["gathered"], late["middle"], late["second"],
+            gains, late["router"], late["every"], late["joint"], late["hidden"], late["rows"],
+            late["joint_e"], late["hidden_e"], late["w_in"], late["w_so"], late["w1"], late["w2"],
         ],
         [
-            ((t, D), f32), ((16, D), f32), ((2, 2, D, FF_DEV), bf16), ((2, FF_DEV, D), bf16),
-            ((2, D, FF_DEV), bf16), ((FF_DEV, D), bf16),
+            ((t, D), f32), ((16, D), f32), ((2, 2, 4, 4, 48, FF_DEV), bf16, 1),
+            ((2, 4, 128, D), bf16, 1),
         ],
         [
             ((SEQ, t, D), bf16), ((2, SEQ, t, FF_DEV), bf16), (slots, bf16), ((2, *slots), bf16),
-            ((2, 2, 2, SLOTS, FF_DEV), bf16), ((SLOTS, D), bf16), ((SLOTS, D), bf16),
-            ((SLOTS, D), f32), (slots, bf16), (slots, bf16), ((2, t, D), bf16), ((2, t, D), bf16),
-            ((t, D), bf16), ((t, D), bf16),
+            ((2, 2, 2, EXPERTS, CAP, FF_DEV), bf16), (slots, bf16), (slots, bf16),
+            ((EXPERTS * CHUNKS[0][1], D), f32), (slots, bf16), (slots, bf16), ((2, t, D), bf16),
+            ((2, t, D), bf16), ((t, D), bf16), ((t, D), bf16), ((2, 4, 4, 48, FF_DEV), bf16),
+            ((4, 128, D), bf16),
         ],
         jobs, shards, cid,
     )
@@ -1143,6 +1346,8 @@
     near = net.copy(every_m.at[net.s], every_m.at[net.s], seq=net.seq(1))
     ground.at(0)
 
+    net.need(w_out)
+
     def project(b):
         d = dot_nt(every_m[b], w_out[...].reshape(COLS, D)).astype(bf16)
         for i in range(HEADS_DEV):
@@ -1157,12 +1362,14 @@
     passed.wait_recv()
     project(net.seq(3))
     ground.at(1)
+    net.need(attended)
     tokens = every_m[...].reshape(SEQ * t, D)
     low = jnp.concatenate(
         [attended[i].reshape(SEQ * t, HEAD_DIM).astype(bf16) for i in range(HEADS_DEV)], 1
     )
     d_w_out[...] = dot_tn(low, tokens).astype(bf16).reshape(SEQ, 48, D)
     scale = HEAD_DIM**-0.5
+    net.need(queries, keys, values, totals)
 
     def head(i):
         d_k[i] = jnp.zeros_like(d_k[i])
@@ -1187,6 +1394,8 @@
         head(i)
         ground.at(2 + i)
 
+    net.need(cosine, sine, w_qkv)
+
     def part(b):
         c, sn = cosine[b], -sine[b]
         pieces = [turn(d_q[i, b], c, sn) for i in range(HEADS_DEV)]
@@ -1206,10 +1415,12 @@
     away_sum = net.copy(away_out, away_in, seq=net.seq(2))
     own = own + near_in[0].astype(f32)
     ground.at(5)
+    net.need(every)
     d_w = dot_tn(every[...].reshape(SEQ * t, D), d_joint[...].reshape(SEQ * t, 3 * COLS))
     d_w_qkv[...] = d_w.astype(bf16).reshape(4, 4, 48, 3 * COLS)
     ground.at(6)
     away_sum.wait_recv()
+    net.need(h)
     d_x, gain = norm_back(h[...], gains[0:1, :], own + away_in[...].astype(f32))
     grad[...] = up + d_x
     row = lax.broadcasted_iota(jnp.int32, (8, D), 0)
@@ -1226,7 +1437,8 @@
     head = (HEADS_DEV, SEQ, t, HEAD_DIM)
     return call(
         attn_backward_kernel,
-        [d_middle, h, gains, every, queries, keys, values, attended, totals, *weights, *tables],
+        [d_middle, Late(h), gains]
+        + [Late(x) for x in (every, queries, keys, values, attended, totals, *weights, *tables)],
         [((t, D), f32), ((8, D), f32), ((4, 4, 48, 3 * COLS), bf16), ((4, 48, D), bf16)],
         [
             ((SEQ, t, D), bf16), (head, bf16), (head, f32), (head, f32), (head, f32),
@@ -1238,18 +1450,36 @@
 
 
 FORWARD_ATTN_FIRST = (
-    (AttnFetchHere, 0, (0, 1, 3, 3)),
-    (ExpertFetch, 0, (1, 4, 6, 9)),
-    (SharedFetch, 0, (2, 4, 7, 9)),
-    (AttnFetch, 1, (4, 7, 8, 9)),
+    (AttnFetchHere, 0, (0, 1, 2, 3)),
+    (SharedFetch, 0, (2, 3, 6, 9)),
+    (ExpertFetch, 0, (4, 8, 9)),
 )
-FORWARD_FFN_FIRST = ((ExpertPlane, 1, (3, 9)),)
-FORWARD_ATTN = ((ExpertSides, 1, (1, 5, 9)), (SharedFetch, 1, (1, 2, 5, 9)))
-BACKWARD_FFN = ((ExpertPlaneReturn, 1, (3, 6, 9)), (AttnReturn, 1, (0, 3, 6, 8, 9)))
-BACKWARD_ATTN = ((ExpertSidesReturn, 1, (0, 4, 9)), (SharedReturn, 1, (0, 3, 5, 9)))
+FORWARD_FFN_FIRST = (
+    (ExpertJoin, 0, (0, 3, 9)),
+    (AttnFetch, 1, (0, 1, 3, 9)),
+    (ExpertPlane, 1, (3, 9)),
+)
+FORWARD_ATTN = ((ExpertNear, 1, (1, 9)), (SharedFetch, 1, (1, 2, 5, 9)))
+FORWARD_FFN = ((ExpertJoin, 1, (0, 3, 9)),)
+BACKWARD_FFN_FIRST = ((SharedAcross, 1, (3, 9)),)
+BACKWARD_ATTN = (
+    (GateSides, 1, (0, 3, 9)),
+    (UpSides, 1, (0, 3, 9)),
+    (SecondSides, 1, (0, 4, 9)),
+    (SharedReturn, 1, (0, 4, 5, 9)),
+)
+BACKWARD_FFN = (
+    (SharedAcross, 0, (3, 9)),
+    (AttnReturn, 1, (0, 2, 5, 8, 9)),
+    (GatePlane, 1, (3, 7, 9)),
+    (UpPlane, 1, (3, 8, 9)),
+    (SecondPlane, 1, (3, 7, 9)),
+)
 BACKWARD_ATTN_LAST = (
-    (ExpertReturn, 0, (0, 3, 5, 9)),
-    (SharedReturn, 0, (0, 3, 5, 9)),
+    (GateReturn, 0, (0, 3, 5, 9)),
+    (UpReturn, 0, (0, 3, 5, 9)),
+    (SecondReturn, 0, (0, 4, 6, 9)),
+    (SharedReturn, 0, (0, 4, 5, 9)),
     (AttnReturnHere, 0, (6, 9)),
     (SmallReturnHere, 0, (7, 9)),
 )
@@ -1300,20 +1530,23 @@
         (middle, second, every_one, queries, keys, values, attended, totals), fetched = attn_forward(
             h, gains[layer], attn, tables, jobs, shards, 12 + layer
         )
+        names = ("ax", "ay", "bx", "by")
         if first:
-            attn, fetched, next_attn = fetched[:2], fetched[2:6], fetched[6:]
-        w_qkv, w_out = attn
-        w1, w2 = fetched[0].reshape(2, 2, D, FF_DEV), fetched[1].reshape(FF_CORE, D)
-        w_in, w_so = fetched[2].reshape(2, D, FF_DEV), fetched[3].reshape(FF_DEV, D)
+            attn, shared, fetched = fetched[:2], fetched[2:4], fetched[4:]
+            names = ("p1", "p2") + names
+        else:
+            fetched, shared = fetched[:4], fetched[4:]
+        shards.update(zip(names, fetched))
+        w_in, w_so = shared[0].reshape(2, D, FF_DEV), shared[1].reshape(FF_DEV, D)
         router_pad = jnp.pad(routers[layer], ((0, 0), (0, 124)))
         outs, fetched = ffn_forward(
-            second, middle, router_pad, onehot, routes[1], w_in, w_so, w1, w2,
-            FORWARD_FFN_FIRST if first else (), shards, 14 + layer,
+            second, middle, router_pad, onehot, routes[1], w_in, w_so,
+            FORWARD_FFN_FIRST if first else FORWARD_FFN, shards, 14 + layer,
         )
-        attn_weights, ffn_weights = attn, (w_in, w_so, w1, w2)
+        attn_weights, ffn_weights = attn, (w_in, w_so, fetched[0], fetched[1])
         if first:
-            attn = next_attn
-            shards["p1"], shards["p2"] = fetched
+            attn = fetched[2:4]
+            shards["p1"], shards["p2"] = fetched[4:]
         result, gates, gathered, every_two, joint, hidden, rows, joint_e, hidden_e = outs
         attn_saved = (h, every_one, queries, keys, values, attended, totals)
         ffn_saved = (
@@ -1330,16 +1563,13 @@
     for layer in reversed(range(LAYERS)):
         last = layer == 0
         attn_weights, ffn_weights, attn_saved, ffn_saved, router_pad = kept_layers[layer]
-        (d_middle, small, d_w1, d_w2, d_w_in, d_w_so), done = ffn_backward(
-            grad, ffn_saved, gains[layer], router_pad, ffn_weights, BACKWARD_FFN if last else (),
-            grads, 18 + layer,
+        (d_middle, small, grads["d_w1"], grads["d_w2"]), done = ffn_backward(
+            grad, ffn_saved, gains[layer], router_pad, ffn_weights,
+            BACKWARD_FFN if last else BACKWARD_FFN_FIRST, grads, 18 + layer,
         )
+        grads["r1"], grads["r2"] = done[:2]
         if last:
-            returned["d_expert", 1], returned["d_attn", 1] = done[:2], done[2:]
-        grads["d_w1"] = d_w1.reshape(2, 2, 4, 4, 48, FF_DEV)
-        grads["d_w2"] = d_w2.reshape(2, 4, 128, D)
-        grads["d_w_in"] = d_w_in.reshape(2, 4, 4, 48, FF_DEV)
-        grads["d_w_so"] = d_w_so.reshape(4, 128, D)
+            returned["d_attn", 1], returned["d_expert", 1] = done[2:4], done[4:]
         smalls[layer] = jnp.concatenate([small[:1], small[8:12]], 0)
         if last:
             rows = jnp.concatenate([jnp.zeros((1, D), f32), smalls[0], d_gain[:1], smalls[1]], 0)
@@ -1349,11 +1579,11 @@
             BACKWARD_ATTN_LAST if last else BACKWARD_ATTN, grads, 16 + layer,
         )
         if last:
-            returned["d_expert", 0], returned["d_shared", 0] = done[:2], done[2:4]
-            returned["d_attn", 0], total_small = done[4:6], done[6]
+            returned["d_expert", 0], returned["d_shared", 0] = done[:3], done[3:5]
+            returned["d_attn", 0], total_small = done[5:7], done[7]
         else:
-            grads["q1"], grads["q2"] = done[:2]
-            returned["d_shared", 1] = done[2:]
+            grads["q_gate"], grads["q_up"], grads["q_second"] = done[:3]
+            returned["d_shared", 1] = done[3:]
             grads["d_w_qkv"], grads["d_w_out"] = d_w_qkv, d_w_out
     total_small = rep_rest(total_small, reps)[:12].reshape(LAYERS, 6, D)
     total_small = lax.dynamic_slice_in_dim(total_small, (s * FSDP + z) * 48, 48, 2)
@@ -1365,7 +1595,8 @@
     return (
         output, grad[None], total_small[:, :2], d_qkv.reshape(LAYERS, 48, 3 * D),
         stack("d_attn", 1), total_small[:, 2:].transpose(0, 2, 1), stack("d_shared", 0),
-        stack("d_shared", 1), stack("d_expert", 0), stack("d_expert", 1),
+        stack("d_shared", 1), jnp.concatenate([stack("d_expert", 0), stack("d_expert", 1)], -1),
+        stack("d_expert", 2),
     )
 
 

time: 872 us -> 721 us (0.83)
  Pallas kernels: 820 us -> 666 us
    pallas_call x9, Pallas kernels: 820 us -> 666 us  [call(): pl.pallas_call(body, out_shape=[jax.ShapeDtypeStruct(x[0], x[1]) for x in...]
where the time goes in v4:
time: 721 us; the launch traced here: 709 us
  Pallas kernels  666 us (92%)
  other arithmetic  20.9 us (3%)
  local copies, waits for them, and re-layouts  19 us (3%)
    pallas_call x9, Pallas kernels, call(): pl.pallas_call(body, out_shape=[jax.ShapeDtypeStruct(x[0], x[1]) for x in...  666 us

profile of v4, /device:TPU:8, one launch (start us, length us, event | category | flops | bytes accessed | tf_op | source)
XLA Modules:
  0.0 708.9 jit_solution(1449496704199540127)
XLA Ops:
  0.6 1.9 bitcast_convert_fusion.1.refs_0_.refs_1_
  3.9 12.2 %shard_map.195 = bf16[4,4,16,128]{3,2,1,0:T(8,128)(2,1)} custom-call(bf16[16,128]{1,0:T(8,128)(2,1)} %pad.15.refs_0_), custom_call_target="tpu_custom_call" | custom-call | bytes 1048576 | tf_op jit(solution)/shard_map/pallas_call | solution.py:835
  16.1 0.9 copy.55
  17.7 1.9 fusion.12
  19.7 1.3 pad_maximum_fusion
  21.8 1.4 reshape.153.refs_4_.refs_13_
  23.2 103.4 %shard_map.196 = (f32[256,768]{1,0:T(8,128)}, bf16[256,768]{1,0:T(8,128)(2,1)}, bf16[4,256,768]{2,1,0:T(8,128)(2,1)}, bf16[3,4,256,64]{3,2,1,0:T(8,128)(2,1)}, b...) custom-call(f32[256,768]{1,0:T(8,128)} %bitcast_convert_fusion.1.ref, ...), custom_call_target="tpu_custom_call" | custom-call | bytes 1048576 | tf_op jit(solution)/shard_map/pallas_call | solution.py:835
  128.0 0.9 fusion.10.refs_3_.refs_2_
  130.3 1.0 fusion.refs_4_.refs_3_
  131.3 90.1 %shard_map.197 = (f32[256,768]{1,0:T(8,128)}, f32[256,128]{1,0:T(8,128)}, bf16[512,768]{1,0:T(8,128)(2,1)}, bf16[4,256,768]{2,1,0:T(8,128)(2,1)}, bf16[2,4,256,5...) custom-call(bf16[256,768]{1,0:T(8,128)(2,1)} %get-tuple-element.103., ...), custom_call_target="tpu_custom_call" | custom-call | bytes 1048576 | tf_op jit(solution)/shard_map/pallas_call | solution.py:835
  221.4 79.4 %shard_map.198 = (f32[256,768]{1,0:T(8,128)}, bf16[256,768]{1,0:T(8,128)(2,1)}, bf16[4,256,768]{2,1,0:T(8,128)(2,1)}, bf16[3,4,256,64]{3,2,1,0:T(8,128)(2,1)}, b...) custom-call(f32[256,768]{1,0:T(8,128)} %get-tuple-element.113.refs_0, ...), custom_call_target="tpu_custom_call" | custom-call | bytes 1048576 | tf_op jit(solution)/shard_map/pallas_call | solution.py:835
  301.8 0.9 fusion.11.refs_3_.refs_2_
  304.1 1.0 fusion.1.refs_4_.refs_3_
  305.1 56.9 %shard_map.199 = (f32[256,768]{1,0:T(8,128)}, f32[256,128]{1,0:T(8,128)}, bf16[512,768]{1,0:T(8,128)(2,1)}, bf16[4,256,768]{2,1,0:T(8,128)(2,1)}, bf16[2,4,256,5...) custom-call(bf16[256,768]{1,0:T(8,128)(2,1)} %get-tuple-element.118., ...), custom_call_target="tpu_custom_call" | custom-call | bytes 1048576 | tf_op jit(solution)/shard_map/pallas_call | solution.py:835
  362.0 1.9 convert_bitcast_fusion.1
  363.9 0.9 bitcast_convert_fusion.refs_0_
  364.9 53.8 %shard_map.200 = (f32[256,768]{1,0:T(8,128)}, f32[16,768]{1,0:T(8,128)}, bf16[2,2,4,4,48,512]{5,4,3,2,1,0:T(8,128)(2,1)}, bf16[2,4,128,768]{3,2,1,0:T(8,128)(2,1...) custom-call(f32[256,768]{1,0:T(8,128)} %bitcast_convert_fusion.refs_0_, ...), custom_call_target="tpu_custom_call" | custom-call | bytes 1048576 | tf_op jit(solution)/shard_map/pallas_call | solution.py:835
  418.7 64.4 %shard_map.201 = (f32[256,768]{1,0:T(8,128)}, f32[8,768]{1,0:T(8,128)}, bf16[4,4,48,576]{3,2,1,0:T(8,128)(2,1)}, bf16[4,48,768]{2,1,0:T(8,128)(2,1)}, bf16[2,4,4...) custom-call(f32[256,768]{1,0:T(8,128)} %get-tuple-element.137.refs_0, ...), custom_call_target="tpu_custom_call" | custom-call | bytes 1048576 | tf_op jit(solution)/shard_map/pallas_call | solution.py:835
  483.0 95.1 %shard_map.202 = (f32[256,768]{1,0:T(8,128)}, f32[16,768]{1,0:T(8,128)}, bf16[2,2,4,4,48,512]{5,4,3,2,1,0:T(8,128)(2,1)}, bf16[2,4,128,768]{3,2,1,0:T(8,128)(2,1...) custom-call(f32[256,768]{1,0:T(8,128)} %get-tuple-element.148.refs_0, ...), custom_call_target="tpu_custom_call" | custom-call | bytes 1048576 | tf_op jit(solution)/shard_map/pallas_call | solution.py:835
  578.1 0.7 slice.74
  578.9 0.7 slice.75
  581.1 0.7 slice.78
  582.5 110.2 %shard_map.203 = (f32[256,768]{1,0:T(8,128)}, f32[8,768]{1,0:T(8,128)}, bf16[4,4,48,576]{3,2,1,0:T(8,128)(2,1)}, bf16[4,48,768]{2,1,0:T(8,128)(2,1)}, bf16[4,48,...) custom-call(f32[256,768]{1,0:T(8,128)} %get-tuple-element.164.refs_0, ...), custom_call_target="tpu_custom_call" | custom-call | bytes 1048576 | tf_op jit(solution)/shard_map/pallas_call | solution.py:835
  692.8 0.8 reshape.158
  694.4 1.1 stack.63
  696.1 0.8 copy.45
  696.9 1.7 reshape.164
  700.0 1.2 maximum_convert_fusion.2
  701.3 0.9 maximum_convert_fusion.3
  702.7 3.0 maximum_convert_fusion
  705.7 1.9 maximum_convert_fusion.1
  707.6 0.9 copy.57
  (89 shorter events, 13.5 us)
Async XLA Ops:
  17.7 3.2 copy-start.7
  23.2 104.5 %copy-start.16 = (s32[2,1,256,2]{2,3,1,0:T(2,128)S(1)}, s32[2,1,256,2]{2,3,1,0:T(2,128)}, u32[]{:S(2)}) copy-start(s32[2,1,256,2]{2,3,1,0:T(2,128)} %param.13) | copy-start | bytes 12292
  126.6 2.2 copy-start.17
  305.1 58.8 %copy-start.10 = (bf16[1,256,768]{2,1,0:T(8,128)(2,1)S(1)}, bf16[1,256,768]{2,1,0:T(8,128)(2,1)}, u32[]{:S(2)}) copy-start(bf16[1,256,768]{2,1,0:T(8,128)(2,1)} %param.23) | copy-start | bytes 1179652
  582.5 111.7 %copy-start.11 = (bf16[4,48,576]{2,1,0:T(8,128)(2,1)S(1)}, bf16[4,48,576]{2,1,0:T(8,128)(2,1)}, u32[]{:S(2)}) copy-start(bf16[4,48,576]{2,1,0:T(8,128)(2,1)} %get-tuple-element.183) | copy-start | bytes 663556
  696.1 2.5 copy-start.14
  696.1 2.5 copy-start.15
  696.9 3.1 copy-start.8
  696.9 3.1 copy-start.9
  698.6 2.7 copy-start.12
  698.6 2.7 copy-start.13
  700.0 2.2 copy-start.1
  700.0 2.2 copy-start.2
  700.0 2.2 copy-start.4
  700.0 2.7 copy-start.5
  702.7 3.0 copy-start
  702.7 3.0 copy-start.3
  705.7 1.9 copy-start.6

commit v5 on v4

--- a/solution.py
+++ b/solution.py
@@ -2,6 +2,7 @@
 
 import jax
 import jax.numpy as jnp
+import numpy as np
 from jax import lax
 from jax.experimental import pallas as pl
 from jax.experimental.pallas import tpu as pltpu
@@ -209,7 +210,7 @@
 
 
 class ExpertNear(ExpertFetch):
-    inputs = ("p1", "p2")
+    inputs = ("next_p1", "next_p2")
     shapes = ExpertFetch.shapes[2:]
 
     def bind(self, ins, outs, scratch):
@@ -275,32 +276,30 @@
 
     def begin(self):
         n = self.net
-        self.firsts, self.seconds = [], []
+        self.firsts = []
         for d in (3, 2, 1, 0):
             src = self.first.at[self.layer, :, columns(n.half * FF + n.seq(d) * FF_DEV, FF_DEV)]
             dst = self.w_in.at[n.half, n.s, n.z]
             self.firsts.append(n.move(src, dst) if d == 0 else n.copy(src, dst, seq=n.seq(d)))
-        for k in (2, 1, 3, 0):
-            src = self.second.at[self.layer, :, columns(n.half * 384, 384)]
-            dst = self.w_out.at[n.z, :, columns(n.half * 384, 384)]
-            self.seconds.append(n.move(src, dst) if k == 0 else n.copy(src, dst, fsdp=n.plane(k)))
+        src = self.second.at[self.layer, :, columns(n.half * 384, 384)]
+        self.firsts.append(n.move(src, self.w_out.at[n.z, :, columns(n.half * 384, 384)]))
 
     def second_hop(self):
         n = self.net
         wait_all(self.firsts)
-        part = self.w_in.at[n.half, :, n.z]
-        self.firsts = [n.copy(part, part, fsdp=n.plane(k)) for k in (2, 1, 3)]
-        self.across = [n.copy(part, part, rep=n.partner)]
-        wait_all(self.seconds)
-        part = self.w_out.at[:, :, columns(n.half * 384, 384)]
-        self.across.append(n.copy(part, part, rep=n.partner))
+        part, low = self.w_in.at[n.half, :, n.z], self.w_out.at[n.z, :, columns(n.half * 384, 384)]
+        self.sent = {}
+        for k in (2, 1, 3):
+            self.sent[k] = [n.copy(part, part, fsdp=n.plane(k)), n.copy(low, low, fsdp=n.plane(k))]
+        self.across = [n.copy(part, part, rep=n.partner), n.copy(low, low, rep=n.partner)]
 
     def third_hop(self):
         n = self.net
-        for copy, k in zip(self.firsts[1:] + self.firsts[:1], (1, 3, 2)):
-            copy.wait()
-            part = self.w_in.at[n.half, :, n.plane(FSDP - k)]
-            self.across.append(n.copy(part, part, rep=n.partner))
+        for k in (1, 3, 2):
+            wait_all(self.sent[k])
+            z = n.plane(FSDP - k)
+            for part in (self.w_in.at[n.half, :, z], self.w_out.at[z, :, columns(n.half * 384, 384)]):
+                self.across.append(n.copy(part, part, rep=n.partner))
 
     def finish(self):
         wait_all(self.across)
@@ -353,6 +352,8 @@
 
 
 class SmallFetch(Job):
+    out_space = pltpu.VMEM
+
     inputs = ("small",)
     shapes = ((4, 4, 16, 128),)
 
@@ -430,6 +431,7 @@
 class FirstPlane(Job):
     space = pltpu.VMEM
     shapes = ((EXPERTS, 48, FF),)
+    half_only = False
 
     def bind(self, ins, outs, scratch):
         (self.q,), (self.o,) = ins, outs
@@ -440,7 +442,8 @@
     def plane_begin(self):
         n = self.net
         self.sent = []
-        dst = self.o.at[n.z, :, columns(n.half * FF_CORE + n.core * FF_DEV, FF_DEV)]
+        at = n.core * FF_DEV if self.half_only else n.half * FF_CORE + n.core * FF_DEV
+        dst = self.o.at[n.z, :, columns(at, FF_DEV)]
         for k in (2, 1, 3, 0):
             for d in (1, 0):
                 core = n.core if d == 0 else 1 - n.core
@@ -461,39 +464,50 @@
 
 
 class FirstReturn(FirstSides, FirstPlane):
+    shapes = FirstPlane.shapes
+    scratch = FirstSides.scratch + FirstSides.shapes
     space = pl.ANY
     out_space = pl.ANY
-    shapes = FirstPlane.shapes
-    scratch = FirstSides.scratch + FirstSides.shapes
 
     def bind(self, ins, outs, scratch):
         FirstSides.bind(self, ins, scratch[2:], scratch[:2])
         FirstPlane.bind(self, scratch[2:], outs, ())
 
-    def stages(self):
-        def turn_over():
-            self.sides_finish()
-            self.plane_begin()
-
+    def turn_over(self):
+        self.sides_finish()
+        self.plane_begin()
+
+    def stages(self):
         return [
-            self.sides_begin, self.sides_second, turn_over, self.plane_second, self.plane_finish,
+            self.sides_begin, self.sides_second, self.turn_over, self.plane_second,
+            self.plane_finish,
         ]
 
 
-class GateSides(FirstSides):
-    gu = 0
-
-
-class UpSides(FirstSides):
-    gu = 1
-
-
-class GatePlane(FirstPlane):
-    inputs = ("q_gate",)
-
-
-class UpPlane(FirstPlane):
-    inputs = ("q_up",)
+class FirstToPlane(FirstReturn):
+    shapes = ((EXPERTS, 48, FF_CORE),)
+    half_only = True
+
+    def stages(self):
+        return [self.sides_begin, self.sides_second, self.turn_over, self.plane_finish]
+
+
+class FirstFinal(Job):
+    shapes = ((EXPERTS, 48, FF),)
+
+    def bind(self, ins, outs, scratch):
+        (self.q,), (self.o,) = ins, outs
+
+    def stages(self):
+        return [self.begin, self.finish]
+
+    def begin(self):
+        n = self.net
+        part = self.o.at[:, :, columns(n.half * FF_CORE, FF_CORE)]
+        self.sent = [n.copy(self.q, part, rep=n.partner), n.move(self.q, part)]
+
+    def finish(self):
+        wait_all(self.sent)
 
 
 class GateReturn(FirstReturn):
@@ -504,54 +518,72 @@
     gu = 1
 
 
-class SecondSides(Job):
+class GateToPlane(FirstToPlane):
+    gu = 0
+
+
+class UpToPlane(FirstToPlane):
+    gu = 1
+
+
+class GateFinal(FirstFinal):
+    inputs = ("q_gate",)
+
+
+class UpFinal(FirstFinal):
+    inputs = ("q_up",)
+
+
+class SecondReturn(Job):
     inputs = ("d_w2",)
-    out_space = pltpu.VMEM
-    shapes = ((4, 128, 384),)
-    scratch = ((2, 4, 128, 384), (2, 4, 128, 384))
+    shapes = ((EXPERTS, 128, D),)
+    scratch = ((2, 4, 128, 384), (2, 4, 128, 384), (4, 128, 384))
+    rep_first = True
 
     def bind(self, ins, outs, scratch):
-        (self.d,), (self.q,) = ins, outs
-        self.own, self.got = scratch
-
-    def stages(self):
-        return [self.sides_begin, self.sides_second, self.sides_finish]
+        (self.d,), (self.o,) = ins, outs
+        self.own, self.got, self.q = scratch
+
+    def stages(self):
+        return [
+            self.sides_begin, self.sides_second, self.turn_over, self.plane_second,
+            self.plane_finish,
+        ]
 
     def sides_begin(self):
         n = self.net
-        src = self.d.at[:, :, :, columns((1 - n.half) * 384, 384)]
-        kept = self.d.at[:, :, :, columns(n.half * 384, 384)]
-        self.sent = [n.copy(src, self.got, rep=n.partner), n.move(kept, self.own)]
+        halves = [columns(h * 384, 384) for h in (0, 1)]
+        mine, rest = columns(n.half * 384, 384), columns((1 - n.half) * 384, 384)
+        if self.rep_first:
+            src = [self.d.at[f, :, :, rest] for f in (0, 1)]
+            kept = [self.d.at[f, :, :, mine] for f in (0, 1)]
+            device = {"rep": n.partner}
+        else:
+            src = [self.d.at[1 - n.far, :, :, h] for h in halves]
+            kept = [self.d.at[n.far, :, :, h] for h in halves]
+            device = {"seq": n.seq(2)}
+        self.sent = [n.copy(src[i], self.got.at[i], **device) for i in (0, 1)]
+        self.sent += [n.move(kept[i], self.own.at[i]) for i in (0, 1)]
 
     def sides_second(self):
         n = self.net
         wait_all(self.sent)
-        goes = 1 - n.far
+        self.stays = n.far if self.rep_first else n.half
+        device = {"seq": n.seq(2)} if self.rep_first else {"rep": n.partner}
+        goes = 1 - self.stays
         self.got[goes] = total(self.got[goes], self.own[goes])
-        self.sent = [n.copy(self.got.at[goes], self.q, seq=n.seq(2))]
-        self.got[n.far] = total(self.got[n.far], self.own[n.far])
-
-    def sides_finish(self):
+        self.sent = [n.copy(self.got.at[goes], self.q, **device)]
+        self.got[self.stays] = total(self.got[self.stays], self.own[self.stays])
+
+    def target(self):
+        return columns(self.net.half * 384, 384)
+
+    def turn_over(self):
         n = self.net
         wait_all(self.sent)
-        self.q[...] = total(self.q[...], self.got[n.far])
-
-
-class SecondPlane(Job):
-    space = pltpu.VMEM
-    inputs = ("q_second",)
-    shapes = ((EXPERTS, 128, D),)
-
-    def bind(self, ins, outs, scratch):
-        (self.q,), (self.o,) = ins, outs
-
-    def stages(self):
-        return [self.plane_begin, self.plane_second, self.plane_finish]
-
-    def plane_begin(self):
-        n = self.net
+        self.q[...] = total(self.q[...], self.got[self.stays])
         self.sent = []
-        dst = self.o.at[n.z, :, columns(n.half * 384, 384)]
+        dst = self.o.at[n.z, :, self.target()]
         for k in (2, 1, 3, 0):
             src = self.q.at[n.plane(k)]
             self.sent.append(n.move(src, dst) if k == 0 else n.copy(src, dst, fsdp=n.plane(k)))
@@ -566,18 +598,24 @@
         wait_all(self.sent)
 
 
-class SecondReturn(SecondSides, SecondPlane):
-    space = pl.ANY
-    out_space = pl.ANY
-    inputs = SecondSides.inputs
-    shapes = SecondPlane.shapes
-    scratch = SecondSides.scratch + SecondSides.shapes
-
-    def bind(self, ins, outs, scratch):
-        SecondSides.bind(self, ins, scratch[2:], scratch[:2])
-        SecondPlane.bind(self, scratch[2:], outs, ())
-
-    stages = FirstReturn.stages
+class SecondToPlane(SecondReturn):
+    shapes = ((EXPERTS, 128, 384),)
+
+    def stages(self):
+        return [self.sides_begin, self.sides_second, self.turn_over, self.plane_finish]
+
+    def target(self):
+        return pl.ds(0, 384)
+
+
+class SecondFinal(FirstFinal):
+    inputs = ("q_second",)
+    shapes = ((EXPERTS, 128, D),)
+
+    def begin(self):
+        n = self.net
+        part = self.o.at[:, :, columns(n.half * 384, 384)]
+        self.sent = [n.copy(self.q, part, rep=n.partner), n.move(self.q, part)]
 
 
 class SharedAcross(Job):
@@ -720,7 +758,7 @@
 
 
 class SmallReturnHere(Job):
-    inputs = ("small_rows",)
+    inputs = ("small_0", "gain_1", "small_1")
     space = pltpu.VMEM
     out_space = pltpu.VMEM
     kind = f32
@@ -729,7 +767,7 @@
     scratch = ((16, D), (16, D), (3, 16, D), (3, 16, D))
 
     def bind(self, ins, outs, scratch):
-        self.rows, self.gain = ins
+        self.zero, self.gain_one, self.one, self.gain = ins
         (self.out,) = outs
         self.acc, self.rx, self.rz, self.rs = scratch
 
@@ -738,8 +776,11 @@
 
     def begin(self):
         n = self.net
-        self.acc[...] = self.rows[...]
-        self.acc[0:8] += self.gain[...]
+        self.acc[12:16] = jnp.zeros((4, D), f32)
+        for at, gain, rest in ((0, self.gain, self.zero), (6, self.gain_one, self.one)):
+            self.acc[at : at + 1] = gain[0:1]
+            self.acc[at + 1 : at + 2] = rest[0:1]
+            self.acc[at + 2 : at + 6] = rest[8:12]
         self.copies = [n.copy(self.acc, self.rx, rep=n.partner)]
 
     def second_hop(self):
@@ -779,10 +820,8 @@
                 queue.pop(0)[1]()
 
     def drain(self):
-        while any(self.queues):
-            for queue in self.queues:
-                if queue:
-                    queue.pop(0)[1]()
+        for point in range(9, 30):
+            self.at(point)
 
 
 COPIES = 112
@@ -855,12 +894,6 @@
     return made[: len(outputs)], made[len(outputs) :]
 
 
-def prologue_kernel(net, ground):
-    net.greet(net.everyone())
-    net.met()
-    ground.drain()
-
-
 def rms_rows(x):
     return lax.rsqrt(jnp.mean(x * x, -1, keepdims=True) + EPS)
 
@@ -870,22 +903,41 @@
     return x * cosine + jnp.concatenate([x[:, half:], x[:, :half]], 1) * sine
 
 
-def attn_forward_kernel(
-    here, net, ground, h, gains, cosine, sine, *refs
-):
+def spread(small):
+    lane = lax.broadcasted_iota(jnp.int32, (128, D), 0)
+    col = lax.broadcasted_iota(jnp.int32, (128, D), 1)
+    out = jnp.zeros((16, D), f32)
+    for i in range(16):
+        place = jnp.where((col == lane + 48 * i) & (lane < 48), 1.0, 0.0).astype(bf16)
+        out = out + dot(small[i // 4, i % 4], place)
+    return out
+
+
+def attn_forward_kernel(here, net, ground, h, cosine, sine, *refs):
     if here:
-        w_qkv, w_out = ground.made[0][1]
+        w_qkv, w_out = ground.made[1][1]
+        small, *refs = refs
     else:
-        w_qkv, w_out, *refs = refs
+        gains, w_qkv, w_out, *refs = refs
     (
         middle, second, every, queries, keys, values, attended, totals,
         near_out, near_in, away_out, away_in,
     ) = refs
     net.greet(net.everyone())
-    x = h[...]
-    every[net.s] = (x * rms_rows(x) * gains[0:1, :]).astype(bf16)
-    net.met()
-    ground.at(0)
+    x = h[...].astype(f32)
+    factor = rms_rows(x)
+    if here:
+        net.met()
+        for point in (-2, -1, 0):
+            ground.at(point)
+        small[...] = spread(ground.made[0][1][0])
+        gain_one, gain_two = small[0:1, :], small[1:2, :]
+    else:
+        gain_one, gain_two = gains[0:1, :], gains[1:2, :]
+    every[net.s] = (x * factor * gain_one).astype(bf16)
+    if not here:
+        net.met()
+        ground.at(0)
     far = net.copy(every.at[net.s], every.at[net.s], seq=net.seq(2))
     near = net.copy(every.at[net.s], every.at[net.s], seq=net.seq(1))
     ground.at(1)
@@ -951,12 +1003,12 @@
     near_sum.wait_recv()
     away_out[...] = (away + near_in[1].astype(f32)).astype(bf16)
     away_sum = net.copy(away_out, away_in, seq=net.seq(2))
-    own = h[...] + own + near_in[0].astype(f32)
+    own = h[...].astype(f32) + own + near_in[0].astype(f32)
     ground.at(8)
     away_sum.wait_recv()
     own = own + away_in[...].astype(f32)
     middle[...] = own
-    second[...] = (own * rms_rows(own) * gains[1:2, :]).astype(bf16)
+    second[...] = (own * rms_rows(own) * gain_two).astype(bf16)
     for copy in (far, near, passed, near_sum, away_sum):
         copy.wait_send()
     ground.drain()
@@ -965,10 +1017,12 @@
 def attn_forward(h, gains, weights, tables, jobs, shards, cid):
     t = h.shape[0]
     head = (HEADS_DEV, SEQ, t, HEAD_DIM)
+    here = not weights
     return call(
-        functools.partial(attn_forward_kernel, not weights),
-        [h, gains, *tables, *weights],
-        [
+        functools.partial(attn_forward_kernel, here),
+        [h, *tables] if here else [h, *tables, gains, *weights],
+        ([((16, D), f32)] if here else [])
+        + [
             ((t, D), f32), ((t, D), bf16), ((SEQ, t, D), bf16, 1), (head, bf16, 1), (head, bf16, 1),
             (head, bf16, 1), (head, f32, 1), ((HEADS_DEV, SEQ, t, 128), f32, 1),
         ],
@@ -1188,7 +1242,7 @@
     t = grad.shape[0]
     net.greet(net.everyone())
     g0, g1 = gates[:, 0:1], gates[:, 1:2]
-    up = grad[...]
+    up = grad[...].astype(f32)
     pairs = jnp.concatenate([(up * g0).astype(bf16), (up * g1).astype(bf16)], 0)
     rows_out[...] = dot(chosen[...], pairs).astype(bf16).reshape(EXPERTS, CAP, D)
     every_g[net.s] = up.astype(bf16)
@@ -1421,7 +1475,7 @@
     ground.at(6)
     away_sum.wait_recv()
     net.need(h)
-    d_x, gain = norm_back(h[...], gains[0:1, :], own + away_in[...].astype(f32))
+    d_x, gain = norm_back(h[...].astype(f32), gains[0:1, :], own + away_in[...].astype(f32))
     grad[...] = up + d_x
     row = lax.broadcasted_iota(jnp.int32, (8, D), 0)
     d_gain[...] = jnp.where(row == 0, gain, 0.0)
@@ -1450,38 +1504,40 @@
 
 
 FORWARD_ATTN_FIRST = (
-    (AttnFetchHere, 0, (0, 1, 2, 3)),
-    (SharedFetch, 0, (2, 3, 6, 9)),
-    (ExpertFetch, 0, (4, 8, 9)),
+    (SmallFetch, 0, (-2, -1, 0)),
+    (AttnFetchHere, 0, (-2, -1, 2, 3)),
+    (ExpertFetch, 0, (-2, 5, 9)),
+    (SharedFetch, 0, (1, 4, 8, 10)),
+    (ExpertPlane, 1, (8, 11)),
 )
 FORWARD_FFN_FIRST = (
     (ExpertJoin, 0, (0, 3, 9)),
-    (AttnFetch, 1, (0, 1, 3, 9)),
-    (ExpertPlane, 1, (3, 9)),
+    (AttnFetch, 1, (0, 3, 6, 9)),
+    (ExpertNear, 1, (4, 9)),
 )
-FORWARD_ATTN = ((ExpertNear, 1, (1, 9)), (SharedFetch, 1, (1, 2, 5, 9)))
+FORWARD_ATTN = ((SharedFetch, 1, (0, 1, 4, 9)),)
 FORWARD_FFN = ((ExpertJoin, 1, (0, 3, 9)),)
 BACKWARD_FFN_FIRST = ((SharedAcross, 1, (3, 9)),)
 BACKWARD_ATTN = (
-    (GateSides, 1, (0, 3, 9)),
-    (UpSides, 1, (0, 3, 9)),
-    (SecondSides, 1, (0, 4, 9)),
-    (SharedReturn, 1, (0, 4, 5, 9)),
+    (GateToPlane, 1, (0, 2, 5, 12)),
+    (UpToPlane, 1, (0, 2, 5, 12)),
+    (SecondToPlane, 1, (2, 8, 10, 12)),
+    (SharedReturn, 1, (0, 4, 6, 11)),
 )
 BACKWARD_FFN = (
     (SharedAcross, 0, (3, 9)),
-    (AttnReturn, 1, (0, 2, 5, 8, 9)),
-    (GatePlane, 1, (3, 7, 9)),
-    (UpPlane, 1, (3, 8, 9)),
-    (SecondPlane, 1, (3, 7, 9)),
+    (AttnReturn, 1, (0, 3, 6, 8, 9)),
+    (GateFinal, 1, (0, 9)),
+    (UpFinal, 1, (0, 9)),
+    (SecondFinal, 1, (0, 9)),
 )
 BACKWARD_ATTN_LAST = (
-    (GateReturn, 0, (0, 3, 5, 9)),
-    (UpReturn, 0, (0, 3, 5, 9)),
-    (SecondReturn, 0, (0, 4, 6, 9)),
-    (SharedReturn, 0, (0, 4, 5, 9)),
-    (AttnReturnHere, 0, (6, 9)),
-    (SmallReturnHere, 0, (7, 9)),
+    (GateReturn, 0, (0, 2, 5, 10, 20)),
+    (UpReturn, 0, (0, 2, 5, 11, 20)),
+    (SharedReturn, 0, (0, 4, 6, 19)),
+    (SecondReturn, 0, (2, 8, 12, 15, 20)),
+    (AttnReturnHere, 0, (6, 9, 13, 14, 20)),
+    (SmallReturnHere, 0, (7, 8, 10, 13)),
 )
 
 
@@ -1491,13 +1547,13 @@
 ):
     r, s, z = lax.axis_index("rep"), lax.axis_index("seq"), lax.axis_index("fsdp")
     tokens = inputs.shape[1]
-    position = jnp.arange(SEQ * tokens, dtype=jnp.int32)
     half = HEAD_DIM // 2
-    inverse = jnp.exp(-jnp.log(10000.0) * jnp.arange(half, dtype=f32) * 2.0 / HEAD_DIM)
-    angle = position.astype(f32)[:, None] * inverse[None, :]
-    cosine, sine = jnp.cos(angle)[:, None, :], jnp.sin(angle)[:, None, :]
-    table_cos = jnp.concatenate([cosine, cosine], -1).reshape(SEQ, tokens, HEAD_DIM)
-    table_sin = jnp.concatenate([-sine, sine], -1).reshape(SEQ, tokens, HEAD_DIM)
+    inverse = np.exp(-np.log(np.float32(10000.0)) * np.arange(half, dtype=np.float32) * np.float32(2.0 / HEAD_DIM))
+    angle = np.arange(SEQ * tokens, dtype=np.float32)[:, None] * inverse.astype(np.float32)[None, :]
+    cosine, sine = np.cos(angle.astype(np.float64)), np.sin(angle.astype(np.float64))
+    shape = (SEQ, tokens, HEAD_DIM)
+    table_cos = jnp.asarray(np.concatenate([cosine, cosine], -1).reshape(shape), f32)
+    table_sin = jnp.asarray(np.concatenate([-sine, sine], -1).reshape(shape), f32)
     small = jnp.concatenate([norm_gains, router.transpose(0, 2, 1)], 1).reshape(12, 48)
     shards = {
         "small": jnp.pad(small, ((0, 4), (0, 80))),
@@ -1510,14 +1566,10 @@
         "expert_in": expert_in,
         "expert_out": expert_out,
     }
-    h = inputs[0].astype(f32)
+    h = inputs[0]
     kept_layers = []
-    _, (small,) = call(prologue_kernel, [], [], [], [(SmallFetch, 0, (0,))], shards, 11)
-    small = small.reshape(16, 16, 128)[:, :12, :48].transpose(1, 0, 2).reshape(LAYERS, 6, D)
-    gains = small[:, :2].astype(f32)
-    routers = small[:, 2:].transpose(0, 2, 1)
     tables = (table_cos, table_sin)
-    attn = ()
+    attn, gains, small = (), [None] * LAYERS, None
     for layer in range(LAYERS):
         first = layer == 0
         routes = routing(expert_choice[layer, 0], pair_order[layer, 0, 0])
@@ -1527,18 +1579,24 @@
             jobs = FORWARD_ATTN_FIRST
         else:
             jobs = FORWARD_ATTN
-        (middle, second, every_one, queries, keys, values, attended, totals), fetched = attn_forward(
-            h, gains[layer], attn, tables, jobs, shards, 12 + layer
-        )
+        outs, fetched = attn_forward(h, gains[layer], attn, tables, jobs, shards, 12 + layer)
+        if first:
+            small, *outs = outs
+            small = small[:12].reshape(LAYERS, 6, D)
+            gains = small[:, :2]
+            routers = small[:, 2:].astype(bf16).transpose(0, 2, 1)
+        middle, second, every_one, queries, keys, values, attended, totals = outs
         names = ("ax", "ay", "bx", "by")
         if first:
-            attn, shared, fetched = fetched[:2], fetched[2:4], fetched[4:]
             names = ("p1", "p2") + names
+            attn, shared, next_plane = fetched[1:3], fetched[9:11], fetched[11:]
+            shards.update(zip(names, fetched[3:9]))
         else:
-            fetched, shared = fetched[:4], fetched[4:]
-        shards.update(zip(names, fetched))
+            shared = fetched
         w_in, w_so = shared[0].reshape(2, D, FF_DEV), shared[1].reshape(FF_DEV, D)
         router_pad = jnp.pad(routers[layer], ((0, 0), (0, 124)))
+        if first:
+            shards["next_p1"], shards["next_p2"] = next_plane
         outs, fetched = ffn_forward(
             second, middle, router_pad, onehot, routes[1], w_in, w_so,
             FORWARD_FFN_FIRST if first else FORWARD_FFN, shards, 14 + layer,
@@ -1546,7 +1604,8 @@
         attn_weights, ffn_weights = attn, (w_in, w_so, fetched[0], fetched[1])
         if first:
             attn = fetched[2:4]
-            shards["p1"], shards["p2"] = fetched[4:]
+            shards["p1"], shards["p2"] = next_plane
+            shards.update(zip(names[2:], fetched[4:]))
         result, gates, gathered, every_two, joint, hidden, rows, joint_e, hidden_e = outs
         attn_saved = (h, every_one, queries, keys, values, attended, totals)
         ffn_saved = (
@@ -1556,8 +1615,7 @@
         h = result
         kept_layers.append((attn_weights, ffn_weights, attn_saved, ffn_saved, router_pad))
     output = h.astype(bf16)[None]
-    grad = cotangent[0].astype(f32)
-    smalls = [None] * LAYERS
+    grad = cotangent[0]
     returned = {}
     grads = {}
     for layer in reversed(range(LAYERS)):
@@ -1570,21 +1628,18 @@
         grads["r1"], grads["r2"] = done[:2]
         if last:
             returned["d_attn", 1], returned["d_expert", 1] = done[2:4], done[4:]
-        smalls[layer] = jnp.concatenate([small[:1], small[8:12]], 0)
-        if last:
-            rows = jnp.concatenate([jnp.zeros((1, D), f32), smalls[0], d_gain[:1], smalls[1]], 0)
-            grads["small_rows"] = jnp.pad(rows, ((0, 4), (0, 0)))
+        grads[f"small_{layer}"] = small
         (grad, d_gain, d_w_qkv, d_w_out), done = attn_backward(
             d_middle, attn_saved, gains[layer], attn_weights, tables,
             BACKWARD_ATTN_LAST if last else BACKWARD_ATTN, grads, 16 + layer,
         )
         if last:
-            returned["d_expert", 0], returned["d_shared", 0] = done[:3], done[3:5]
+            returned["d_expert", 0], returned["d_shared", 0] = [*done[:2], done[4]], done[2:4]
             returned["d_attn", 0], total_small = done[5:7], done[7]
         else:
             grads["q_gate"], grads["q_up"], grads["q_second"] = done[:3]
             returned["d_shared", 1] = done[3:]
-            grads["d_w_qkv"], grads["d_w_out"] = d_w_qkv, d_w_out
+            grads["d_w_qkv"], grads["d_w_out"], grads["gain_1"] = d_w_qkv, d_w_out, d_gain
     total_small = rep_rest(total_small, reps)[:12].reshape(LAYERS, 6, D)
     total_small = lax.dynamic_slice_in_dim(total_small, (s * FSDP + z) * 48, 48, 2)
 

time: 721 us -> 681 us (0.945)
  Pallas kernels: 666 us -> 638 us
    pallas_call x9 -> x8, Pallas kernels: 666 us -> 638 us  [call(): pl.pallas_call(body, out_shape=[jax.ShapeDtypeStruct(x[0], x[1]) for x in...]
where the time goes in v5:
time: 681 us; the launch traced here: 672 us
  Pallas kernels  638 us (94%)
  local copies, waits for them, and re-layouts  15.5 us (2%)
  other arithmetic  15 us (2%)
    pallas_call x8, Pallas kernels, call(): pl.pallas_call(body, out_shape=[jax.ShapeDtypeStruct(x[0], x[1]) for x in...  638 us

profile of v5, /device:TPU:8, one launch (start us, length us, event | category | flops | bytes accessed | tf_op | source)
XLA Modules:
  0.0 672.4 jit_solution(7787193232441239355)
XLA Ops:
  0.6 0.7 pad_maximum_fusion
  2.0 1.6 reshape.85
  3.9 1.4 reshape.86.refs_4_.refs_13_
  5.3 115.7 %shard_map.213 = (f32[16,768]{1,0:T(8,128)}, f32[256,768]{1,0:T(8,128)}, bf16[256,768]{1,0:T(8,128)(2,1)}, bf16[4,256,768]{2,1,0:T(8,128)(2,1)}, bf16[3,4,256,64...) custom-call(bf16[256,768]{1,0:T(8,128)(2,1)} %bitcast.91, ...), custom_call_target="tpu_custom_call" | custom-call | bytes 1048576 | tf_op jit(solution)/shard_map/pallas_call | solution.py:874
  121.0 0.8 reshape.87
  122.2 0.7 pad.12.refs_2_.refs_8_
  123.1 0.9 fusion.10.refs_3_.refs_2_
  125.5 1.0 fusion.refs_4_.refs_3_
  126.5 72.0 %shard_map.214 = (f32[256,768]{1,0:T(8,128)}, f32[256,128]{1,0:T(8,128)}, bf16[512,768]{1,0:T(8,128)(2,1)}, bf16[4,256,768]{2,1,0:T(8,128)(2,1)}, bf16[2,4,256,5...) custom-call(bf16[256,768]{1,0:T(8,128)(2,1)} %get-tuple-element.104., ...), custom_call_target="tpu_custom_call" | custom-call | bytes 1048576 | tf_op jit(solution)/shard_map/pallas_call | solution.py:874
  199.1 60.1 %shard_map.215 = (f32[256,768]{1,0:T(8,128)}, bf16[256,768]{1,0:T(8,128)(2,1)}, bf16[4,256,768]{2,1,0:T(8,128)(2,1)}, bf16[3,4,256,64]{3,2,1,0:T(8,128)(2,1)}, b...) custom-call(f32[256,768]{1,0:T(8,128)} %get-tuple-element.117.refs_0, ...), custom_call_target="tpu_custom_call" | custom-call | bytes 1048576 | tf_op jit(solution)/shard_map/pallas_call | solution.py:874
  259.2 0.7 pad.13.refs_2_.refs_8_
  260.1 0.9 fusion.11.refs_3_.refs_2_
  262.7 1.0 fusion.1.refs_4_.refs_3_
  263.7 56.3 %shard_map.216 = (f32[256,768]{1,0:T(8,128)}, f32[256,128]{1,0:T(8,128)}, bf16[512,768]{1,0:T(8,128)(2,1)}, bf16[4,256,768]{2,1,0:T(8,128)(2,1)}, bf16[2,4,256,5...) custom-call(bf16[256,768]{1,0:T(8,128)(2,1)} %get-tuple-element.120., ...), custom_call_target="tpu_custom_call" | custom-call | bytes 1048576 | tf_op jit(solution)/shard_map/pallas_call | solution.py:874
  320.0 1.9 convert_bitcast_fusion.1
  321.9 53.3 %shard_map.217 = (f32[256,768]{1,0:T(8,128)}, f32[16,768]{1,0:T(8,128)}, bf16[2,2,4,4,48,512]{5,4,3,2,1,0:T(8,128)(2,1)}, bf16[2,4,128,768]{3,2,1,0:T(8,128)(2,1...) custom-call(bf16[256,768]{1,0:T(8,128)(2,1)} %bitcast.103, f32[256,128]{1,0:T(8,128)} %get-tuple-element.129.refs_1_, ...), custom_call_target="tpu_custom_call" | custom-call | bytes 1048576 | tf_op jit(solution)/shard_map/pallas_call | solution.py:874
  375.2 77.5 %shard_map.218 = (f32[256,768]{1,0:T(8,128)}, f32[8,768]{1,0:T(8,128)}, bf16[4,4,48,576]{3,2,1,0:T(8,128)(2,1)}, bf16[4,48,768]{2,1,0:T(8,128)(2,1)}, bf16[4,48,...) custom-call(f32[256,768]{1,0:T(8,128)} %get-tuple-element.139.refs_0, ...), custom_call_target="tpu_custom_call" | custom-call | bytes 1048576 | tf_op jit(solution)/shard_map/pallas_call | solution.py:874
  452.7 79.1 %shard_map.219 = (f32[256,768]{1,0:T(8,128)}, f32[16,768]{1,0:T(8,128)}, bf16[2,2,4,4,48,512]{5,4,3,2,1,0:T(8,128)(2,1)}, bf16[2,4,128,768]{3,2,1,0:T(8,128)(2,1...) custom-call(f32[256,768]{1,0:T(8,128)} %get-tuple-element.150.refs_0, ...), custom_call_target="tpu_custom_call" | custom-call | bytes 1048576 | tf_op jit(solution)/shard_map/pallas_call | solution.py:874
  531.8 124.1 %shard_map.220 = (f32[256,768]{1,0:T(8,128)}, f32[8,768]{1,0:T(8,128)}, bf16[4,4,48,576]{3,2,1,0:T(8,128)(2,1)}, bf16[4,48,768]{2,1,0:T(8,128)(2,1)}, bf16[4,48,...) custom-call(f32[256,768]{1,0:T(8,128)} %get-tuple-element.166.refs_0, ...), custom_call_target="tpu_custom_call" | custom-call | bytes 1048576 | tf_op jit(solution)/shard_map/pallas_call | solution.py:874
  655.9 0.8 reshape.92
  656.7 0.7 constant_dynamic-slice_fusion
  657.6 1.1 stack.63
  658.7 0.8 convert_bitcast_fusion
  659.5 0.8 copy.54
  660.3 1.7 reshape.96
  662.0 0.7 maximum_convert_fusion.4
  662.7 0.7 dynamic-slice_bitcast_fusion
  663.4 1.2 maximum_convert_fusion.2
  664.7 0.9 maximum_convert_fusion.3
  666.1 3.0 maximum_convert_fusion
  669.2 1.9 maximum_convert_fusion.1
  671.0 0.9 copy.65
  (68 shorter events, 6.1 us)
Async XLA Ops:
  5.3 117.6 %copy-start.14 = (s32[2,1,256,2]{2,3,1,0:T(2,128)S(1)}, s32[2,1,256,2]{2,3,1,0:T(2,128)}, u32[]{:S(2)}) copy-start(s32[2,1,256,2]{2,3,1,0:T(2,128)} %param.15) | copy-start | bytes 12292
  121.0 3.0 copy-start.15
  531.8 125.6 %copy-start.9 = (bf16[4,48,576]{2,1,0:T(8,128)(2,1)S(1)}, bf16[4,48,576]{2,1,0:T(8,128)(2,1)}, u32[]{:S(2)}) copy-start(bf16[4,48,576]{2,1,0:T(8,128)(2,1)} %get-tuple-element.185) | copy-start | bytes 663556
  659.5 2.5 copy-start.12
  659.5 2.5 copy-start.13
  660.3 3.1 copy-start.7
  660.3 3.1 copy-start.8
  662.0 2.7 copy-start.10
  662.0 2.7 copy-start.11
  663.4 2.2 copy-start.1
  663.4 2.2 copy-start.2
  663.4 2.2 copy-start.4
  663.4 2.7 copy-start.5
  666.1 3.0 copy-start
  666.1 3.0 copy-start.3
  669.2 1.9 copy-start.6

commit v6 on v5

--- a/solution.py
+++ b/solution.py
@@ -263,6 +263,16 @@
         wait_all(self.copies)
 
 
+class JoinFirst(ExpertJoin):
+    inputs = ()
+    linked = ((2, 0), (2, 1), (2, 2), (2, 3), (2, 4), (2, 5))
+
+
+class JoinNext(ExpertJoin):
+    inputs = ("next_p1", "next_p2")
+    linked = ((0, 0), (0, 1), (0, 2), (0, 3))
+
+
 class SharedFetch(Job):
     inputs = ("shared_in", "shared_out")
     shapes = ((2, 4, 4, 48, FF_DEV), (4, 128, D))
@@ -806,6 +816,7 @@
         for job, layer, points in jobs:
             a, b, c = len(job.inputs), len(job.shapes), len(job.scratch)
             given = list(ins[:a]) + [own_outs[i] for i in getattr(job, "own", ())]
+            given += [self.made[i][1][k] for i, k in getattr(job, "linked", ())]
             made = job(net, layer, given, outs[:b], scratch[:c])
             self.made.append((made, outs[:b]))
             stages = made.stages()
@@ -820,11 +831,12 @@
                 queue.pop(0)[1]()
 
     def drain(self):
-        for point in range(9, 30):
+        for point in range(9, 70):
             self.at(point)
 
 
-COPIES = 112
+COPIES = 160
+MOVES = 64
 
 
 class Late:
@@ -869,6 +881,7 @@
         ground = Background(net, jobs, refs[a:b], outs + list(refs[d:e]), refs[c:d], refs[e:f])
         kernel(net, ground, *ins, *outs, *refs[d:e])
         assert not net.coming and not there
+        assert net.count <= COPIES and net.local_count <= MOVES
         wait_all(net.going)
 
     made = pl.pallas_call(
@@ -884,7 +897,7 @@
         + [
             pltpu.SemaphoreType.DMA((COPIES,)),
             pltpu.SemaphoreType.DMA((COPIES,)),
-            pltpu.SemaphoreType.DMA((56,)),
+            pltpu.SemaphoreType.DMA((MOVES,)),
         ],
         compiler_params=pltpu.CompilerParams(
             collective_id=cid, has_side_effects=True, vmem_limit_bytes=60 << 20
@@ -913,16 +926,12 @@
     return out
 
 
-def attn_forward_kernel(here, net, ground, h, cosine, sine, *refs):
-    if here:
-        w_qkv, w_out = ground.made[1][1]
-        small, *refs = refs
-    else:
-        gains, w_qkv, w_out, *refs = refs
+def attn_forward_part(layer, net, ground, h, cosine, sine, small, w_qkv, w_out, refs):
     (
         middle, second, every, queries, keys, values, attended, totals,
         near_out, near_in, away_out, away_in,
     ) = refs
+    here = layer == 0
     net.greet(net.everyone())
     x = h[...].astype(f32)
     factor = rms_rows(x)
@@ -931,9 +940,7 @@
         for point in (-2, -1, 0):
             ground.at(point)
         small[...] = spread(ground.made[0][1][0])
-        gain_one, gain_two = small[0:1, :], small[1:2, :]
-    else:
-        gain_one, gain_two = gains[0:1, :], gains[1:2, :]
+    gain_one, gain_two = small[6 * layer : 6 * layer + 1, :], small[6 * layer + 1 : 6 * layer + 2, :]
     every[net.s] = (x * factor * gain_one).astype(bf16)
     if not here:
         net.met()
@@ -1011,24 +1018,6 @@
     second[...] = (own * rms_rows(own) * gain_two).astype(bf16)
     for copy in (far, near, passed, near_sum, away_sum):
         copy.wait_send()
-    ground.drain()
-
-
-def attn_forward(h, gains, weights, tables, jobs, shards, cid):
-    t = h.shape[0]
-    head = (HEADS_DEV, SEQ, t, HEAD_DIM)
-    here = not weights
-    return call(
-        functools.partial(attn_forward_kernel, here),
-        [h, *tables] if here else [h, *tables, gains, *weights],
-        ([((16, D), f32)] if here else [])
-        + [
-            ((t, D), f32), ((t, D), bf16), ((SEQ, t, D), bf16, 1), (head, bf16, 1), (head, bf16, 1),
-            (head, bf16, 1), (head, f32, 1), ((HEADS_DEV, SEQ, t, 128), f32, 1),
-        ],
-        [((2, t, D), bf16), ((2, t, D), bf16), ((t, D), bf16), ((t, D), bf16)],
-        jobs, shards, cid,
-    )
 
 
 def silu_gate(g, u):
@@ -1102,49 +1091,52 @@
             copy.wait_send()
 
 
-def ffn_forward_kernel(
-    net, ground, second, middle, router, onehot, chosen, w_in, w_so,
-    result, gates, gathered, every, joint, hidden, rows, joint_e, hidden_e,
-    rows_out, prod_out, prod_in, prod_own, back_out, yields, near_out, near_in, away_out, away_in,
-):
+def ffn_forward_part(layer, net, ground, second, middle, small, onehot, chosen, jobs, refs):
+    (
+        result, gates, gathered, every, joint, hidden, rows, joint_e, hidden_e,
+        rows_out, prod_out, prod_in, prod_own, back_out, yields, near_out, near_in, away_out,
+        away_in, w_in, w_so, router,
+    ) = refs
     t = second.shape[0]
-    w1, w2 = ground.made[0][0].w1, ground.made[0][0].w2
-    net.greet(net.everyone())
+    shared_job, join = jobs
+    w1, w2 = join.w1, join.w2
     picked = chosen[:, :t] + chosen[:, t:]
     rows_out[...] = dot(picked, second[...]).astype(bf16).reshape(EXPERTS, CAP, D)
     every[net.s] = second[...]
-    net.met()
     trip = SlotTrip(net, rows_out, rows)
     far = net.copy(every.at[net.s], every.at[net.s], seq=net.seq(2))
     near = net.copy(every.at[net.s], every.at[net.s], seq=net.seq(1))
-    ground.at(0)
-    logits = dot(second[...], router[...])
-    l0 = jnp.sum(onehot[0] * logits, -1, keepdims=True)
-    l1 = jnp.sum(onehot[1] * logits, -1, keepdims=True)
+    ground.at(30)
+    loads = [net.move(shared_job.w_in, w_in), net.move(shared_job.w_out, w_so)]
+    router[4:8, :] = jnp.zeros((4, D), f32)
+    router[0:4, :] = small[6 * layer + 2 : 6 * layer + 6, :]
+    logits = dot_nt(second[...], router[...].astype(bf16))
+    l0 = jnp.sum(onehot[0, :, 0:8] * logits, -1, keepdims=True)
+    l1 = jnp.sum(onehot[1, :, 0:8] * logits, -1, keepdims=True)
     top = jnp.maximum(l0, l1)
     e0, e1 = jnp.exp(l0 - top), jnp.exp(l1 - top)
     g0, g1 = e0 / (e0 + e1), e1 / (e0 + e1)
     lane = lax.broadcasted_iota(jnp.int32, (t, 128), 1)
     gates[...] = jnp.where(lane == 0, g0, jnp.where(lane == 1, g1, 0.0))
-    net.need(w_in, w_so)
+    wait_all(loads)
 
     def shared(b):
-        g, u = dot(every[b], w_in[0]), dot(every[b], w_in[1])
+        g, u = dot(every[b], w_in[0].reshape(D, FF_DEV)), dot(every[b], w_in[1].reshape(D, FF_DEV))
         joint[0, b] = g.astype(bf16)
         joint[1, b] = u.astype(bf16)
         low = silu_gate(g, u).astype(bf16)
         hidden[b] = low
-        return dot(low, w_so[...])
+        return dot(low, w_so[...].reshape(FF_DEV, D))
 
     own_part = shared(net.s)
-    ground.at(1)
+    ground.at(31)
     near.wait_recv()
     near_out[0] = shared(net.seq(1)).astype(bf16)
     far.wait_recv()
     passed_far = net.copy(every.at[net.seq(2)], every.at[net.seq(2)], seq=net.seq(1))
     away_out[...] = shared(net.seq(2)).astype(bf16)
     trip.hand_on(0)
-    ground.at(2)
+    ground.at(32)
     passed_far.wait_recv()
     near_out[1] = shared(net.seq(3)).astype(bf16)
     near_sum = net.copy(near_out, near_in, seq=net.seq(1))
@@ -1168,22 +1160,21 @@
         return total
 
     trip.here(0)
-    ground.at(3)
+    ground.at(33)
     back = SlotReturn(net, prod_out, prod_in, prod_own, back_out, yields)
     back.other(0, expert(1 - net.core, 0))
     trip.hand_on(1)
     near_sum.wait_recv()
     away_out[...] = (away_out[...].astype(f32) + near_in[1].astype(f32)).astype(bf16)
     away_sum = net.copy(away_out, away_in, seq=net.seq(2))
-    ground.at(4)
+    ground.at(34)
     back.mine(0, expert(net.core, 0))
-    ground.at(5)
+    ground.at(35)
     trip.here(1)
     back.other(1, expert(1 - net.core, 1))
     back.mine(1, expert(net.core, 1))
     net.done(rows, joint_e, hidden_e)
-    ground.at(6)
-    net.need(middle)
+    ground.at(36)
     away_sum.wait_recv()
     base = middle[...] + own_part + near_in[0].astype(f32) + away_in[...].astype(f32)
     back.wait()
@@ -1194,26 +1185,49 @@
         copy.wait_send()
     trip.close()
     back.close()
+
+
+def layer_forward_kernel(layer, places, net, ground, h, cosine, sine, onehot, chosen, *refs):
+    if layer == 0:
+        small, *refs = refs
+        w_qkv, w_out = ground.made[1][1]
+    else:
+        small, w_qkv, w_out, *refs = refs
+    attn, ffn = refs[:8] + refs[17:21], refs[8:17] + refs[21:]
+    attn_forward_part(layer, net, ground, h, cosine, sine, small, w_qkv, w_out, attn)
+    jobs = [ground.made[i][0] for i in places]
+    ffn_forward_part(layer, net, ground, attn[1], attn[0], small, onehot, chosen, jobs, ffn)
     ground.drain()
 
 
-def ffn_forward(second, middle, router, onehot, chosen, w_in, w_so, jobs, shards, cid):
-    t = second.shape[0]
+def layer_forward(layer, h, tables, onehot, chosen, small, weights, jobs, shards, cid):
+    t = h.shape[0]
+    head = (HEADS_DEV, SEQ, t, HEAD_DIM)
     slots = (EXPERTS, CAP, FF_DEV)
+    sums = [((2, t, D), bf16), ((2, t, D), bf16), ((t, D), bf16), ((t, D), bf16)]
+    names = [job.__name__ for job, *_ in jobs]
+    places = (names.index("SharedFetch"), names.index("JoinNext" if layer else "JoinFirst"))
     return call(
-        ffn_forward_kernel,
-        [second, Late(middle), router, onehot, chosen, Late(w_in), Late(w_so)],
-        [
+        functools.partial(layer_forward_kernel, layer, places),
+        [h, *tables, onehot, chosen] + ([small, *weights] if layer else []),
+        ([] if layer else [((16, D), f32)])
+        + [
+            ((t, D), f32), ((t, D), bf16), ((SEQ, t, D), bf16, 1), (head, bf16, 1), (head, bf16, 1),
+            (head, bf16, 1), (head, f32, 1), ((HEADS_DEV, SEQ, t, 128), f32, 1),
+        ]
+        + [
             ((t, D), f32), ((t, 128), f32), ((2 * t, D), bf16), ((SEQ, t, D), bf16, 1),
             ((2, SEQ, t, FF_DEV), bf16, 1), ((SEQ, t, FF_DEV), bf16, 1),
             ((2, EXPERTS, CAP, D), bf16, 1), ((2, 2, 2, *slots), bf16, 1), ((2, 2, *slots), bf16, 1),
         ],
-        [
+        sums
+        + [
             ((EXPERTS, CAP, D), bf16), ((EXPERTS, CAP, D), bf16), ((EXPERTS, CAP, D), bf16),
             ((EXPERTS * CHUNKS[0][1], D), f32), ((EXPERTS, CAP, D), bf16),
-            ((EXPERTS, CAP, D), bf16), ((2, t, D), bf16), ((2, t, D), bf16), ((t, D), bf16),
-            ((t, D), bf16),
-        ],
+            ((EXPERTS, CAP, D), bf16),
+        ]
+        + sums
+        + [((2, 4, 4, 48, FF_DEV), bf16), ((4, 128, D), bf16), ((8, D), f32)],
         jobs, shards, cid,
     )
 
@@ -1503,20 +1517,20 @@
     )
 
 
-FORWARD_ATTN_FIRST = (
+FORWARD_FIRST = (
     (SmallFetch, 0, (-2, -1, 0)),
     (AttnFetchHere, 0, (-2, -1, 2, 3)),
-    (ExpertFetch, 0, (-2, 5, 9)),
-    (SharedFetch, 0, (1, 4, 8, 10)),
-    (ExpertPlane, 1, (8, 11)),
+    (ExpertFetch, 0, (-2, 3, 30)),
+    (SharedFetch, 0, (1, 3, 7, 30)),
+    (JoinFirst, 0, (30, 33, 39)),
+    (ExpertPlane, 1, (8, 40)),
+    (AttnFetch, 1, (30, 33, 36, 40)),
 )
-FORWARD_FFN_FIRST = (
-    (ExpertJoin, 0, (0, 3, 9)),
-    (AttnFetch, 1, (0, 3, 6, 9)),
-    (ExpertNear, 1, (4, 9)),
+FORWARD_NEXT = (
+    (ExpertNear, 1, (2, 30)),
+    (SharedFetch, 1, (0, 1, 4, 30)),
+    (JoinNext, 1, (30, 33, 39)),
 )
-FORWARD_ATTN = ((SharedFetch, 1, (0, 1, 4, 9)),)
-FORWARD_FFN = ((ExpertJoin, 1, (0, 3, 9)),)
 BACKWARD_FFN_FIRST = ((SharedAcross, 1, (3, 9)),)
 BACKWARD_ATTN = (
     (GateToPlane, 1, (0, 2, 5, 12)),
@@ -1575,38 +1589,26 @@
         routes = routing(expert_choice[layer, 0], pair_order[layer, 0, 0])
         onehot = expert_choice[layer, 0].T[..., None] == jnp.arange(128, dtype=jnp.int32)
         onehot = onehot.astype(f32)
-        if first:
-            jobs = FORWARD_ATTN_FIRST
-        else:
-            jobs = FORWARD_ATTN
-        outs, fetched = attn_forward(h, gains[layer], attn, tables, jobs, shards, 12 + layer)
+        outs, fetched = layer_forward(
+            layer, h, tables, onehot, routes[1], small, attn, FORWARD_FIRST if first else FORWARD_NEXT,
+            shards, 12 + layer,
+        )
         if first:
             small, *outs = outs
-            small = small[:12].reshape(LAYERS, 6, D)
-            gains = small[:, :2]
-            routers = small[:, 2:].astype(bf16).transpose(0, 2, 1)
-        middle, second, every_one, queries, keys, values, attended, totals = outs
-        names = ("ax", "ay", "bx", "by")
+            spread_small = small[:12].reshape(LAYERS, 6, D)
+            gains, routers = spread_small[:, :2], spread_small[:, 2:].astype(bf16)
+            attn, shared, w1, w2 = fetched[1:3], fetched[9:11], fetched[11], fetched[12]
+            shards["next_p1"], shards["next_p2"] = fetched[13:15]
+            next_attn = fetched[15:17]
+        else:
+            shared, w1, w2 = fetched[4:6], fetched[6], fetched[7]
+        middle, second, every_one, queries, keys, values, attended, totals = outs[:8]
+        result, gates, gathered, every_two, joint, hidden, rows, joint_e, hidden_e = outs[8:]
+        w_in, w_so = shared[0].reshape(2, D, FF_DEV), shared[1].reshape(FF_DEV, D)
+        router_pad = jnp.pad(routers[layer].T, ((0, 0), (0, 124)))
+        attn_weights, ffn_weights = attn, (w_in, w_so, w1, w2)
         if first:
-            names = ("p1", "p2") + names
-            attn, shared, next_plane = fetched[1:3], fetched[9:11], fetched[11:]
-            shards.update(zip(names, fetched[3:9]))
-        else:
-            shared = fetched
-        w_in, w_so = shared[0].reshape(2, D, FF_DEV), shared[1].reshape(FF_DEV, D)
-        router_pad = jnp.pad(routers[layer], ((0, 0), (0, 124)))
-        if first:
-            shards["next_p1"], shards["next_p2"] = next_plane
-        outs, fetched = ffn_forward(
-            second, middle, router_pad, onehot, routes[1], w_in, w_so,
-            FORWARD_FFN_FIRST if first else FORWARD_FFN, shards, 14 + layer,
-        )
-        attn_weights, ffn_weights = attn, (w_in, w_so, fetched[0], fetched[1])
-        if first:
-            attn = fetched[2:4]
-            shards["p1"], shards["p2"] = next_plane
-            shards.update(zip(names[2:], fetched[4:]))
-        result, gates, gathered, every_two, joint, hidden, rows, joint_e, hidden_e = outs
+            attn = next_attn
         attn_saved = (h, every_one, queries, keys, values, attended, totals)
         ffn_saved = (
             gates, onehot, routes[1], gathered, middle, second, every_two, joint, hidden, rows,

time: 681 us -> 659 us (0.968)
  Pallas kernels: 638 us -> 616 us
    pallas_call x8 -> x6, Pallas kernels: 638 us -> 616 us  [call(): pl.pallas_call(body, out_shape=[jax.ShapeDtypeStruct(x[0], x[1]) for x in...]
where the time goes in v6:
time: 659 us; the launch traced here: 649 us
  Pallas kernels  616 us (93%)
  local copies, waits for them, and re-layouts  15.2 us (2%)
  other arithmetic  14.1 us (2%)
    pallas_call x6, Pallas kernels, call(): pl.pallas_call(body, out_shape=[jax.ShapeDtypeStruct(x[0], x[1]) for x in...  616 us

profile of v6, /device:TPU:8, one launch (start us, length us, event | category | flops | bytes accessed | tf_op | source)
XLA Modules:
  0.0 648.8 jit_solution(16595221029871154756)
XLA Ops:
  0.7 0.8 fusion.21
  1.7 0.9 fusion.10.refs_3_.refs_2_
  2.5 0.7 fusion.20
  4.7 1.0 fusion.refs_4_.refs_3_
  5.7 0.6 pad.11.refs_5_
  6.3 0.6 reshape.85
  7.2 1.4 reshape.86.refs_6_.refs_14_
  8.6 166.4 %shard_map.213 = (f32[16,768]{1,0:T(8,128)}, f32[256,768]{1,0:T(8,128)}, bf16[256,768]{1,0:T(8,128)(2,1)}, bf16[4,256,768]{2,1,0:T(8,128)(2,1)}, bf16[3,4,256,64...) custom-call(bf16[256,768]{1,0:T(8,128)(2,1)} %bitcast.88, ...), custom_call_target="tpu_custom_call" | custom-call | bytes 1048576 | tf_op jit(solution)/shard_map/pallas_call | solution.py:887
  175.2 0.9 fusion.11.refs_3_.refs_2_
  177.5 1.0 fusion.1.refs_4_.refs_3_
  178.5 113.4 %shard_map.214 = (f32[256,768]{1,0:T(8,128)}, bf16[256,768]{1,0:T(8,128)(2,1)}, bf16[4,256,768]{2,1,0:T(8,128)(2,1)}, bf16[3,4,256,64]{3,2,1,0:T(8,128)(2,1)}, b...) custom-call(f32[256,768]{1,0:T(8,128)} %get-tuple-element.94.refs_0_, ...), custom_call_target="tpu_custom_call" | custom-call | bytes 1048576 | tf_op jit(solution)/shard_map/pallas_call | solution.py:887
  291.9 1.9 convert_bitcast_fusion.1
  293.8 0.6 slice_bitcast_fusion.2
  294.8 0.7 pad.12.refs_8_
  295.6 55.5 %shard_map.215 = (f32[256,768]{1,0:T(8,128)}, f32[16,768]{1,0:T(8,128)}, bf16[2,2,4,4,48,512]{5,4,3,2,1,0:T(8,128)(2,1)}, bf16[2,4,128,768]{3,2,1,0:T(8,128)(2,1...) custom-call(bf16[256,768]{1,0:T(8,128)(2,1)} %bitcast.101, f32[256,128]{1,0:T(8,128)} %get-tuple-element.101.refs_1_, ...), custom_call_target="tpu_custom_call" | custom-call | bytes 1048576 | tf_op jit(solution)/shard_map/pallas_call | solution.py:887
  351.1 78.1 %shard_map.216 = (f32[256,768]{1,0:T(8,128)}, f32[8,768]{1,0:T(8,128)}, bf16[4,4,48,576]{3,2,1,0:T(8,128)(2,1)}, bf16[4,48,768]{2,1,0:T(8,128)(2,1)}, bf16[4,48,...) custom-call(f32[256,768]{1,0:T(8,128)} %get-tuple-element.115.refs_0, ...), custom_call_target="tpu_custom_call" | custom-call | bytes 1048576 | tf_op jit(solution)/shard_map/pallas_call | solution.py:887
  429.2 0.7 pad.13.refs_8_
  430.0 81.7 %shard_map.217 = (f32[256,768]{1,0:T(8,128)}, f32[16,768]{1,0:T(8,128)}, bf16[2,2,4,4,48,512]{5,4,3,2,1,0:T(8,128)(2,1)}, bf16[2,4,128,768]{3,2,1,0:T(8,128)(2,1...) custom-call(f32[256,768]{1,0:T(8,128)} %get-tuple-element.126.refs_0, ...), custom_call_target="tpu_custom_call" | custom-call | bytes 1048576 | tf_op jit(solution)/shard_map/pallas_call | solution.py:887
  511.7 121.0 %shard_map.218 = (f32[256,768]{1,0:T(8,128)}, f32[8,768]{1,0:T(8,128)}, bf16[4,4,48,576]{3,2,1,0:T(8,128)(2,1)}, bf16[4,48,768]{2,1,0:T(8,128)(2,1)}, bf16[4,48,...) custom-call(f32[256,768]{1,0:T(8,128)} %get-tuple-element.146.refs_0, ...), custom_call_target="tpu_custom_call" | custom-call | bytes 1048576 | tf_op jit(solution)/shard_map/pallas_call | solution.py:887
  632.7 0.8 reshape.92
  633.5 0.7 constant_dynamic-slice_fusion
  634.3 1.1 stack.63
  635.5 0.6 convert_bitcast_fusion
  636.0 0.8 copy.42
  636.8 1.7 reshape.96
  638.5 0.7 maximum_convert_fusion.4
  639.3 0.7 dynamic-slice_bitcast_fusion
  640.0 1.2 maximum_convert_fusion.2
  641.2 0.9 maximum_convert_fusion.3
  642.6 3.0 maximum_convert_fusion
  645.7 1.9 maximum_convert_fusion.1
  647.6 0.9 copy.50
  (69 shorter events, 4.8 us)
Async XLA Ops:
  0.6 5.0 copy-start.16
  0.7 5.0 copy-start.17
  0.7 5.7 copy-start.7
  178.5 115.3 %copy-start.11 = (f32[16,768]{1,0:T(8,128)S(1)}, f32[16,768]{1,0:T(8,128)}, u32[]{:S(2)}) copy-start(f32[16,768]{1,0:T(8,128)} %get-tuple-element.95.refs_5_) | copy-start | bytes 147460
  511.7 122.5 %copy-start.10 = (bf16[4,48,576]{2,1,0:T(8,128)(2,1)S(1)}, bf16[4,48,576]{2,1,0:T(8,128)(2,1)}, u32[]{:S(2)}) copy-start(bf16[4,48,576]{2,1,0:T(8,128)(2,1)} %get-tuple-element.165) | copy-start | bytes 663556
  636.0 2.5 copy-start.14
  636.0 2.5 copy-start.15
  636.8 3.1 copy-start.8
  636.8 3.1 copy-start.9
  638.5 2.7 copy-start.12
  638.5 2.7 copy-start.13
  639.9 2.2 copy-start.1
  639.9 2.2 copy-start.2
  639.9 2.2 copy-start.4
  639.9 2.7 copy-start.5
  642.6 3.0 copy-start
  642.6 3.0 copy-start.3
  645.7 1.9 copy-start.6

commit v7 on v6

--- a/solution.py
+++ b/solution.py
@@ -1546,12 +1546,12 @@
     (SecondFinal, 1, (0, 9)),
 )
 BACKWARD_ATTN_LAST = (
-    (GateReturn, 0, (0, 2, 5, 10, 20)),
-    (UpReturn, 0, (0, 2, 5, 11, 20)),
-    (SharedReturn, 0, (0, 4, 6, 19)),
-    (SecondReturn, 0, (2, 8, 12, 15, 20)),
-    (AttnReturnHere, 0, (6, 9, 13, 14, 20)),
-    (SmallReturnHere, 0, (7, 8, 10, 13)),
+    (GateReturn, 0, (0, 3, 5, 9, 11)),
+    (UpReturn, 0, (0, 3, 5, 9, 11)),
+    (SharedReturn, 0, (0, 4, 5, 11)),
+    (SecondReturn, 0, (0, 4, 6, 9, 11)),
+    (AttnReturnHere, 0, (6, 9, 10, 11, 12)),
+    (SmallReturnHere, 0, (7, 8, 9, 10)),
 )
 
 

time: 659 us -> 644 us (0.977)
  Pallas kernels: 616 us -> 601 us
    pallas_call x6, Pallas kernels: 616 us -> 601 us  [call(): pl.pallas_call(body, out_shape=[jax.ShapeDtypeStruct(x[0], x[1]) for x in...]
where the time goes in v7:
time: 644 us; the launch traced here: 633 us
  Pallas kernels  601 us (93%)
  local copies, waits for them, and re-layouts  15.2 us (2%)
  other arithmetic  14.1 us (2%)
    pallas_call x6, Pallas kernels, call(): pl.pallas_call(body, out_shape=[jax.ShapeDtypeStruct(x[0], x[1]) for x in...  601 us

profile of v7, /device:TPU:8, one launch (start us, length us, event | category | flops | bytes accessed | tf_op | source)
XLA Modules:
  0.0 633.3 jit_solution(14101604561189520708)
XLA Ops:
  0.7 0.8 fusion.21
  1.7 0.9 fusion.10.refs_3_.refs_2_
  2.5 0.7 fusion.20
  4.7 1.0 fusion.refs_4_.refs_3_
  5.7 0.6 pad.11.refs_5_
  6.3 0.6 reshape.85
  7.2 1.4 reshape.86.refs_6_.refs_14_
  8.6 166.4 %shard_map.213 = (f32[16,768]{1,0:T(8,128)}, f32[256,768]{1,0:T(8,128)}, bf16[256,768]{1,0:T(8,128)(2,1)}, bf16[4,256,768]{2,1,0:T(8,128)(2,1)}, bf16[3,4,256,64...) custom-call(bf16[256,768]{1,0:T(8,128)(2,1)} %bitcast.88, ...), custom_call_target="tpu_custom_call" | custom-call | bytes 1048576 | tf_op jit(solution)/shard_map/pallas_call | solution.py:887
  175.2 0.9 fusion.11.refs_3_.refs_2_
  177.5 1.0 fusion.1.refs_4_.refs_3_
  178.5 113.4 %shard_map.214 = (f32[256,768]{1,0:T(8,128)}, bf16[256,768]{1,0:T(8,128)(2,1)}, bf16[4,256,768]{2,1,0:T(8,128)(2,1)}, bf16[3,4,256,64]{3,2,1,0:T(8,128)(2,1)}, b...) custom-call(f32[256,768]{1,0:T(8,128)} %get-tuple-element.94.refs_0_, ...), custom_call_target="tpu_custom_call" | custom-call | bytes 1048576 | tf_op jit(solution)/shard_map/pallas_call | solution.py:887
  291.9 1.9 convert_bitcast_fusion.1
  293.8 0.6 slice_bitcast_fusion.2
  294.8 0.7 pad.12.refs_8_
  295.6 55.5 %shard_map.215 = (f32[256,768]{1,0:T(8,128)}, f32[16,768]{1,0:T(8,128)}, bf16[2,2,4,4,48,512]{5,4,3,2,1,0:T(8,128)(2,1)}, bf16[2,4,128,768]{3,2,1,0:T(8,128)(2,1...) custom-call(bf16[256,768]{1,0:T(8,128)(2,1)} %bitcast.101, f32[256,128]{1,0:T(8,128)} %get-tuple-element.101.refs_1_, ...), custom_call_target="tpu_custom_call" | custom-call | bytes 1048576 | tf_op jit(solution)/shard_map/pallas_call | solution.py:887
  351.1 78.1 %shard_map.216 = (f32[256,768]{1,0:T(8,128)}, f32[8,768]{1,0:T(8,128)}, bf16[4,4,48,576]{3,2,1,0:T(8,128)(2,1)}, bf16[4,48,768]{2,1,0:T(8,128)(2,1)}, bf16[4,48,...) custom-call(f32[256,768]{1,0:T(8,128)} %get-tuple-element.115.refs_0, ...), custom_call_target="tpu_custom_call" | custom-call | bytes 1048576 | tf_op jit(solution)/shard_map/pallas_call | solution.py:887
  429.2 0.7 pad.13.refs_8_
  430.0 81.7 %shard_map.217 = (f32[256,768]{1,0:T(8,128)}, f32[16,768]{1,0:T(8,128)}, bf16[2,2,4,4,48,512]{5,4,3,2,1,0:T(8,128)(2,1)}, bf16[2,4,128,768]{3,2,1,0:T(8,128)(2,1...) custom-call(f32[256,768]{1,0:T(8,128)} %get-tuple-element.126.refs_0, ...), custom_call_target="tpu_custom_call" | custom-call | bytes 1048576 | tf_op jit(solution)/shard_map/pallas_call | solution.py:887
  511.7 105.5 %shard_map.218 = (f32[256,768]{1,0:T(8,128)}, f32[8,768]{1,0:T(8,128)}, bf16[4,4,48,576]{3,2,1,0:T(8,128)(2,1)}, bf16[4,48,768]{2,1,0:T(8,128)(2,1)}, bf16[4,48,...) custom-call(f32[256,768]{1,0:T(8,128)} %get-tuple-element.146.refs_0, ...), custom_call_target="tpu_custom_call" | custom-call | bytes 1048576 | tf_op jit(solution)/shard_map/pallas_call | solution.py:887
  617.2 0.8 reshape.92
  618.0 0.7 constant_dynamic-slice_fusion
  618.8 1.1 stack.63
  620.0 0.6 convert_bitcast_fusion
  620.6 0.8 copy.42
  621.3 1.7 reshape.96
  623.0 0.7 maximum_convert_fusion.4
  623.8 0.7 dynamic-slice_bitcast_fusion
  624.5 1.2 maximum_convert_fusion.2
  625.7 0.9 maximum_convert_fusion.3
  627.1 3.0 maximum_convert_fusion
  630.2 1.9 maximum_convert_fusion.1
  632.1 0.9 copy.50
  (69 shorter events, 4.8 us)
Async XLA Ops:
  0.6 5.0 copy-start.16
  0.7 5.0 copy-start.17
  0.7 5.7 copy-start.7
  178.5 115.3 %copy-start.11 = (f32[16,768]{1,0:T(8,128)S(1)}, f32[16,768]{1,0:T(8,128)}, u32[]{:S(2)}) copy-start(f32[16,768]{1,0:T(8,128)} %get-tuple-element.95.refs_5_) | copy-start | bytes 147460
  511.7 107.0 %copy-start.10 = (bf16[4,48,576]{2,1,0:T(8,128)(2,1)S(1)}, bf16[4,48,576]{2,1,0:T(8,128)(2,1)}, u32[]{:S(2)}) copy-start(bf16[4,48,576]{2,1,0:T(8,128)(2,1)} %get-tuple-element.165) | copy-start | bytes 663556
  620.5 2.5 copy-start.14
  620.5 2.5 copy-start.15
  621.3 3.1 copy-start.8
  621.3 3.1 copy-start.9
  623.0 2.7 copy-start.12
  623.0 2.7 copy-start.13
  624.4 2.2 copy-start.1
  624.4 2.2 copy-start.2
  624.4 2.2 copy-start.4
  624.5 2.7 copy-start.5
  627.1 3.0 copy-start
  627.1 3.0 copy-start.3
  630.2 1.9 copy-start.6

commit v8 on v7

--- a/solution.py
+++ b/solution.py
@@ -1533,10 +1533,10 @@
 )
 BACKWARD_FFN_FIRST = ((SharedAcross, 1, (3, 9)),)
 BACKWARD_ATTN = (
-    (GateToPlane, 1, (0, 2, 5, 12)),
-    (UpToPlane, 1, (0, 2, 5, 12)),
-    (SecondToPlane, 1, (2, 8, 10, 12)),
-    (SharedReturn, 1, (0, 4, 6, 11)),
+    (GateToPlane, 1, (0, 3, 5, 9)),
+    (UpToPlane, 1, (0, 3, 5, 9)),
+    (SecondToPlane, 1, (0, 4, 6, 9)),
+    (SharedReturn, 1, (0, 4, 5, 9)),
 )
 BACKWARD_FFN = (
     (SharedAcross, 0, (3, 9)),

time: 644 us -> 643 us (level)
  no operation moved by 1% of the time
where the time goes in v8:
time: 643 us; the launch traced here: 631 us
  Pallas kernels  598 us (93%)
  local copies, waits for them, and re-layouts  15.2 us (2%)
  other arithmetic  14.1 us (2%)
    pallas_call x6, Pallas kernels, call(): pl.pallas_call(body, out_shape=[jax.ShapeDtypeStruct(x[0], x[1]) for x in...  598 us

profile of v8, /device:TPU:8, one launch (start us, length us, event | category | flops | bytes accessed | tf_op | source)
XLA Modules:
  0.0 631.2 jit_solution(15437084122870372126)
XLA Ops:
  0.7 0.8 fusion.21
  1.7 0.9 fusion.10.refs_3_.refs_2_
  2.5 0.7 fusion.20
  4.7 1.0 fusion.refs_4_.refs_3_
  5.7 0.6 pad.11.refs_5_
  6.3 0.6 reshape.85
  7.2 1.4 reshape.86.refs_6_.refs_14_
  8.6 166.4 %shard_map.213 = (f32[16,768]{1,0:T(8,128)}, f32[256,768]{1,0:T(8,128)}, bf16[256,768]{1,0:T(8,128)(2,1)}, bf16[4,256,768]{2,1,0:T(8,128)(2,1)}, bf16[3,4,256,64...) custom-call(bf16[256,768]{1,0:T(8,128)(2,1)} %bitcast.88, ...), custom_call_target="tpu_custom_call" | custom-call | bytes 1048576 | tf_op jit(solution)/shard_map/pallas_call | solution.py:887
  175.2 0.9 fusion.11.refs_3_.refs_2_
  177.5 1.0 fusion.1.refs_4_.refs_3_
  178.5 113.4 %shard_map.214 = (f32[256,768]{1,0:T(8,128)}, bf16[256,768]{1,0:T(8,128)(2,1)}, bf16[4,256,768]{2,1,0:T(8,128)(2,1)}, bf16[3,4,256,64]{3,2,1,0:T(8,128)(2,1)}, b...) custom-call(f32[256,768]{1,0:T(8,128)} %get-tuple-element.94.refs_0_, ...), custom_call_target="tpu_custom_call" | custom-call | bytes 1048576 | tf_op jit(solution)/shard_map/pallas_call | solution.py:887
  291.9 1.9 convert_bitcast_fusion.1
  293.8 0.6 slice_bitcast_fusion.2
  294.8 0.7 pad.12.refs_8_
  295.6 55.5 %shard_map.215 = (f32[256,768]{1,0:T(8,128)}, f32[16,768]{1,0:T(8,128)}, bf16[2,2,4,4,48,512]{5,4,3,2,1,0:T(8,128)(2,1)}, bf16[2,4,128,768]{3,2,1,0:T(8,128)(2,1...) custom-call(bf16[256,768]{1,0:T(8,128)(2,1)} %bitcast.101, f32[256,128]{1,0:T(8,128)} %get-tuple-element.101.refs_1_, ...), custom_call_target="tpu_custom_call" | custom-call | bytes 1048576 | tf_op jit(solution)/shard_map/pallas_call | solution.py:887
  351.1 76.3 %shard_map.216 = (f32[256,768]{1,0:T(8,128)}, f32[8,768]{1,0:T(8,128)}, bf16[4,4,48,576]{3,2,1,0:T(8,128)(2,1)}, bf16[4,48,768]{2,1,0:T(8,128)(2,1)}, bf16[4,48,...) custom-call(f32[256,768]{1,0:T(8,128)} %get-tuple-element.115.refs_0, ...), custom_call_target="tpu_custom_call" | custom-call | bytes 1048576 | tf_op jit(solution)/shard_map/pallas_call | solution.py:887
  427.4 0.7 pad.13.refs_8_
  428.1 81.2 %shard_map.217 = (f32[256,768]{1,0:T(8,128)}, f32[16,768]{1,0:T(8,128)}, bf16[2,2,4,4,48,512]{5,4,3,2,1,0:T(8,128)(2,1)}, bf16[2,4,128,768]{3,2,1,0:T(8,128)(2,1...) custom-call(f32[256,768]{1,0:T(8,128)} %get-tuple-element.126.refs_0, ...), custom_call_target="tpu_custom_call" | custom-call | bytes 1048576 | tf_op jit(solution)/shard_map/pallas_call | solution.py:887
  509.4 105.7 %shard_map.218 = (f32[256,768]{1,0:T(8,128)}, f32[8,768]{1,0:T(8,128)}, bf16[4,4,48,576]{3,2,1,0:T(8,128)(2,1)}, bf16[4,48,768]{2,1,0:T(8,128)(2,1)}, bf16[4,48,...) custom-call(f32[256,768]{1,0:T(8,128)} %get-tuple-element.146.refs_0, ...), custom_call_target="tpu_custom_call" | custom-call | bytes 1048576 | tf_op jit(solution)/shard_map/pallas_call | solution.py:887
  615.0 0.8 reshape.92
  615.8 0.7 constant_dynamic-slice_fusion
  616.7 1.1 stack.63
  617.8 0.6 convert_bitcast_fusion
  618.4 0.8 copy.42
  619.2 1.7 reshape.96
  620.9 0.7 maximum_convert_fusion.4
  621.6 0.7 dynamic-slice_bitcast_fusion
  622.3 1.2 maximum_convert_fusion.2
  623.6 0.9 maximum_convert_fusion.3
  625.0 3.0 maximum_convert_fusion
  628.0 1.9 maximum_convert_fusion.1
  629.9 0.9 copy.50
  (69 shorter events, 4.8 us)
Async XLA Ops:
  0.6 5.0 copy-start.16
  0.7 5.0 copy-start.17
  0.7 5.7 copy-start.7
  178.5 115.3 %copy-start.11 = (f32[16,768]{1,0:T(8,128)S(1)}, f32[16,768]{1,0:T(8,128)}, u32[]{:S(2)}) copy-start(f32[16,768]{1,0:T(8,128)} %get-tuple-element.95.refs_5_) | copy-start | bytes 147460
  509.4 107.1 %copy-start.10 = (bf16[4,48,576]{2,1,0:T(8,128)(2,1)S(1)}, bf16[4,48,576]{2,1,0:T(8,128)(2,1)}, u32[]{:S(2)}) copy-start(bf16[4,48,576]{2,1,0:T(8,128)(2,1)} %get-tuple-element.165) | copy-start | bytes 663556
  618.4 2.5 copy-start.14
  618.4 2.5 copy-start.15
  619.2 3.1 copy-start.8
  619.2 3.1 copy-start.9
  620.9 2.7 copy-start.12
  620.9 2.7 copy-start.13
  622.3 2.2 copy-start.1
  622.3 2.2 copy-start.2
  622.3 2.2 copy-start.4
  622.3 2.7 copy-start.5
  625.0 3.0 copy-start
  625.0 3.0 copy-start.3
  628.0 1.9 copy-start.6

commit v9 on v8

--- a/solution.py
+++ b/solution.py
@@ -1024,7 +1024,7 @@
     return g / (1.0 + jnp.exp(-g)) * u
 
 
-CHUNKS = ((0, 80), (80, 64))
+CHUNKS = ((0, 64), (64, 80))
 
 
 class SlotTrip:
@@ -1223,7 +1223,7 @@
         sums
         + [
             ((EXPERTS, CAP, D), bf16), ((EXPERTS, CAP, D), bf16), ((EXPERTS, CAP, D), bf16),
-            ((EXPERTS * CHUNKS[0][1], D), f32), ((EXPERTS, CAP, D), bf16),
+            ((EXPERTS * CHUNKS[1][1], D), f32), ((EXPERTS, CAP, D), bf16),
             ((EXPERTS, CAP, D), bf16),
         ]
         + sums
@@ -1391,7 +1391,7 @@
         [
             ((SEQ, t, D), bf16), ((2, SEQ, t, FF_DEV), bf16), (slots, bf16), ((2, *slots), bf16),
             ((2, 2, 2, EXPERTS, CAP, FF_DEV), bf16), (slots, bf16), (slots, bf16),
-            ((EXPERTS * CHUNKS[0][1], D), f32), (slots, bf16), (slots, bf16), ((2, t, D), bf16),
+            ((EXPERTS * CHUNKS[1][1], D), f32), (slots, bf16), (slots, bf16), ((2, t, D), bf16),
             ((2, t, D), bf16), ((t, D), bf16), ((t, D), bf16), ((2, 4, 4, 48, FF_DEV), bf16),
             ((4, 128, D), bf16),
         ],

time: 643 us -> 640 us (level)
  no operation moved by 1% of the time
where the time goes in v9:
time: 640 us; the launch traced here: 629 us
  Pallas kernels  596 us (93%)
  local copies, waits for them, and re-layouts  15.2 us (2%)
  other arithmetic  14.1 us (2%)
    pallas_call x6, Pallas kernels, call(): pl.pallas_call(body, out_shape=[jax.ShapeDtypeStruct(x[0], x[1]) for x in...  596 us

profile of v9, /device:TPU:8, one launch (start us, length us, event | category | flops | bytes accessed | tf_op | source)
XLA Modules:
  0.0 629.1 jit_solution(16030412974099966955)
XLA Ops:
  0.7 0.8 fusion.21
  1.7 0.9 fusion.10.refs_3_.refs_2_
  2.5 0.7 fusion.20
  4.7 1.0 fusion.refs_4_.refs_3_
  5.7 0.6 pad.11.refs_5_
  6.3 0.6 reshape.85
  7.2 1.4 reshape.86.refs_6_.refs_14_
  8.6 167.2 %shard_map.213 = (f32[16,768]{1,0:T(8,128)}, f32[256,768]{1,0:T(8,128)}, bf16[256,768]{1,0:T(8,128)(2,1)}, bf16[4,256,768]{2,1,0:T(8,128)(2,1)}, bf16[3,4,256,64...) custom-call(bf16[256,768]{1,0:T(8,128)(2,1)} %bitcast.88, ...), custom_call_target="tpu_custom_call" | custom-call | bytes 1048576 | tf_op jit(solution)/shard_map/pallas_call | solution.py:887
  176.0 0.9 fusion.11.refs_3_.refs_2_
  178.4 1.0 fusion.1.refs_4_.refs_3_
  179.4 111.3 %shard_map.214 = (f32[256,768]{1,0:T(8,128)}, bf16[256,768]{1,0:T(8,128)(2,1)}, bf16[4,256,768]{2,1,0:T(8,128)(2,1)}, bf16[3,4,256,64]{3,2,1,0:T(8,128)(2,1)}, b...) custom-call(f32[256,768]{1,0:T(8,128)} %get-tuple-element.94.refs_0_, ...), custom_call_target="tpu_custom_call" | custom-call | bytes 1048576 | tf_op jit(solution)/shard_map/pallas_call | solution.py:887
  290.7 1.9 convert_bitcast_fusion.1
  292.6 0.6 slice_bitcast_fusion.2
  293.6 0.7 pad.12.refs_8_
  294.3 54.8 %shard_map.215 = (f32[256,768]{1,0:T(8,128)}, f32[16,768]{1,0:T(8,128)}, bf16[2,2,4,4,48,512]{5,4,3,2,1,0:T(8,128)(2,1)}, bf16[2,4,128,768]{3,2,1,0:T(8,128)(2,1...) custom-call(bf16[256,768]{1,0:T(8,128)(2,1)} %bitcast.101, f32[256,128]{1,0:T(8,128)} %get-tuple-element.101.refs_1_, ...), custom_call_target="tpu_custom_call" | custom-call | bytes 1048576 | tf_op jit(solution)/shard_map/pallas_call | solution.py:887
  349.2 76.1 %shard_map.216 = (f32[256,768]{1,0:T(8,128)}, f32[8,768]{1,0:T(8,128)}, bf16[4,4,48,576]{3,2,1,0:T(8,128)(2,1)}, bf16[4,48,768]{2,1,0:T(8,128)(2,1)}, bf16[4,48,...) custom-call(f32[256,768]{1,0:T(8,128)} %get-tuple-element.115.refs_0, ...), custom_call_target="tpu_custom_call" | custom-call | bytes 1048576 | tf_op jit(solution)/shard_map/pallas_call | solution.py:887
  425.3 0.7 pad.13.refs_8_
  426.0 81.4 %shard_map.217 = (f32[256,768]{1,0:T(8,128)}, f32[16,768]{1,0:T(8,128)}, bf16[2,2,4,4,48,512]{5,4,3,2,1,0:T(8,128)(2,1)}, bf16[2,4,128,768]{3,2,1,0:T(8,128)(2,1...) custom-call(f32[256,768]{1,0:T(8,128)} %get-tuple-element.126.refs_0, ...), custom_call_target="tpu_custom_call" | custom-call | bytes 1048576 | tf_op jit(solution)/shard_map/pallas_call | solution.py:887
  507.5 105.5 %shard_map.218 = (f32[256,768]{1,0:T(8,128)}, f32[8,768]{1,0:T(8,128)}, bf16[4,4,48,576]{3,2,1,0:T(8,128)(2,1)}, bf16[4,48,768]{2,1,0:T(8,128)(2,1)}, bf16[4,48,...) custom-call(f32[256,768]{1,0:T(8,128)} %get-tuple-element.146.refs_0, ...), custom_call_target="tpu_custom_call" | custom-call | bytes 1048576 | tf_op jit(solution)/shard_map/pallas_call | solution.py:887
  612.9 0.8 reshape.92
  613.7 0.7 constant_dynamic-slice_fusion
  614.6 1.1 stack.63
  615.7 0.6 convert_bitcast_fusion
  616.3 0.8 copy.42
  617.1 1.7 reshape.96
  618.8 0.7 maximum_convert_fusion.4
  619.5 0.7 dynamic-slice_bitcast_fusion
  620.2 1.2 maximum_convert_fusion.2
  621.5 0.9 maximum_convert_fusion.3
  622.9 3.0 maximum_convert_fusion
  625.9 1.9 maximum_convert_fusion.1
  627.8 0.9 copy.50
  (69 shorter events, 4.8 us)
Async XLA Ops:
  0.6 5.0 copy-start.16
  0.7 5.0 copy-start.17
  0.7 5.7 copy-start.7
  179.4 113.2 %copy-start.11 = (f32[16,768]{1,0:T(8,128)S(1)}, f32[16,768]{1,0:T(8,128)}, u32[]{:S(2)}) copy-start(f32[16,768]{1,0:T(8,128)} %get-tuple-element.95.refs_5_) | copy-start | bytes 147460
  507.4 107.0 %copy-start.10 = (bf16[4,48,576]{2,1,0:T(8,128)(2,1)S(1)}, bf16[4,48,576]{2,1,0:T(8,128)(2,1)}, u32[]{:S(2)}) copy-start(bf16[4,48,576]{2,1,0:T(8,128)(2,1)} %get-tuple-element.165) | copy-start | bytes 663556
  616.3 2.5 copy-start.14
  616.3 2.5 copy-start.15
  617.1 3.1 copy-start.8
  617.1 3.1 copy-start.9
  618.8 2.7 copy-start.12
  618.8 2.7 copy-start.13
  620.2 2.2 copy-start.1
  620.2 2.2 copy-start.2
  620.2 2.2 copy-start.4
  620.2 2.7 copy-start.5
  622.9 3.0 copy-start
  622.9 3.0 copy-start.3
  625.9 1.9 copy-start.6
